TPU v7x, 32 devices: a whole 2x2x4 slice. The times are simulated.
32 devices in a mesh: dp: 4 (over z), ctx: 2 (over x), tensor: 4 (over y, core).
Axes of the slice: x: 2, y: 2, z: 4, core: 2. Of those that a mesh axis runs over, the one named last changes fastest.
Arguments:
- tokens_in: bfloat16 [4096, 2048], P(('dp', 'ctx')), may hold values from -6 to 6
- cotangent: bfloat16 [4096, 2048], P(('dp', 'ctx')), may hold values from -6 to 6
- seq_lengths: int32 [4, 2], P('dp'), may hold values from 256 to 768, as said below
- block_order: int32 [4, 2, 2], P('dp'), may hold values from 0 to 3, as said below
- gain_one: float32 [2048], replicated, may hold values from 0.5 to 1.5
- down_q: bfloat16 [2048, 1024], P(('dp', 'ctx')), may hold values from -0.125 to 0.125
- gain_q: float32 [1024], replicated, may hold values from 0.5 to 1.5
- up_q: bfloat16 [1024, 4096], P(('dp', 'ctx'), 'tensor'), may hold values from -0.1875 to 0.1875
- key_w: bfloat16 [2048, 256], P(('dp', 'ctx')), may hold values from -0.125 to 0.125
- value_w: bfloat16 [2048, 256], P(('dp', 'ctx')), may hold values from -0.125 to 0.125
- out_w: bfloat16 [2048, 4096], P(('dp', 'ctx'), 'tensor'), may hold values from -0.5 to 0.5
- gain_two: float32 [2048], replicated, may hold values from 0.5 to 1.5
- gate_w: bfloat16 [2048, 5632], P(('dp', 'ctx'), 'tensor'), may hold values from -0.125 to 0.125
- up_w: bfloat16 [2048, 5632], P(('dp', 'ctx'), 'tensor'), may hold values from -0.125 to 0.125
- down_w: bfloat16 [2048, 5632], P(('dp', 'ctx'), 'tensor'), may hold values from -0.078125 to 0.078125
Outputs:
- out_tokens: bfloat16 [4096, 2048], P(('dp', 'ctx'))
- grad_tokens: float32 [4096, 2048], P(('dp', 'ctx'))
- grad_gain_one: float32 [2048], P(('dp', 'ctx'))
- grad_down_q: float32 [2048, 1024], P(('dp', 'ctx'))
- grad_gain_q: float32 [1024], P(('dp', 'ctx'))
- grad_up_q: float32 [1024, 4096], P(('dp', 'ctx'), 'tensor')
- grad_key_w: float32 [2048, 256], P(('dp', 'ctx'))
- grad_value_w: float32 [2048, 256], P(('dp', 'ctx'))
- grad_out_w: float32 [2048, 4096], P(('dp', 'ctx'), 'tensor')
- grad_gain_two: float32 [2048], P(('dp', 'ctx'))
- grad_gate_w: float32 [2048, 5632], P(('dp', 'ctx'), 'tensor')
- grad_up_w: float32 [2048, 5632], P(('dp', 'ctx'), 'tensor')
- grad_down_w: float32 [2048, 5632], P(('dp', 'ctx'), 'tensor')
Inputs may be any that keep to these rules, and one draw needn't show every extreme that they name: `seq_lengths`: row g holds the lengths of group g's first and second sequence; they add up to 1024. block_order[g, r] holds r and 3 - r, in either order.
All inputs are finite; a program needn't handle non-finite values.
Results may differ from a plain program's by a relative error of at most 0.017.
Values may be sent and summed in bfloat16 or wider, within the bound.
No kernel may reach another device: no remote copies, remote signals or barrier semaphores. Data moves between devices by JAX's collectives and lax.ppermute only.
A program may use at most 192 MiB of HBM per device.

v0:
```python
import jax
import jax.numpy as jnp
from jax import lax
from jax.sharding import PartitionSpec as P

HD = 256


EPSILON = 1e-06


def times_trans(left, right):
    return lax.dot_general(
        left, right, (((1,), (1,)), ((), ())), preferred_element_type=jnp.float32
    )


def trans_times(left, right):
    return lax.dot_general(
        left, right, (((0,), (0,)), ((), ())), preferred_element_type=jnp.float32
    )


def rms_parts(array):
    inverse = lax.rsqrt(jnp.mean(array * array, axis=-1, keepdims=True) + EPSILON)
    return (array * inverse, inverse)


def rms_back(grad_out, plain, inverse, gain):
    grad_plain = grad_out * gain
    grad_in = inverse * (grad_plain - plain * jnp.mean(grad_plain * plain, axis=-1, keepdims=True))
    return (grad_in, jnp.sum(grad_out * plain, axis=0))


def rotate(array, places):
    half = array.shape[-1] // 2
    freqs = 10000.0 ** (-jnp.arange(half, dtype=jnp.float32) / half)
    angles = places[:, None] * freqs[None, :]
    cosine = jnp.cos(angles)
    sine = jnp.sin(angles)
    first = array[..., :half]
    latter = array[..., half:]
    return jnp.concatenate(
        [first * cosine - latter * sine, latter * cosine + first * sine], axis=-1
    )


def forward(token_rows, attention_w, ffn_w, gains, own_pos, allowed):
    gain_one, gain_q, gain_two = gains
    down_q, up_q, key_w, value_w, out_w = attention_w
    gate_w, up_w, down_w = ffn_w
    row_count = token_rows.shape[0]
    heads = up_q.shape[1] // HD
    scale = HD ** (-0.5)
    plain_one, inverse_one = rms_parts(token_rows)
    normed = (plain_one * gain_one).astype(jnp.bfloat16)
    latent = jnp.dot(normed, down_q, preferred_element_type=jnp.float32)
    plain_q, inverse_q = rms_parts(latent)
    query_in = (plain_q * gain_q).astype(jnp.bfloat16)
    query_pre = jnp.dot(query_in, up_q, preferred_element_type=jnp.float32)
    query = rotate(query_pre.reshape(row_count, heads, HD).transpose(1, 0, 2), own_pos).astype(
        jnp.bfloat16
    )
    keys = rotate(jnp.dot(normed, key_w, preferred_element_type=jnp.float32), own_pos).astype(
        jnp.bfloat16
    )
    values = jnp.dot(normed, value_w, preferred_element_type=jnp.float32).astype(jnp.bfloat16)
    keys_all, values_all = (
        lax.all_gather(keys, "ctx", axis=0, tiled=True),
        lax.all_gather(values, "ctx", axis=0, tiled=True),
    )

    def one_head(q_head):
        scores = jnp.where(allowed, times_trans(q_head, keys_all) * scale, -1e30)
        largest = jnp.max(scores, axis=-1, keepdims=True)
        exponent = jnp.exp(scores - largest)
        totals = jnp.sum(exponent, axis=-1, keepdims=True)
        soft = (exponent / totals).astype(jnp.bfloat16)
        return (
            jnp.dot(soft, values_all, preferred_element_type=jnp.float32),
            (largest + jnp.log(totals))[:, 0],
        )

    mixed_heads, log_totals = lax.map(one_head, query)
    attended = mixed_heads.transpose(1, 0, 2).reshape(row_count, heads * HD).astype(jnp.bfloat16)
    branch = lax.psum(times_trans(attended, out_w), "tensor")
    middle = token_rows + branch
    plain_two, inverse_two = rms_parts(middle)
    normed_two = (plain_two * gain_two).astype(jnp.bfloat16)
    gate_pre = jnp.dot(normed_two, gate_w, preferred_element_type=jnp.float32)
    up_pre = jnp.dot(normed_two, up_w, preferred_element_type=jnp.float32)
    hidden = (jax.nn.silu(gate_pre) * up_pre).astype(jnp.bfloat16)
    result = middle + lax.psum(times_trans(hidden, down_w).astype(jnp.bfloat16), "tensor").astype(
        jnp.float32
    )
    kept_values = (
        plain_one,
        inverse_one,
        normed,
        plain_q,
        inverse_q,
        query_in,
        query,
        keys_all,
        values_all,
        log_totals,
        attended,
        plain_two,
        inverse_two,
        normed_two,
        gate_pre,
        up_pre,
        hidden,
    )
    return (result, kept_values)


def backward(cotangent, attention_w, ffn_w, gains, own_pos, allowed, kept_values):
    gain_one, gain_q, gain_two = gains
    down_q, up_q, key_w, value_w, out_w = attention_w
    gate_w, up_w, down_w = ffn_w
    (
        plain_one,
        inverse_one,
        normed,
        plain_q,
        inverse_q,
        query_in,
        query,
        keys_all,
        values_all,
        log_totals,
        attended,
        plain_two,
        inverse_two,
        normed_two,
        gate_pre,
        up_pre,
        hidden,
    ) = kept_values
    row_count = cotangent.shape[0]
    heads = query.shape[0]
    scale = HD ** (-0.5)
    grad_down = trans_times(cotangent, hidden)
    grad_hidden = jnp.dot(cotangent, down_w, preferred_element_type=jnp.float32)
    sigma = jax.nn.sigmoid(gate_pre)
    grad_gate = (grad_hidden * up_pre * sigma * (1.0 + gate_pre * (1.0 - sigma))).astype(
        jnp.bfloat16
    )
    grad_up = (grad_hidden * gate_pre * sigma).astype(jnp.bfloat16)
    grad_gate_w = trans_times(normed_two, grad_gate)
    grad_up_w = trans_times(normed_two, grad_up)
    grad_norm_two = lax.psum(times_trans(grad_gate, gate_w) + times_trans(grad_up, up_w), "tensor")
    grad_mid_part, grad_gain_two = rms_back(grad_norm_two, plain_two, inverse_two, gain_two)
    ffn_grads = (
        lax.psum_scatter(grad_gate_w, ("dp", "ctx"), scatter_dimension=0, tiled=True),
        lax.psum_scatter(grad_up_w, ("dp", "ctx"), scatter_dimension=0, tiled=True),
        lax.psum_scatter(grad_down, ("dp", "ctx"), scatter_dimension=0, tiled=True),
        lax.psum_scatter(grad_gain_two, ("dp", "ctx"), scatter_dimension=0, tiled=True),
    )
    grad_middle = cotangent.astype(jnp.float32) + grad_mid_part
    grad_branch = grad_middle.astype(jnp.bfloat16)
    grad_out_w = trans_times(grad_branch, attended)
    grad_attended = jnp.dot(grad_branch, out_w, preferred_element_type=jnp.float32).astype(
        jnp.bfloat16
    )
    grad_heads = grad_attended.reshape(row_count, heads, HD).transpose(1, 0, 2)

    def head_back(carry, item):
        key_acc, value_acc = carry
        q_head, grad_head, lse_head = item
        scores = jnp.where(allowed, times_trans(q_head, keys_all) * scale, -1e30)
        soft = jnp.exp(scores - lse_head[:, None])
        grad_soft = times_trans(grad_head, values_all)
        inner = jnp.sum(soft * grad_soft, axis=-1, keepdims=True)
        grad_scores = (soft * (grad_soft - inner)).astype(jnp.bfloat16)
        grad_q = jnp.dot(grad_scores, keys_all, preferred_element_type=jnp.float32) * scale
        key_acc = key_acc + trans_times(grad_scores, q_head) * scale
        value_acc = value_acc + trans_times(soft.astype(jnp.bfloat16), grad_head)
        return ((key_acc, value_acc), grad_q)

    empty = jnp.zeros(keys_all.shape, jnp.float32)
    (key_total, value_total), grad_query = lax.scan(
        head_back, (empty, empty), (query, grad_heads, log_totals)
    )
    key_own, value_own = (
        lax.psum_scatter(key_total, "ctx", scatter_dimension=0, tiled=True),
        lax.psum_scatter(value_total, "ctx", scatter_dimension=0, tiled=True),
    )
    grad_query_pre = (
        rotate(grad_query, -own_pos)
        .transpose(1, 0, 2)
        .reshape(row_count, heads * HD)
        .astype(jnp.bfloat16)
    )
    grad_up_q = trans_times(query_in, grad_query_pre)
    grad_qin_part = times_trans(grad_query_pre, up_q)
    grad_qin, grad_keys_rot, grad_values = lax.psum((grad_qin_part, key_own, value_own), "tensor")
    grad_key_pre = rotate(grad_keys_rot, -own_pos).astype(jnp.bfloat16)
    grad_value_low = grad_values.astype(jnp.bfloat16)
    grad_latent, grad_gain_q = rms_back(grad_qin, plain_q, inverse_q, gain_q)
    grad_latent_low = grad_latent.astype(jnp.bfloat16)
    grad_down_q = trans_times(normed, grad_latent_low)
    grad_key_w = trans_times(normed, grad_key_pre)
    grad_value_w = trans_times(normed, grad_value_low)
    grad_norm_one = (
        times_trans(grad_latent_low, down_q)
        + times_trans(grad_key_pre, key_w)
        + times_trans(grad_value_low, value_w)
    )
    grad_in_part, grad_gain_one = rms_back(grad_norm_one, plain_one, inverse_one, gain_one)
    grad_tokens = grad_middle + grad_in_part
    attention_grads = (
        lax.psum_scatter(grad_gain_one, ("dp", "ctx"), scatter_dimension=0, tiled=True),
        lax.psum_scatter(grad_down_q, ("dp", "ctx"), scatter_dimension=0, tiled=True),
        lax.psum_scatter(grad_gain_q, ("dp", "ctx"), scatter_dimension=0, tiled=True),
        lax.psum_scatter(grad_up_q, ("dp", "ctx"), scatter_dimension=0, tiled=True),
        lax.psum_scatter(grad_key_w, ("dp", "ctx"), scatter_dimension=0, tiled=True),
        lax.psum_scatter(grad_value_w, ("dp", "ctx"), scatter_dimension=0, tiled=True),
        lax.psum_scatter(grad_out_w, ("dp", "ctx"), scatter_dimension=0, tiled=True),
    )
    return (grad_tokens, attention_grads, ffn_grads)


def per_device(
    tokens_in,
    cotangent,
    seq_lengths,
    block_order,
    gain_one,
    down_q,
    gain_q,
    up_q,
    key_w,
    value_w,
    out_w,
    gain_two,
    gate_w,
    up_w,
    down_w,
):
    token_rows = tokens_in.astype(jnp.float32)
    row_count = tokens_in.shape[0]
    block_rows = row_count // 2
    places = (
        block_order[0][:, :, None] * block_rows
        + jnp.arange(block_rows, dtype=jnp.int32)[None, None, :]
    ).reshape(-1)
    second = (places >= seq_lengths[0, 0]).astype(jnp.int32)
    in_sequence = places - second * seq_lengths[0, 0]
    start = lax.axis_index("ctx") * row_count
    own_places = lax.dynamic_slice_in_dim(places, start, row_count)
    own_second = lax.dynamic_slice_in_dim(second, start, row_count)
    own_pos = lax.dynamic_slice_in_dim(in_sequence, start, row_count).astype(jnp.float32)
    allowed = (own_second[:, None] == second[None, :]) & (places[None, :] <= own_places[:, None])
    gains = (gain_one, gain_q, gain_two)
    attention_w = (
        lax.all_gather(down_q, ("dp", "ctx"), axis=0, tiled=True),
        lax.all_gather(up_q, ("dp", "ctx"), axis=0, tiled=True),
        lax.all_gather(key_w, ("dp", "ctx"), axis=0, tiled=True),
        lax.all_gather(value_w, ("dp", "ctx"), axis=0, tiled=True),
        lax.all_gather(out_w, ("dp", "ctx"), axis=0, tiled=True),
    )
    ffn_w = (
        lax.all_gather(gate_w, ("dp", "ctx"), axis=0, tiled=True),
        lax.all_gather(up_w, ("dp", "ctx"), axis=0, tiled=True),
        lax.all_gather(down_w, ("dp", "ctx"), axis=0, tiled=True),
    )
    result, kept_values = forward(token_rows, attention_w, ffn_w, gains, own_pos, allowed)
    attention_w = (
        lax.all_gather(down_q, ("dp", "ctx"), axis=0, tiled=True),
        lax.all_gather(up_q, ("dp", "ctx"), axis=0, tiled=True),
        lax.all_gather(key_w, ("dp", "ctx"), axis=0, tiled=True),
        lax.all_gather(value_w, ("dp", "ctx"), axis=0, tiled=True),
        lax.all_gather(out_w, ("dp", "ctx"), axis=0, tiled=True),
    )
    ffn_w = (
        lax.all_gather(gate_w, ("dp", "ctx"), axis=0, tiled=True),
        lax.all_gather(up_w, ("dp", "ctx"), axis=0, tiled=True),
        lax.all_gather(down_w, ("dp", "ctx"), axis=0, tiled=True),
    )
    unused, kept_values = forward(token_rows, attention_w, ffn_w, gains, own_pos, allowed)
    grad_tokens, attention_grads, ffn_grads = backward(
        cotangent, attention_w, ffn_w, gains, own_pos, allowed, kept_values
    )
    grad_gain_one, grad_down_q, grad_gain_q, grad_up_q, grad_key_w, grad_value_w, grad_out_w = (
        attention_grads
    )
    grad_gate_w, grad_up_w, grad_down_w, grad_gain_two = ffn_grads
    return (
        result.astype(jnp.bfloat16),
        grad_tokens,
        grad_gain_one,
        grad_down_q,
        grad_gain_q,
        grad_up_q,
        grad_key_w,
        grad_value_w,
        grad_out_w,
        grad_gain_two,
        grad_gate_w,
        grad_up_w,
        grad_down_w,
    )


def solution(mesh):
    return jax.shard_map(
        per_device,
        mesh=mesh,
        in_specs=(
            P(("dp", "ctx"), None),
            P(("dp", "ctx"), None),
            P("dp", None),
            P("dp", None, None),
            P(),
            P(("dp", "ctx"), None),
            P(),
            P(("dp", "ctx"), "tensor"),
            P(("dp", "ctx"), None),
            P(("dp", "ctx"), None),
            P(("dp", "ctx"), "tensor"),
            P(),
            P(("dp", "ctx"), "tensor"),
            P(("dp", "ctx"), "tensor"),
            P(("dp", "ctx"), "tensor"),
        ),
        out_specs=(
            P(("dp", "ctx"), None),
            P(("dp", "ctx"), None),
            P(("dp", "ctx")),
            P(("dp", "ctx"), None),
            P(("dp", "ctx")),
            P(("dp", "ctx"), "tensor"),
            P(("dp", "ctx"), None),
            P(("dp", "ctx"), None),
            P(("dp", "ctx"), "tensor"),
            P(("dp", "ctx")),
            P(("dp", "ctx"), "tensor"),
            P(("dp", "ctx"), "tensor"),
            P(("dp", "ctx"), "tensor"),
        ),
        check_vma=False,
    )
```

profile of v0, /device:TPU:0, one launch (start us, length us, event | category | flops | bytes accessed | tf_op | source)
XLA Modules:
  0.0 2217.3 jit_solution(11342079444066812490)
XLA Ops:
  16.8 36.2 %all-gather.13.cloned.1.call-done = bf16[2048,256]{1,0:T(8,128)(2,1)} async-done(((bf16[256,256]{1,0:T(8,128)(2,1)}), bf16[2048,256]{1,0:T(8,128)(2,1)}) %all-gather.13.cloned.1.call-update) | async-done | bytes 1048592 | tf_op jit(solution)/shard_map/all_gather | solution.py:260
  59.2 9.1 all_gather.43
  68.5 25.9 %all-gather.15.cloned.1.call-done = bf16[2048,256]{1,0:T(8,128)(2,1)} async-done(((bf16[256,256]{1,0:T(8,128)(2,1)}), bf16[2048,256]{1,0:T(8,128)(2,1)}) %all-gather.15.cloned.1.call-update) | async-done | bytes 1048592 | tf_op jit(solution)/shard_map/all_gather | solution.py:261
  104.1 64.6 %all-gather.9.cloned.1.call-done = bf16[2048,1024]{1,0:T(8,128)(2,1)} async-done(((bf16[256,1024]{1,0:T(8,128)(2,1)}), bf16[2048,1024]{1,0:T(8,128)(2,1)}) %all-gather.9.cloned.1.call-update) | async-done | bytes 4194320 | tf_op jit(solution)/shard_map/all_gather | solution.py:258
  174.6 43.7 %all-gather.11.cloned.1.call-done = bf16[1024,1024]{1,0:T(8,128)(2,1)} async-done(((bf16[128,1024]{1,0:T(8,128)(2,1)}), bf16[1024,1024]{1,0:T(8,128)(2,1)}) %all-gather.11.cloned.1.call-update) | async-done | bytes 2097168 | tf_op jit(solution)/shard_map/all_gather | solution.py:259
  224.1 26.2 %while.43 = (s32[]{:T(128)}, bf16[4,512,256]{1,2,0:T(8,128)(2,1)}, f32[4,512]{1,0:T(4,128)S(1)}, bf16[4,512,256]{2,1,0:T(8,128)(2,1)}, bf16[1024,256]{1,0:T(8,12...) while((s32[]{:T(128)}, bf16[4,512,256]{1,2,0:T(8,128)(2,1)}, ...), condition=%wide.region_12.13_spmd.clone.clone, body=%wide.region_9.12_spmd.clone.sunk.clone | while | flops 542637568 | bytes 16548997 | solution.py:84
  250.4 41.8 %all-gather.17.cloned.1.call-done = bf16[2048,1024]{1,0:T(8,128)(2,1)} async-done(((bf16[256,1024]{1,0:T(8,128)(2,1)}), bf16[2048,1024]{1,0:T(8,128)(2,1)}) %all-gather.17.cloned.1.call-update) | async-done | bytes 4194320 | tf_op jit(solution)/shard_map/all_gather | solution.py:262
  301.4 14.7 while.42
  323.1 59.9 %all-reduce.14.cloned.1.call-done = f32[512,2048]{1,0:T(8,128)} async-done(((f32[512,2048]{1,0:T(8,128)}), f32[512,2048]{1,0:T(8,128)}) %all-reduce.14.cloned.1.call-update) | async-done | bytes 4194320 | tf_op jit(solution)/shard_map/psum | solution.py:86
  388.5 89.8 %all-gather.21.cloned.1.call-done = bf16[2048,1408]{1,0:T(8,128)(2,1)} async-done(((bf16[256,1408]{1,0:T(8,128)(2,1)}), bf16[2048,1408]{1,0:T(8,128)(2,1)}) %all-gather.21.cloned.1.call-update) | async-done | bytes 5767184 | tf_op jit(solution)/shard_map/all_gather | solution.py:266
  486.5 85.0 %all-gather.19.cloned.1.call-done = bf16[2048,1408]{1,0:T(8,128)(2,1)} async-done(((bf16[256,1408]{1,0:T(8,128)(2,1)}), bf16[2048,1408]{1,0:T(8,128)(2,1)}) %all-gather.19.cloned.1.call-update) | async-done | bytes 5767184 | tf_op jit(solution)/shard_map/all_gather | solution.py:265
  579.8 85.0 %all-gather.23.cloned.1.call-done = bf16[2048,1408]{1,0:T(8,128)(2,1)} async-done(((bf16[256,1408]{1,0:T(8,128)(2,1)}), bf16[2048,1408]{1,0:T(8,128)(2,1)}) %all-gather.23.cloned.1.call-update) | async-done | bytes 5767184 | tf_op jit(solution)/shard_map/all_gather | solution.py:267
  664.8 9.1 multiply_convert_fusion.4
  685.6 151.5 %all-reduce.18.cloned.1.call-done = (f32[512,2048]{1,0:T(8,128)}, f32[512,2048]{1,0:T(8,128)}) async-done(((f32[512,2048]{1,0:T(8,128)}, f32[512,2048]{1,0:T(8,128)}), (f32[512,2048]{1,0:T(8,128)}, f32[512,2048]{1,0:T(8,128)})) %all-reduce.18.cloned.1.call-update) | async-done | bytes 8388624 | tf_op jit(solution)/shard_map/psum | solution.py:153
  852.8 62.5 %while.44 = (s32[]{:T(128)}, f32[1024,256]{1,0:T(8,128)}, f32[1024,256]{1,0:T(8,128)}, f32[4,512,256]{1,2,0:T(8,128)}, bf16[4,512,256]{2,1,0:T(8,128)(2,1)}, /*i...) while((s32[]{:T(128)}, f32[1024,256]{1,0:T(8,128)}, ...), condition=%wide.region_19.20_spmd.clone.clone, body=%wide.region_17.19_spmd.clone.sunk.clone | while | flops 1349910016 | bytes 33579772 | solution.py:183
  928.1 10.5 reduce-scatter.11.cloned.1.call-done
  938.7 13.2 convolution_convert_fusion
  953.6 8.8 convolution_bitcast_fusion.2
  962.5 24.9 %all-reduce.19 = bf16[512,256]{1,0:T(8,128)(2,1)S(1)} all-reduce(f32[512,256]{1,0:T(8,128)} %reduce-scatter.13.cloned.1.call-done), channel_id=1, replica_groups=mesh['dp'=4,'ctx'=2,'tensor'=4] {'tensor'}, use_global_device_ids=true, to_apply=%region_25.26 | all-reduce | flops 131072 | bytes 786432 | tf_op jit(solution)/shard_map/psum | solution.py:198
  990.0 39.3 %all-reduce.16.cloned.1.call-done = (f32[512,1024]{1,0:T(8,128)}, f32[512,256]{0,1:T(8,128)}) async-done(((f32[512,1024]{1,0:T(8,128)}, f32[512,256]{0,1:T(8,128)}), (f32[512,1024]{1,0:T(8,128)}, f32[512,256]{0,1:T(8,128)})) %all-reduce.16.cloned.1.call-update) | async-done | bytes 2621456 | tf_op jit(solution)/shard_map/psum | solution.py:198
  1050.5 9.7 fusion.83
  1060.5 9.7 fusion.84
  1091.3 38.8 %all-reduce.3 = (f32[2048]{0:T(1024)S(1)}, f32[1024]{0:T(1024)S(1)}, f32[2048]{0:T(1024)S(1)}) all-reduce(f32[2048]{0:T(1024)S(1)} %get-tuple-element.378, f32[1024]{0:T(1024)S(1)} %copy-done.38, f32[2048]{0:T(1024)S(1)} %get-tuple-element.376), channel_id=4, replica_groups=mesh['dp'=4,'ctx'=2,'tensor'=4] {'dp','ctx'}, use_global_device_ids=true, to_apply=%region_28.29.clone | all-reduce | flops 5120 | bytes 40960
  1132.0 8.5 fusion.42
  1140.5 139.5 %reduce-scatter.29.cloned.1.call-done = f32[256,1408]{0,1:T(8,128)} async-done(((f32[2048,1408]{0,1:T(8,128)}), f32[256,1408]{0,1:T(8,128)}) %reduce-scatter.29.cloned.1.call-update) | async-done | bytes 1441808 | tf_op jit(solution)/shard_map/reduce_scatter | solution.py:158
  1282.9 67.7 %reduce-scatter.21.cloned.1.call-done = f32[256,256]{1,0:T(8,128)} async-done(((f32[2048,256]{1,0:T(8,128)}), f32[256,256]{1,0:T(8,128)}) %reduce-scatter.21.cloned.1.call-update) | async-done | bytes 262160 | tf_op jit(solution)/shard_map/reduce_scatter | solution.py:219
  1350.6 70.7 %reduce-scatter.19.cloned.1.call-done = f32[256,256]{1,0:T(8,128)} async-done(((f32[2048,256]{1,0:T(8,128)}), f32[256,256]{1,0:T(8,128)}) %reduce-scatter.19.cloned.1.call-update) | async-done | bytes 262160 | tf_op jit(solution)/shard_map/reduce_scatter | solution.py:218
  1421.3 91.2 %reduce-scatter.17.cloned.1.call-done = f32[128,1024]{1,0:T(8,128)} async-done(((f32[1024,1024]{1,0:T(8,128)}), f32[128,1024]{1,0:T(8,128)}) %reduce-scatter.17.cloned.1.call-update) | async-done | bytes 524304 | tf_op jit(solution)/shard_map/reduce_scatter | solution.py:217
  1512.5 153.4 %reduce-scatter.23.cloned.1.call-done = f32[256,1024]{1,0:T(8,128)} async-done(((f32[2048,1024]{1,0:T(8,128)}), f32[256,1024]{1,0:T(8,128)}) %reduce-scatter.23.cloned.1.call-update) | async-done | bytes 1048592 | tf_op jit(solution)/shard_map/reduce_scatter | solution.py:220
  1665.9 195.7 %reduce-scatter.25.cloned.1.call-done = f32[256,1408]{1,0:T(8,128)} async-done(((f32[2048,1408]{1,0:T(8,128)}), f32[256,1408]{1,0:T(8,128)}) %reduce-scatter.25.cloned.1.call-update) | async-done | bytes 1441808 | tf_op jit(solution)/shard_map/reduce_scatter | solution.py:156
  1861.7 196.0 %reduce-scatter.27.cloned.1.call-done = f32[256,1408]{1,0:T(8,128)} async-done(((f32[2048,1408]{1,0:T(8,128)}), f32[256,1408]{1,0:T(8,128)}) %reduce-scatter.27.cloned.1.call-update) | async-done | bytes 1441808 | tf_op jit(solution)/shard_map/reduce_scatter | solution.py:157
  2057.7 152.4 %reduce-scatter.15.cloned.1.call-done = f32[256,1024]{1,0:T(8,128)} async-done(((f32[2048,1024]{1,0:T(8,128)}), f32[256,1024]{1,0:T(8,128)}) %reduce-scatter.15.cloned.1.call-update) | async-done | bytes 1048592 | tf_op jit(solution)/shard_map/reduce_scatter | solution.py:215
  (311 shorter events, 268.6 us)
Async XLA Ops:
  7.2 45.8 %all-gather.13.cloned.1.call-start = ((), (), s32[]{:S(2)}) async-start(), calls=%async_computation.12 | async-start | bytes 1179648 | tf_op jit(solution)/shard_map/all_gather | solution.py:260
  7.9 86.5 %all-gather.15.cloned.1.call-start = ((), (), s32[]{:S(2)}) async-start(), calls=%async_computation.13 | async-start | bytes 1179648 | tf_op jit(solution)/shard_map/all_gather | solution.py:261
  8.7 160.0 %all-gather.9.cloned.1.call-start = ((), (), s32[]{:S(2)}) async-start(), calls=%async_computation.10 | async-start | bytes 4718592 | tf_op jit(solution)/shard_map/all_gather | solution.py:258
  9.4 208.9 %all-gather.11.cloned.1.call-start = ((), (), s32[]{:S(2)}) async-start(), calls=%async_computation.11 | async-start | bytes 2359296 | tf_op jit(solution)/shard_map/all_gather | solution.py:259
  10.0 282.2 %all-gather.17.cloned.1.call-start = ((), (), s32[]{:S(2)}) async-start(), calls=%async_computation.14 | async-start | bytes 4718592 | tf_op jit(solution)/shard_map/all_gather | solution.py:262
  10.6 372.4 %all-reduce.14.cloned.1.call-start = ((), (), s32[]{:S(2)}) async-start(), calls=%async_computation.19 | async-start | bytes 8388608 | tf_op jit(solution)/shard_map/psum | solution.py:86
  10.6 44.6 %copy-start.39 = (f32[128]{0:T(128)}, f32[128]{0:T(128)S(1)}, u32[]{:S(2)}) copy-start(f32[128]{0:T(128)S(1)} %multiply_power_fusion) | copy-start | bytes 1540
  13.9 41.3 %copy-start.33 = (f32[512]{0:T(512)}, f32[512]{0:T(512)S(1)}, u32[]{:S(2)}) copy-start(f32[512]{0:T(512)S(1)} %get-tuple-element.454) | copy-start | bytes 6148
  13.9 39.1 %copy-start.29 = (f32[2048]{0:T(1024)S(1)}, f32[2048]{0:T(1024)}, u32[]{:S(2)}) copy-start(f32[2048]{0:T(1024)} %param.25) | copy-start | bytes 24580
  14.4 154.3 %copy-start.34 = (f32[512]{0:T(512)}, f32[512]{0:T(512)S(1)}, u32[]{:S(2)}) copy-start(f32[512]{0:T(512)S(1)} %add_rsqrt_fusion.3) | copy-start | bytes 6148
  104.1 114.2 %copy-start.24 = (f32[1024]{0:T(1024)S(1)}, f32[1024]{0:T(1024)}, u32[]{:S(2)}) copy-start(f32[1024]{0:T(1024)} %param.27) | copy-start | bytes 12292
  174.6 47.2 %copy-start.27 = (f32[512]{0:T(512)}, f32[512]{0:T(512)S(1)}, u32[]{:S(2)}) copy-start(f32[512]{0:T(512)S(1)} %add_rsqrt_fusion.2) | copy-start | bytes 6148
  299.1 179.1 %all-gather.21.cloned.1.call-start = ((), (), s32[]{:S(2)}) async-start(), calls=%async_computation.16 | async-start | bytes 6488064 | tf_op jit(solution)/shard_map/all_gather | solution.py:266
  299.9 271.6 %all-gather.19.cloned.1.call-start = ((), (), s32[]{:S(2)}) async-start(), calls=%async_computation.15 | async-start | bytes 6488064 | tf_op jit(solution)/shard_map/all_gather | solution.py:265
  300.6 364.2 %all-gather.23.cloned.1.call-start = ((), (), s32[]{:S(2)}) async-start(), calls=%async_computation.17 | async-start | bytes 6488064 | tf_op jit(solution)/shard_map/all_gather | solution.py:267
  301.3 535.7 %all-reduce.18.cloned.1.call-start = ((), (), s32[]{:S(2)}) async-start(), calls=%async_computation.31 | async-start | bytes 16777216 | tf_op jit(solution)/shard_map/psum | solution.py:153
  323.1 62.8 %copy-start.26 = (f32[2048]{0:T(1024)S(1)}, f32[2048]{0:T(1024)}, u32[]{:S(2)}) copy-start(f32[2048]{0:T(1024)} %param.32) | copy-start | bytes 24580
  685.5 253.2 %reduce-scatter.11.cloned.1.call-start = ((), (), s32[]{:S(2)}) async-start(), calls=%async_computation.20 | async-start | bytes 1572864 | tf_op jit(solution)/shard_map/reduce_scatter | solution.py:187
  918.1 44.4 %reduce-scatter.13.cloned.1.call-start = ((), (), s32[]{:S(2)}) async-start(), calls=%async_computation.21 | async-start | bytes 1572864 | tf_op jit(solution)/shard_map/reduce_scatter | solution.py:188
  918.6 110.6 %all-reduce.16.cloned.1.call-start = ((), (), s32[]{:S(2)}) async-start(), calls=%async_computation.30 | async-start | bytes 5242880 | tf_op jit(solution)/shard_map/psum | solution.py:198
  938.7 193.3 %all-reduce.12.cloned.1.call-start = ((), (), s32[]{:S(2)}) async-start(), calls=%async_computation.18 | async-start | bytes 4194304 | tf_op jit(solution)/shard_map/psum | solution.py:93
  952.0 328.0 %reduce-scatter.29.cloned.1.call-start = ((), (), s32[]{:S(2)}) async-start(), calls=%async_computation.29 | async-start | bytes 12976128 | tf_op jit(solution)/shard_map/reduce_scatter | solution.py:158
  962.4 25.0 %copy-start.1 = (bf16[512,2048]{1,0:T(8,128)(2,1)S(1)}, bf16[512,2048]{1,0:T(8,128)(2,1)}, u32[]{:S(2)}) copy-start(bf16[512,2048]{1,0:T(8,128)(2,1)} %param.21) | copy-start | bytes 6291460
  962.4 25.0 %copy-start.30 = (f32[2048]{0:T(1024)S(1)}, f32[2048]{0:T(1024)}, u32[]{:S(2)}) copy-start(f32[2048]{0:T(1024)} %param.25) | copy-start | bytes 24580
  962.4 25.0 %copy-start.35 = (f32[512]{0:T(512)S(1)}, f32[512]{0:T(512)}, u32[]{:S(2)}) copy-start(f32[512]{0:T(512)} %copy-done.34) | copy-start | bytes 6148
  962.4 388.2 %reduce-scatter.21.cloned.1.call-start = ((), (), s32[]{:S(2)}) async-start(), calls=%async_computation.25 | async-start | bytes 2359296 | tf_op jit(solution)/shard_map/reduce_scatter | solution.py:219
  989.7 431.6 %reduce-scatter.19.cloned.1.call-start = ((), (), s32[]{:S(2)}) async-start(), calls=%async_computation.24 | async-start | bytes 2359296 | tf_op jit(solution)/shard_map/reduce_scatter | solution.py:218
  1035.1 477.4 %reduce-scatter.17.cloned.1.call-start = ((), (), s32[]{:S(2)}) async-start(), calls=%async_computation.23 | async-start | bytes 4718592 | tf_op jit(solution)/shard_map/reduce_scatter | solution.py:217
  1041.2 624.7 %reduce-scatter.23.cloned.1.call-start = ((), (), s32[]{:S(2)}) async-start(), calls=%async_computation.26 | async-start | bytes 9437184 | tf_op jit(solution)/shard_map/reduce_scatter | solution.py:220
  1050.4 811.3 %reduce-scatter.25.cloned.1.call-start = ((), (), s32[]{:S(2)}) async-start(), calls=%async_computation.27 | async-start | bytes 12976128 | tf_op jit(solution)/shard_map/reduce_scatter | solution.py:156
  1060.2 997.5 %reduce-scatter.27.cloned.1.call-start = ((), (), s32[]{:S(2)}) async-start(), calls=%async_computation.28 | async-start | bytes 12976128 | tf_op jit(solution)/shard_map/reduce_scatter | solution.py:157
  1070.2 1139.9 %reduce-scatter.15.cloned.1.call-start = ((), (), s32[]{:S(2)}) async-start(), calls=%async_computation.22 | async-start | bytes 9437184 | tf_op jit(solution)/shard_map/reduce_scatter | solution.py:215
  (54 other events, 169.9 us)
Sparse Core Ops, SparseCore 0:
  10.1 42.8 all-gather.12
  55.2 39.1 all-gather.14
  96.5 72.1 all-gather.8
  170.7 47.5 all-gather.10
  220.2 71.8 all-gather.16
  299.2 83.7 all-reduce.13
  385.4 92.7 all-gather.20
  480.6 90.8 all-gather.18
  573.9 90.8 all-gather.22
  685.6 151.4 all-reduce.17
  918.2 20.4 reduce-scatter.10
  940.7 20.3 reduce-scatter.12
  963.8 65.4 all-reduce.15
  1031.6 51.4 all-reduce.11
  1086.6 193.3 reduce-scatter.28
  1284.0 66.6 reduce-scatter.20
  1354.6 66.6 reduce-scatter.18
  1425.4 87.0 reduce-scatter.16
  1517.1 148.7 reduce-scatter.22
  1669.9 191.6 reduce-scatter.24
  1865.8 191.7 reduce-scatter.26
  2061.9 148.1 reduce-scatter.14
where the time goes:
time: 2230 us; the launch traced here: 2220 us
  waiting for transfers between devices  1810 us (81%)
  matrix products  225 us (10%)
  blocking collectives  80.5 us (4%)
  local copies, waits for them, and re-layouts  44.8 us (2%)
  other arithmetic  42.6 us (2%)
    reduce_scatter x1, waiting for transfers between devices, backward(): lax.psum_scatter(grad_up_w, ('dp', 'ctx'), scatter_dimension=0, tiled=True)  196 us
    reduce_scatter x1, waiting for transfers between devices, backward(): lax.psum_scatter(grad_gate_w, ('dp', 'ctx'), scatter_dimension=0, tiled=T...  196 us
    reduce_scatter x1, waiting for transfers between devices, backward(): lax.psum_scatter(grad_out_w, ('dp', 'ctx'), scatter_dimension=0, tiled=True)  153 us
    reduce_scatter x1, waiting for transfers between devices, backward(): lax.psum_scatter(grad_down_q, ('dp', 'ctx'), scatter_dimension=0, tiled=T...  152 us
    psum x1, waiting for transfers between devices, backward(): lax.psum(times_trans(grad_gate, gate_w) + times_trans(grad_up, up_w), 'te...  151 us
    reduce_scatter x1, waiting for transfers between devices, backward(): lax.psum_scatter(grad_down, ('dp', 'ctx'), scatter_dimension=0, tiled=True)  140 us
    reduce_scatter x1, waiting for transfers between devices, backward(): lax.psum_scatter(grad_up_q, ('dp', 'ctx'), scatter_dimension=0, tiled=True)  91.2 us
    all_gather x1, waiting for transfers between devices, per_device(): lax.all_gather(up_w, ('dp', 'ctx'), axis=0, tiled=True)  89.8 us
  transfers between devices with their start and end apart: 22, of which 20 were waited for; matrix products, arithmetic and copies ran while one was open for 9% of the time, Pallas kernels for 0%

commit v1 on v0

--- a/solution.py
+++ b/solution.py
@@ -1,6 +1,8 @@
 import jax
 import jax.numpy as jnp
 from jax import lax
+from jax.experimental import pallas as pl
+from jax.experimental.pallas import tpu as pltpu
 from jax.sharding import PartitionSpec as P
 
 HD = 256
@@ -8,17 +10,21 @@
 
 EPSILON = 1e-06
 
+AXES = ("dp", "ctx", "tensor")
+BF = jnp.bfloat16
+F32 = jnp.float32
+
+
+def dot(left, right):
+    return jnp.dot(left, right, preferred_element_type=F32)
+
 
 def times_trans(left, right):
-    return lax.dot_general(
-        left, right, (((1,), (1,)), ((), ())), preferred_element_type=jnp.float32
-    )
+    return lax.dot_general(left, right, (((1,), (1,)), ((), ())), preferred_element_type=F32)
 
 
 def trans_times(left, right):
-    return lax.dot_general(
-        left, right, (((0,), (0,)), ((), ())), preferred_element_type=jnp.float32
-    )
+    return lax.dot_general(left, right, (((0,), (0,)), ((), ())), preferred_element_type=F32)
 
 
 def rms_parts(array):
@@ -30,6 +36,424 @@
     grad_plain = grad_out * gain
     grad_in = inverse * (grad_plain - plain * jnp.mean(grad_plain * plain, axis=-1, keepdims=True))
     return (grad_in, jnp.sum(grad_out * plain, axis=0))
+
+
+def angles_of(places, half):
+    freqs = 10000.0 ** (-jnp.arange(half, dtype=F32) / half)
+    angles = places[:, None] * freqs[None, :]
+    return (jnp.cos(angles), jnp.sin(angles))
+
+
+def turn(array, cosine, sine):
+    half = array.shape[-1] // 2
+    first = array[..., :half]
+    latter = array[..., half:]
+    return jnp.concatenate(
+        [first * cosine - latter * sine, latter * cosine + first * sine], axis=-1
+    )
+
+
+def routes(move):
+    pairs = []
+    for z in range(4):
+        for x in range(2):
+            for y in range(2):
+                for c in range(2):
+                    to = move(z, x, y, c)
+                    if to is not None:
+                        tz, tx, ty, tc = to
+                        pairs.append(
+                            (((z * 2 + x) * 2 + y) * 2 + c, ((tz * 2 + tx) * 2 + ty) * 2 + tc)
+                        )
+    return pairs
+
+
+OVER_X = routes(lambda z, x, y, c: (z, 1 - x, y, c))
+OVER_Y = routes(lambda z, x, y, c: (z, x, 1 - y, c))
+OVER_XY = routes(lambda z, x, y, c: (z, 1 - x, 1 - y, c))
+OVER_C = routes(lambda z, x, y, c: (z, x, y, 1 - c))
+TRANSPOSE = routes(lambda z, x, y, c: (z, c, y, x))
+Z_ONE = routes(lambda z, x, y, c: (z ^ 1, x, y, c))
+Z_TWO = routes(lambda z, x, y, c: (z ^ 2, x, y, c))
+Z_THREE = routes(lambda z, x, y, c: (z ^ 3, x, y, c))
+Z_INNER = routes(lambda z, x, y, c: (3 - z, x, y, c) if z in (1, 2) else None)
+Z_OUTWARD = routes(lambda z, x, y, c: ({1: 0, 2: 3}[z], x, y, c) if z in (1, 2) else None)
+Z_INWARD = routes(lambda z, x, y, c: ({0: 1, 3: 2}[z], x, y, c) if z in (0, 3) else None)
+
+
+def send(array, pairs):
+    return lax.ppermute(array, AXES, pairs)
+
+
+def gather_z(array, inner):
+    one = send(array, Z_ONE)
+    two = send(array, Z_TWO)
+    middle = send(array, Z_INNER)
+    passed = send(two, Z_OUTWARD)
+    three = jnp.where(inner, middle, passed)
+    return [array, one, two, three]
+
+
+def reduce_z(slabs):
+    own, one, two, three = slabs
+    passed = send(three, Z_INWARD)
+    got_one = send(one, Z_ONE)
+    got_three = send(three, Z_INNER)
+    got_two = send((two.astype(F32) + passed.astype(F32)).astype(BF), Z_TWO)
+    return own.astype(F32) + got_one.astype(F32) + got_two.astype(F32) + got_three.astype(F32)
+
+
+def extract_columns(array, block, picks):
+    rows = array.shape[0]
+    count = picks.shape[0]
+
+    def body(picks_ref, in_ref, out_ref):
+        out_ref[...] = in_ref[...]
+
+    return pl.pallas_call(
+        body,
+        grid_spec=pltpu.PrefetchScalarGridSpec(
+            num_scalar_prefetch=1,
+            grid=(count,),
+            in_specs=[pl.BlockSpec((rows, block), lambda i, picks_ref: (0, picks_ref[i]))],
+            out_specs=pl.BlockSpec((rows, block), lambda i, picks_ref: (0, i)),
+        ),
+        out_shape=jax.ShapeDtypeStruct((rows, count * block), array.dtype),
+        cost_estimate=pl.CostEstimate(
+            flops=0, bytes_accessed=2 * rows * count * block * 2, transcendentals=0
+        ),
+    )(picks, array)
+
+
+def assemble_rows(blocks, picks):
+    rows, columns = blocks[0].shape
+    count = len(blocks)
+
+    def body(picks_ref, *refs):
+        ins = refs[:count]
+        out_ref = refs[count]
+        sems = refs[count + 1]
+        copies = []
+        for i in range(count):
+            start = pl.multiple_of(picks_ref[i] * rows, rows)
+            copy = pltpu.make_async_copy(ins[i], out_ref.at[pl.ds(start, rows)], sems.at[i])
+            copy.start()
+            copies.append(copy)
+        for copy in copies:
+            copy.wait()
+
+    return pl.pallas_call(
+        body,
+        grid_spec=pltpu.PrefetchScalarGridSpec(
+            num_scalar_prefetch=1,
+            grid=(1,),
+            in_specs=[pl.BlockSpec(memory_space=pl.ANY)] * count,
+            out_specs=pl.BlockSpec((count * rows, columns), lambda i, picks_ref: (0, 0)),
+            scratch_shapes=[pltpu.SemaphoreType.DMA((count,))],
+        ),
+        out_shape=jax.ShapeDtypeStruct((count * rows, columns), blocks[0].dtype),
+        compiler_params=pltpu.CompilerParams(vmem_limit_bytes=40 * 1024 * 1024),
+        cost_estimate=pl.CostEstimate(
+            flops=0, bytes_accessed=4 * rows * count * columns, transcendentals=0
+        ),
+    )(picks, *blocks)
+
+
+def rows_at(array, start, count):
+    return lax.dynamic_slice_in_dim(array, start, count, axis=0)
+
+
+def both(own, other, index):
+    return jnp.where(
+        index == 0, jnp.concatenate([own, other], 0), jnp.concatenate([other, own], 0)
+    )
+
+
+def both_columns(own, other, index):
+    return jnp.where(
+        index == 0, jnp.concatenate([own, other], 1), jnp.concatenate([other, own], 1)
+    )
+
+
+def plane_reduce(partial, quarter):
+    part = partial.shape[0] // 4
+    low = partial.astype(BF)
+
+    def piece(flip):
+        return rows_at(low, (quarter ^ flip) * part, part)
+
+    got_x = send(piece(2), OVER_X)
+    got_y = send(piece(1), OVER_Y)
+    got_xy = send(piece(3), OVER_XY)
+    return (
+        rows_at(partial, quarter * part, part).astype(F32)
+        + got_x.astype(F32)
+        + got_y.astype(F32)
+        + got_xy.astype(F32)
+    )
+
+
+def plane_gather(part, quarter_picks):
+    got_x = send(part, OVER_X)
+    got_y = send(part, OVER_Y)
+    got_xy = send(part, OVER_XY)
+    return assemble_rows([part, got_y, got_x, got_xy], quarter_picks)
+
+
+def fast_device(
+    tokens_in,
+    cotangent,
+    seq_lengths,
+    block_order,
+    gain_one,
+    down_q,
+    gain_q,
+    up_q,
+    key_w,
+    value_w,
+    out_w,
+    gain_two,
+    gate_w,
+    up_w,
+    down_w,
+):
+    z = lax.axis_index("dp")
+    x = lax.axis_index("ctx")
+    t = lax.axis_index("tensor")
+    y = t // 2
+    c = t % 2
+    inner = (z == 1) | (z == 2)
+    quarter = x * 2 + y
+    ks = jnp.arange(4, dtype=jnp.int32)
+    z_order = z ^ ks
+    own_blocks = z_order * 2 + c
+    other_blocks = z_order * 2 + (1 - c)
+    all_blocks = jnp.concatenate([own_blocks, other_blocks])
+    x_blocks = z_order * 2 + x
+    x_all_blocks = jnp.concatenate([x_blocks, z_order * 2 + (1 - x)])
+    quarter_picks = quarter ^ ks
+    rows = tokens_in.shape[0]
+    half = rows // 2
+    part = rows // 4
+    latent_width = down_q.shape[1]
+
+    first_w = jnp.concatenate([down_q, key_w, value_w], axis=1)
+    wide = first_w.shape[1]
+    side = wide // 2
+    mine = lax.dynamic_slice_in_dim(first_w, c * side, side, axis=1)
+    tok_half = rows_at(tokens_in, c * half, half)
+    tok_got = send(tok_half, OVER_X)
+    mine_all = gather_z(mine, inner)
+    over_all = [send(w, OVER_X) for w in mine_all]
+    tok_other = both(tok_got, send(tok_got, OVER_C), c)
+    tokens = both(tokens_in, tok_other, x)
+    own_side = jnp.concatenate(mine_all + over_all, axis=0)
+    other_side = send(own_side, OVER_C)
+    first_all = both_columns(own_side, other_side, c)
+    first_all = assemble_rows(
+        [first_all[i * 256 : (i + 1) * 256] for i in range(8)], x_all_blocks
+    )
+
+    upq_t = send(up_q, TRANSPOSE)
+    upq_all = gather_z(upq_t, inner)
+    cols = up_q.shape[1] // 2
+
+    def head_side(blocks):
+        keep = [lax.dynamic_slice_in_dim(w, c * cols, cols, axis=1) for w in blocks]
+        give = [lax.dynamic_slice_in_dim(w, (1 - c) * cols, cols, axis=1) for w in blocks]
+        got = [send(w, OVER_C) for w in give]
+        return assemble_rows(keep + got, all_blocks)
+
+    up_q_all = head_side(upq_all)
+    out_t = send(out_w, TRANSPOSE)
+    out_all = head_side(gather_z(out_t, inner))
+
+    def ffn_weight(w):
+        own = gather_z(send(w, TRANSPOSE), inner)
+        got = [send(v, OVER_C) for v in own]
+        return assemble_rows(own + got, all_blocks)
+
+    gate_all = ffn_weight(gate_w)
+    up_all = ffn_weight(up_w)
+    down_all = ffn_weight(down_w)
+
+    cot_got = send(rows_at(cotangent, c * half, half), OVER_X)
+    cot_other = both(cot_got, send(cot_got, OVER_C), c)
+    cot = both(cotangent, cot_other, x)
+
+    block_rows = rows // 2
+    places = (
+        block_order[0][:, :, None] * block_rows
+        + jnp.arange(block_rows, dtype=jnp.int32)[None, None, :]
+    ).reshape(-1)
+    second = (places >= seq_lengths[0, 0]).astype(jnp.int32)
+    pos = (places - second * seq_lengths[0, 0]).astype(F32)
+    allowed = (second[:, None] == second[None, :]) & (places[None, :] <= places[:, None])
+    cosine, sine = angles_of(pos, HD // 2)
+    scale = HD ** (-0.5)
+
+    plain_one, inverse_one = rms_parts(tokens.astype(F32))
+    normed = (plain_one * gain_one).astype(BF)
+    lat = dot(normed, first_all)
+    latent = lat[:, :latent_width]
+    plain_q, inverse_q = rms_parts(latent)
+    query_in = (plain_q * gain_q).astype(BF)
+    keys = turn(lat[:, latent_width : latent_width + HD], cosine, sine).astype(BF)
+    values = lat[:, latent_width + HD :].astype(BF)
+    query_pre = dot(query_in, up_q_all)
+    heads = cols // HD
+    queries = []
+    softs = []
+    mixed = []
+    for h in range(heads):
+        q = turn(query_pre[:, h * HD : (h + 1) * HD], cosine, sine).astype(BF)
+        scores = jnp.where(allowed, times_trans(q, keys) * scale, -1e30)
+        largest = jnp.max(scores, axis=-1, keepdims=True)
+        exponent = jnp.exp(scores - largest)
+        soft = exponent / jnp.sum(exponent, axis=-1, keepdims=True)
+        queries.append(q)
+        softs.append(soft)
+        mixed.append(dot(soft.astype(BF), values).astype(BF))
+    attended = jnp.concatenate(mixed, axis=1)
+    give = times_trans(rows_at(attended, (1 - c) * rows, rows), out_all).astype(BF)
+    keep = times_trans(rows_at(attended, c * rows, rows), out_all)
+    branch = keep + send(give, OVER_C).astype(F32)
+    own_row = c * rows + quarter * part
+    middle = rows_at(tokens, own_row, part).astype(F32) + plane_reduce(branch, quarter)
+
+    plain_two, inverse_two = rms_parts(middle)
+    normed_two = plane_gather((plain_two * gain_two).astype(BF), quarter_picks)
+    gate_pre = dot(normed_two, gate_all)
+    up_pre = dot(normed_two, up_all)
+    sigma = jax.nn.sigmoid(gate_pre)
+    silu = gate_pre * sigma
+    hidden = (silu * up_pre).astype(BF)
+    cot_c = rows_at(cot, c * rows, rows)
+    grad_hidden = dot(cot_c, down_all)
+    grad_gate = (grad_hidden * up_pre * sigma * (1.0 + gate_pre * (1.0 - sigma))).astype(BF)
+    grad_up = (grad_hidden * silu).astype(BF)
+    grad_norm_two = plane_reduce(
+        times_trans(grad_gate, gate_all) + times_trans(grad_up, up_all), quarter
+    )
+    out_part = middle + plane_reduce(times_trans(hidden, down_all), quarter)
+    out_c = plane_gather(out_part.astype(BF), quarter_picks)
+    result = jnp.where(x == c, out_c, send(out_c, OVER_C))
+
+    def with_other(array):
+        return jnp.concatenate([array, send(array, OVER_C)], axis=0)
+
+    def own_half(array):
+        mine_cols = extract_columns(array, 256, own_blocks)
+        give_cols = extract_columns(array, 256, other_blocks)
+        return jnp.concatenate([mine_cols, send(give_cols, OVER_C)], axis=0)
+
+    def slabs_of(grad):
+        low = grad.astype(BF)
+        n = low.shape[0] // 4
+        return [low[i * n : (i + 1) * n] for i in range(4)]
+
+    def home(grad):
+        return send(reduce_z(slabs_of(grad)).astype(BF), TRANSPOSE).astype(F32)
+
+    cot_own = jnp.concatenate(
+        [
+            extract_columns(cot_c, 256, own_blocks),
+            extract_columns(rows_at(cot, (1 - c) * rows, rows), 256, own_blocks),
+        ],
+        axis=0,
+    )
+    grad_down_w = home(trans_times(cot_own, with_other(hidden)))
+    normed_two_own = own_half(normed_two)
+    grad_gate_w = home(trans_times(normed_two_own, with_other(grad_gate)))
+    grad_up_w = home(trans_times(normed_two_own, with_other(grad_up)))
+
+    cot_mine = rows_at(cot, own_row, part).astype(F32)
+    grad_mid, gain_two_part = rms_back(grad_norm_two, plain_two, inverse_two, gain_two)
+    grad_branch_c = plane_gather((cot_mine + grad_mid).astype(BF), quarter_picks)
+    grad_branch = both(grad_branch_c, send(grad_branch_c, OVER_C), c)
+    grad_attended = dot(grad_branch, out_all).astype(BF)
+    key_acc = 0.0
+    value_acc = 0.0
+    grad_queries = []
+    for h in range(heads):
+        grad_head = grad_attended[:, h * HD : (h + 1) * HD]
+        soft = softs[h]
+        grad_soft = times_trans(grad_head, values)
+        summed = jnp.sum(soft * grad_soft, axis=-1, keepdims=True)
+        grad_scores = (soft * (grad_soft - summed)).astype(BF)
+        grad_q = dot(grad_scores, keys) * scale
+        key_acc = key_acc + trans_times(grad_scores, queries[h]) * scale
+        value_acc = value_acc + trans_times(soft.astype(BF), grad_head)
+        grad_queries.append(turn(grad_q, cosine, -sine).astype(BF))
+    grad_query_pre = jnp.concatenate(grad_queries, axis=1)
+    grad_qin = times_trans(grad_query_pre, up_q_all)
+    low_three = jnp.concatenate([grad_qin, key_acc, value_acc], axis=1).astype(BF)
+    got_three = send(rows_at(low_three, (1 - c) * rows, rows), OVER_C)
+    three = rows_at(low_three, c * rows, rows).astype(F32) + got_three.astype(F32)
+    three = plane_reduce(three, quarter)
+    plain_q_mine = rows_at(plain_q, own_row, part)
+    inverse_q_mine = rows_at(inverse_q, own_row, part)
+    grad_latent, gain_q_part = rms_back(
+        three[:, :latent_width], plain_q_mine, inverse_q_mine, gain_q
+    )
+    grad_key_pre = turn(
+        three[:, latent_width : latent_width + HD],
+        rows_at(cosine, own_row, part),
+        -rows_at(sine, own_row, part),
+    )
+    low_lat = jnp.concatenate(
+        [grad_latent, grad_key_pre, three[:, latent_width + HD :]], axis=1
+    ).astype(BF)
+    low_lat_c = plane_gather(low_lat, quarter_picks)
+    grad_lat = both(low_lat_c, send(low_lat_c, OVER_C), c)
+
+    grad_lat_x = rows_at(grad_lat, x * rows, rows)
+    grad_norm_one = times_trans(grad_lat_x, first_all)
+    grad_in, gain_one_part = rms_back(
+        grad_norm_one, rows_at(plain_one, x * rows, rows), rows_at(inverse_one, x * rows, rows), gain_one
+    )
+    grad_tokens = rows_at(grad_branch, x * rows, rows).astype(F32) + grad_in
+
+    attended_all = both_columns(attended, send(attended, OVER_C), c)
+    grad_out_w = home(trans_times(extract_columns(grad_branch, 256, own_blocks), attended_all))
+    query_pre_all = both_columns(grad_query_pre, send(grad_query_pre, OVER_C), c)
+    grad_up_q = home(trans_times(extract_columns(query_in, 128, own_blocks), query_pre_all))
+    lane = wide // 4
+    grad_lat_t = lax.dynamic_slice_in_dim(grad_lat, t * lane, lane, axis=1)
+    first_quarter = reduce_z(
+        slabs_of(trans_times(extract_columns(normed, 256, x_blocks), grad_lat_t))
+    ).astype(BF)
+    first_half = both_columns(first_quarter, send(first_quarter, OVER_C), c)
+    grad_first = both_columns(first_half, send(first_half, OVER_Y), y).astype(F32)
+
+    gains = lax.psum(
+        jnp.concatenate([gain_two_part, gain_q_part, gain_one_part * 0.25]), AXES
+    )
+    dev = z * 2 + x
+    d = gain_one.shape[0]
+    grad_gain_two = lax.dynamic_slice_in_dim(gains, dev * (d // 8), d // 8)
+    grad_gain_q = lax.dynamic_slice_in_dim(
+        gains, d + dev * (latent_width // 8), latent_width // 8
+    )
+    grad_gain_one = lax.dynamic_slice_in_dim(
+        gains, d + latent_width + dev * (d // 8), d // 8
+    )
+
+    return (
+        result,
+        grad_tokens,
+        grad_gain_one,
+        grad_first[:, :latent_width],
+        grad_gain_q,
+        grad_up_q,
+        grad_first[:, latent_width : latent_width + HD],
+        grad_first[:, latent_width + HD :],
+        grad_out_w,
+        grad_gain_two,
+        grad_gate_w,
+        grad_up_w,
+        grad_down_w,
+    )
 
 
 def rotate(array, places):
@@ -305,8 +729,9 @@
 
 
 def solution(mesh):
+    fast = dict(mesh.shape) == {"dp": 4, "ctx": 2, "tensor": 4}
     return jax.shard_map(
-        per_device,
+        fast_device if fast else per_device,
         mesh=mesh,
         in_specs=(
             P(("dp", "ctx"), None),

time: 2230 us -> 955 us (0.43)
  waiting for transfers between devices: 1810 us -> 431 us
  starting transfers between devices: 1.51 us -> 186 us
  matrix products: 225 us -> 87.7 us
  other arithmetic: 42.6 us -> 91.5 us
  Pallas kernels: 0 us -> 45.7 us
  blocking collectives: 80.5 us -> 57.1 us
    reduce_scatter x10 -> x0, waiting for transfers between devices: 1080 us -> none  [the longest x1 196 us: backward(): lax.psum_scatter(grad_up_w, ('dp', 'ctx'), scatter_dimension=0, tiled=True)]
    all_gather x8 -> x0, waiting for transfers between devices: 472 us -> none  [the longest x1 89.8 us: per_device(): lax.all_gather(up_w, ('dp', 'ctx'), axis=0, tiled=True)]
    ppermute x0 -> x124, waiting for transfers between devices: none -> 431 us  [send(): return lax.ppermute(array, AXES, pairs)]
    psum x4 -> x0, waiting for transfers between devices: 251 us -> none  [the longest x1 151 us: backward(): lax.psum(times_trans(grad_gate, gate_w) + times_trans(grad_up, up_w), 'te...]
    ppermute x0 -> x124, starting transfers between devices: none -> 186 us  [send(): return lax.ppermute(array, AXES, pairs)]
    dot_general x16 -> x10, matrix products: 74.3 us -> 24.8 us  [trans_times(): lax.dot_general(left, right, (((0,), (0,)), ((), ())), preferred_element_...]
    pallas_call x0 -> x17, Pallas kernels: none -> 45.7 us  [the longest x7 29.6 us: extract_columns(): pl.pallas_call(body, grid_spec=pltpu.PrefetchScalarGridSpec(num_scalar_pr...]
    dot_general x21 -> x10, matrix products: 73.5 us -> 27.9 us  [dot(): return jnp.dot(left, right, preferred_element_type=F32)]
  transfers between devices with their start and end apart: 22 -> 124, of which waited for: 20 -> 48; matrix products, arithmetic and copies ran while one was open for 9% -> 18% of each run, Pallas kernels for 0% -> 5%
where the time goes in v1:
time: 955 us; the launch traced here: 945 us
  waiting for transfers between devices  431 us (45%)
  starting transfers between devices  186 us (19%)
  other arithmetic  91.5 us (10%)
  matrix products  87.7 us (9%)
  blocking collectives  57.1 us (6%)
  Pallas kernels  45.7 us (5%)
  local copies, waits for them, and re-layouts  43.6 us (5%)
    ppermute x124, waiting for transfers between devices, send(): return lax.ppermute(array, AXES, pairs)  431 us
    ppermute x124, starting transfers between devices, send(): return lax.ppermute(array, AXES, pairs)  186 us
    psum x1, blocking collectives, fast_device(): lax.psum(jnp.concatenate([gain_two_part, gain_q_part, gain_one_part * 0.2...  57.1 us
    dot_general x11, matrix products, times_trans(): lax.dot_general(left, right, (((1,), (1,)), ((), ())), preferred_element_...  35.1 us
    pallas_call x7, Pallas kernels, extract_columns(): pl.pallas_call(body, grid_spec=pltpu.PrefetchScalarGridSpec(num_scalar_pr...  29.6 us
    dot_general x10, matrix products, dot(): return jnp.dot(left, right, preferred_element_type=F32)  27.9 us
    unnamed x237, local copies, waits for them, and re-layouts  26.5 us
    dot_general x10, matrix products, trans_times(): lax.dot_general(left, right, (((0,), (0,)), ((), ())), preferred_element_...  24.8 us
  transfers between devices with their start and end apart: 124, of which 48 were waited for; matrix products, arithmetic and copies ran while one was open for 18% of the time, Pallas kernels for 5%

profile of v1, /device:TPU:0, one launch (start us, length us, event | category | flops | bytes accessed | tf_op | source)
XLA Modules:
  0.0 945.5 jit_solution(13506497074214813166)
XLA Ops:
  22.2 19.2 %collective-permute-done.3 = bf16[256,768]{1,0:T(8,128)(2,1)S(1)} collective-permute-done((bf16[256,768]{1,0:T(8,128)(2,1)S(1)}, bf16[256,768]{1,0:T(8,128)(2,1)S(1)}, u32[]{:S(2)}, u32[]{:S(2)}) %collective-permute-start.3) | collective-permute-done | bytes 393248 | tf_op jit(solution)/shard_map/ppermute | solution.py:85
  64.9 22.6 %collective-permute-done.8 = bf16[256,768]{1,0:T(8,128)(2,1)S(1)} collective-permute-done((bf16[256,768]{1,0:T(8,128)(2,1)S(1)}, bf16[256,768]{1,0:T(8,128)(2,1)S(1)}, u32[]{:S(2)}, u32[]{:S(2)}) %collective-permute-start.8) | collective-permute-done | bytes 393248 | tf_op jit(solution)/shard_map/ppermute | solution.py:85
  88.8 7.1 collective-permute-done.7
  96.7 7.6 collective-permute-done.9
  129.4 6.8 collective-permute-start.45
  192.9 12.8 %collective-permute-start.48 = (bf16[256,1408]{1,0:T(8,128)(2,1)}, bf16[256,1408]{1,0:T(8,128)(2,1)S(1)}, u32[]{:S(2)}, u32[]{:S(2)}) collective-permute-start(bf16[256,1408]{1,0:T(8,128)(2,1)} %collective-permute-done.45.refs_0_), channel_id=1, source_target_pairs={{8,16},{9,17},{10,18},{11,19},{12,20},{13,21},{14,22},{15,23},{16,... | collective-permute-start | bytes 2162696 | tf_op jit(solution)/shard_map/ppermute | solution.py:85
  210.3 15.2 %collective-permute-done.38.refs_2_ = bf16[256,1408]{1,0:T(8,128)(2,1)} collective-permute-done((bf16[256,1408]{1,0:T(8,128)(2,1)}, bf16[256,1408]{1,0:T(8,128)(2,1)}, u32[]{:S(2)}, u32[]{:S(2)}) %collective-permute-start.38) | collective-permute-done | bytes 720928 | tf_op jit(solution)/shard_map/ppermute | solution.py:85
  231.9 54.5 %collective-permute-done.47.refs_2_ = bf16[256,1408]{1,0:T(8,128)(2,1)} collective-permute-done((bf16[256,1408]{1,0:T(8,128)(2,1)}, bf16[256,1408]{1,0:T(8,128)(2,1)}, u32[]{:S(2)}, u32[]{:S(2)}) %collective-permute-start.47) | collective-permute-done | bytes 720928 | tf_op jit(solution)/shard_map/ppermute | solution.py:85
  286.4 14.6 %collective-permute-done.56.refs_2_ = bf16[256,1408]{1,0:T(8,128)(2,1)} collective-permute-done((bf16[256,1408]{1,0:T(8,128)(2,1)}, bf16[256,1408]{1,0:T(8,128)(2,1)}, u32[]{:S(2)}, u32[]{:S(2)}) %collective-permute-start.56) | collective-permute-done | bytes 720928 | tf_op jit(solution)/shard_map/ppermute | solution.py:85
  308.9 7.4 collective-permute-done.46.refs_1_
  318.6 13.2 %collective-permute-done.49 = bf16[256,1408]{1,0:T(8,128)(2,1)S(1)} collective-permute-done((bf16[256,1408]{1,0:T(8,128)(2,1)}, bf16[256,1408]{1,0:T(8,128)(2,1)S(1)}, u32[]{:S(2)}, u32[]{:S(2)}) %collective-permute-start.49) | collective-permute-done | bytes 720928 | tf_op jit(solution)/shard_map/ppermute | solution.py:85
  331.7 15.4 %collective-permute-done.58 = bf16[256,1408]{1,0:T(8,128)(2,1)S(1)} collective-permute-done((bf16[256,1408]{1,0:T(8,128)(2,1)}, bf16[256,1408]{1,0:T(8,128)(2,1)S(1)}, u32[]{:S(2)}, u32[]{:S(2)}) %collective-permute-start.58) | collective-permute-done | bytes 720928 | tf_op jit(solution)/shard_map/ppermute | solution.py:85
  348.0 14.7 %collective-permute-done.55.refs_1_ = bf16[256,1408]{1,0:T(8,128)(2,1)} collective-permute-done((bf16[256,1408]{1,0:T(8,128)(2,1)}, bf16[256,1408]{1,0:T(8,128)(2,1)}, u32[]{:S(2)}, u32[]{:S(2)}) %collective-permute-start.55) | collective-permute-done | bytes 720928 | tf_op jit(solution)/shard_map/ppermute | solution.py:85
  409.2 7.3 collective-permute-done.35.refs_3_
  416.5 7.1 collective-permute-done.34.refs_2_
  461.2 10.7 %collective-permute-done.74 = bf16[128,2048]{1,0:T(8,128)(2,1)S(1)} collective-permute-done((bf16[128,2048]{1,0:T(8,128)(2,1)S(1)}, bf16[128,2048]{1,0:T(8,128)(2,1)S(1)}, u32[]{:S(2)}, u32[]{:S(2)}) %collective-permute-start.74) | collective-permute-done | bytes 524320 | tf_op jit(solution)/shard_map/ppermute | solution.py:85
  474.2 8.9 collective-permute-done.63
  483.1 10.4 %collective-permute-done.65 = bf16[128,2048]{1,0:T(8,128)(2,1)S(1)} collective-permute-done((bf16[128,2048]{1,0:T(8,128)(2,1)S(1)}, bf16[128,2048]{1,0:T(8,128)(2,1)S(1)}, u32[]{:S(2)}, u32[]{:S(2)}) %collective-permute-start.65) | collective-permute-done | bytes 524320 | tf_op jit(solution)/shard_map/ppermute | solution.py:85
  504.2 8.2 collective-permute-done.77.refs_3_
  514.7 9.0 collective-permute-done.76.refs_2_
  525.5 9.4 collective-permute-done.68.refs_3_
  595.5 10.1 %collective-permute-done.114 = bf16[256,1408]{1,0:T(8,128)(2,1)S(1)} collective-permute-done((bf16[256,1408]{1,0:T(8,128)(2,1)}, bf16[256,1408]{1,0:T(8,128)(2,1)S(1)}, u32[]{:S(2)}, u32[]{:S(2)}) %collective-permute-start.114) | collective-permute-done | bytes 720928 | tf_op jit(solution)/shard_map/ppermute | solution.py:85
  609.0 11.9 %collective-permute-done.120 = bf16[256,1408]{1,0:T(8,128)(2,1)S(1)} collective-permute-done((bf16[256,1408]{1,0:T(8,128)(2,1)S(1)}, bf16[256,1408]{1,0:T(8,128)(2,1)S(1)}, u32[]{:S(2)}, u32[]{:S(2)}) %collective-permute-start.120) | collective-permute-done | bytes 720928 | tf_op jit(solution)/shard_map/ppermute | solution.py:85
  670.7 29.9 %collective-permute-done.115 = bf16[256,1408]{1,0:T(8,128)(2,1)S(1)} collective-permute-done((bf16[256,1408]{1,0:T(8,128)(2,1)S(1)}, bf16[256,1408]{1,0:T(8,128)(2,1)S(1)}, u32[]{:S(2)}, u32[]{:S(2)}) %collective-permute-start.115) | collective-permute-done | bytes 720928 | tf_op jit(solution)/shard_map/ppermute | solution.py:85
  728.3 8.3 collective-permute-done.82
  746.6 8.2 collective-permute-done.85.refs_3_
  763.9 23.6 %collective-permute-start.102 = (bf16[256,1024]{1,0:T(8,128)(2,1)S(1)}, bf16[256,1024]{1,0:T(8,128)(2,1)S(1)}, u32[]{:S(2)}, u32[]{:S(2)}) collective-permute-start(bf16[256,1024]{1,0:T(8,128)(2,1)S(1)} %add_convert_fusion.7), channel_id=1, source_target_pairs={{0,16},{1,17},{2,18},{3,19},{4,20},{5,21},{6,22},{7,23},{8,24},{9,... | collective-permute-start | bytes 1572872 | tf_op jit(solution)/shard_map/ppermute | solution.py:85
  787.5 20.3 %collective-permute-done.121 = bf16[256,1408]{1,0:T(8,128)(2,1)S(1)} collective-permute-done((bf16[256,1408]{1,0:T(8,128)(2,1)S(1)}, bf16[256,1408]{1,0:T(8,128)(2,1)S(1)}, u32[]{:S(2)}, u32[]{:S(2)}) %collective-permute-start.121) | collective-permute-done | bytes 720928 | tf_op jit(solution)/shard_map/ppermute | solution.py:85
  816.7 11.4 %collective-permute-done.102 = bf16[256,1024]{1,0:T(8,128)(2,1)S(1)} collective-permute-done((bf16[256,1024]{1,0:T(8,128)(2,1)S(1)}, bf16[256,1024]{1,0:T(8,128)(2,1)S(1)}, u32[]{:S(2)}, u32[]{:S(2)}) %collective-permute-start.102) | collective-permute-done | bytes 524320 | tf_op jit(solution)/shard_map/ppermute | solution.py:85
  831.3 14.0 %collective-permute-done.96 = bf16[128,1024]{1,0:T(8,128)(2,1)S(1)} collective-permute-done((bf16[128,1024]{1,0:T(8,128)(2,1)S(1)}, bf16[128,1024]{1,0:T(8,128)(2,1)S(1)}, u32[]{:S(2)}, u32[]{:S(2)}) %collective-permute-start.96) | collective-permute-done | bytes 262176 | tf_op jit(solution)/shard_map/ppermute | solution.py:85
  869.8 57.1 %psum.7 = f32[5120]{0:T(1024)S(1)} all-reduce(f32[5120]{0:T(1024)S(1)} %pad_maximum_fusion.14), channel_id=1, replica_groups=mesh['dp'=4,'ctx'=2,'tensor'=4] {'dp','ctx','tensor'}, use_global_device_ids=true, to_apply=%region_15.16 | all-reduce | flops 5120 | bytes 40960 | tf_op jit(solution)/shard_map/psum | solution.py:429
  932.3 7.1 multiply_add_fusion
  (615 shorter events, 457.9 us)
Async XLA Ops:
  53.1 57.4 %collective-permute-start = (bf16[256,2048]{1,0:T(8,128)(2,1)}, bf16[256,2048]{1,0:T(8,128)(2,1)}, u32[]{:S(2)}, u32[]{:S(2)}) collective-permute-start(bf16[256,2048]{1,0:T(8,128)(2,1)} %constant_dynamic-slice_fusion.32), channel_id=1, source_target_pairs={{0,4},{1,5},{2,6},{3,7},{4,0},{5,1},{6,2},{7,3},{8,12},{9,13},{10,... | collective-permute-start | bytes 3145736 | tf_op jit(solution)/shard_map/ppermute | solution.py:85
  64.0 43.2 %collective-permute-start.22 = (bf16[256,1024]{1,0:T(8,128)(2,1)S(1)}, bf16[256,1024]{1,0:T(8,128)(2,1)S(1)}, u32[]{:S(2)}, u32[]{:S(2)}) collective-permute-start(bf16[256,1024]{1,0:T(8,128)(2,1)S(1)} %collective-permute-done.20), channel_id=1, source_target_pairs={{0,16},{1,17},{2,18},{3,19},{4,20},{5,21},{6,22},{7,23},{8,24},{9,... | collective-permute-start | bytes 1572872 | tf_op jit(solution)/shard_map/ppermute | solution.py:85
  108.5 51.6 %collective-permute-start.10 = (bf16[2048,768]{1,0:T(8,128)(2,1)}, bf16[2048,768]{1,0:T(8,128)(2,1)}, u32[]{:S(2)}, u32[]{:S(2)}) collective-permute-start(bf16[2048,768]{1,0:T(8,128)(2,1)} %constant_dynamic-update-slice_fusion), channel_id=1, source_target_pairs={{0,1},{1,0},{2,3},{3,2},{4,5},{5,4},{6,7},{7,6},{8,9},{9,8},{10,11... | collective-permute-start | bytes 9437192 | tf_op jit(solution)/shard_map/ppermute | solution.py:85
  129.4 58.9 %collective-permute-start.45 = (bf16[256,1408]{1,0:T(8,128)(2,1)}, bf16[256,1408]{1,0:T(8,128)(2,1)}, u32[]{:S(2)}, u32[]{:S(2)}) collective-permute-start(bf16[256,1408]{1,0:T(8,128)(2,1)} %param.28), channel_id=1, source_target_pairs={{0,0},{1,4},{2,2},{3,6},{4,1},{5,5},{6,3},{7,7},{8,8},{9,12},{10,1... | collective-permute-start | bytes 2162696 | tf_op jit(solution)/shard_map/ppermute | solution.py:85
  137.0 54.8 %collective-permute-start.54 = (bf16[256,1408]{1,0:T(8,128)(2,1)}, bf16[256,1408]{1,0:T(8,128)(2,1)}, u32[]{:S(2)}, u32[]{:S(2)}) collective-permute-start(bf16[256,1408]{1,0:T(8,128)(2,1)} %param.29), channel_id=1, source_target_pairs={{0,0},{1,4},{2,2},{3,6},{4,1},{5,5},{6,3},{7,7},{8,8},{9,12},{10,1... | collective-permute-start | bytes 2162696 | tf_op jit(solution)/shard_map/ppermute | solution.py:85
  147.5 44.3 %collective-permute-start.70 = (bf16[256,2048]{1,0:T(8,128)(2,1)S(1)}, bf16[256,2048]{1,0:T(8,128)(2,1)}, u32[]{:S(2)}, u32[]{:S(2)}) collective-permute-start(bf16[256,2048]{1,0:T(8,128)(2,1)S(1)} %constant_dynamic-slice_fusion.9), channel_id=1, source_target_pairs={{0,4},{1,5},{2,6},{3,7},{4,0},{5,1},{6,2},{7,3},{8,12},{9,13},{10,... | collective-permute-start | bytes 3145736 | tf_op jit(solution)/shard_map/ppermute | solution.py:85
  147.6 45.3 %collective-permute-start.41 = (bf16[256,1408]{1,0:T(8,128)(2,1)}, bf16[256,1408]{1,0:T(8,128)(2,1)S(1)}, u32[]{:S(2)}, u32[]{:S(2)}) collective-permute-start(bf16[256,1408]{1,0:T(8,128)(2,1)} %collective-permute-done.36.refs_0_), channel_id=1, source_target_pairs={{0,1},{1,0},{2,3},{3,2},{4,5},{5,4},{6,7},{7,6},{8,9},{9,8},{10,11... | collective-permute-start | bytes 2162696 | tf_op jit(solution)/shard_map/ppermute | solution.py:85
  160.0 45.6 %collective-permute-start.39 = (bf16[256,1408]{1,0:T(8,128)(2,1)}, bf16[256,1408]{1,0:T(8,128)(2,1)}, u32[]{:S(2)}, u32[]{:S(2)}) collective-permute-start(bf16[256,1408]{1,0:T(8,128)(2,1)} %collective-permute-done.36.refs_0_), channel_id=1, source_target_pairs={{8,16},{9,17},{10,18},{11,19},{12,20},{13,21},{14,22},{15,23},{16,... | collective-permute-start | bytes 2162696 | tf_op jit(solution)/shard_map/ppermute | solution.py:85
  205.7 80.7 %collective-permute-start.47 = (bf16[256,1408]{1,0:T(8,128)(2,1)}, bf16[256,1408]{1,0:T(8,128)(2,1)}, u32[]{:S(2)}, u32[]{:S(2)}) collective-permute-start(bf16[256,1408]{1,0:T(8,128)(2,1)} %collective-permute-done.45.refs_0_), channel_id=1, source_target_pairs={{0,16},{1,17},{2,18},{3,19},{4,20},{5,21},{6,22},{7,23},{8,24},{9,... | collective-permute-start | bytes 2162696 | tf_op jit(solution)/shard_map/ppermute | solution.py:85
  225.6 75.4 %collective-permute-start.56 = (bf16[256,1408]{1,0:T(8,128)(2,1)}, bf16[256,1408]{1,0:T(8,128)(2,1)}, u32[]{:S(2)}, u32[]{:S(2)}) collective-permute-start(bf16[256,1408]{1,0:T(8,128)(2,1)} %collective-permute-done.54.refs_0_), channel_id=1, source_target_pairs={{0,16},{1,17},{2,18},{3,19},{4,20},{5,21},{6,22},{7,23},{8,24},{9,... | collective-permute-start | bytes 2162696 | tf_op jit(solution)/shard_map/ppermute | solution.py:85
  225.6 76.1 %collective-permute-start.71 = (bf16[256,2048]{1,0:T(8,128)(2,1)}, bf16[256,2048]{1,0:T(8,128)(2,1)}, u32[]{:S(2)}, u32[]{:S(2)}) collective-permute-start(bf16[256,2048]{1,0:T(8,128)(2,1)} %collective-permute-done.70), channel_id=1, source_target_pairs={{0,1},{1,0},{2,3},{3,2},{4,5},{5,4},{6,7},{7,6},{8,9},{9,8},{10,11... | collective-permute-start | bytes 3145736 | tf_op jit(solution)/shard_map/ppermute | solution.py:85
  225.6 77.4 %collective-permute-start.40 = (bf16[256,1408]{1,0:T(8,128)(2,1)}, bf16[256,1408]{1,0:T(8,128)(2,1)}, u32[]{:S(2)}, u32[]{:S(2)}) collective-permute-start(bf16[256,1408]{1,0:T(8,128)(2,1)} %collective-permute-done.38.refs_2_), channel_id=1, source_target_pairs={{8,0},{9,1},{10,2},{11,3},{12,4},{13,5},{14,6},{15,7},{16,24},{17,... | collective-permute-start | bytes 2162696 | tf_op jit(solution)/shard_map/ppermute | solution.py:85
  231.4 131.8 %collective-permute-start.29 = (bf16[512,2048]{1,0:T(8,128)(2,1)}, bf16[512,2048]{1,0:T(8,128)(2,1)}, u32[]{:S(2)}, u32[]{:S(2)}) collective-permute-start(bf16[512,2048]{1,0:T(8,128)(2,1)} %convolution_convert_fusion.3), channel_id=1, source_target_pairs={{0,1},{1,0},{2,3},{3,2},{4,5},{5,4},{6,7},{7,6},{8,9},{9,8},{10,11... | collective-permute-start | bytes 6291464 | tf_op jit(solution)/shard_map/ppermute | solution.py:85
  303.0 44.2 %collective-permute-start.58 = (bf16[256,1408]{1,0:T(8,128)(2,1)}, bf16[256,1408]{1,0:T(8,128)(2,1)S(1)}, u32[]{:S(2)}, u32[]{:S(2)}) collective-permute-start(bf16[256,1408]{1,0:T(8,128)(2,1)} %collective-permute-done.56.refs_2_), channel_id=1, source_target_pairs={{8,0},{9,1},{10,2},{11,3},{12,4},{13,5},{14,6},{15,7},{16,24},{17,... | collective-permute-start | bytes 2162696 | tf_op jit(solution)/shard_map/ppermute | solution.py:85
  316.3 46.4 %collective-permute-start.55 = (bf16[256,1408]{1,0:T(8,128)(2,1)}, bf16[256,1408]{1,0:T(8,128)(2,1)}, u32[]{:S(2)}, u32[]{:S(2)}) collective-permute-start(bf16[256,1408]{1,0:T(8,128)(2,1)} %collective-permute-done.54.refs_0_), channel_id=1, source_target_pairs={{0,8},{1,9},{2,10},{3,11},{4,12},{5,13},{6,14},{7,15},{8,0},{9,1},... | collective-permute-start | bytes 2162696 | tf_op jit(solution)/shard_map/ppermute | solution.py:85
  498.9 63.7 %collective-permute-start.106 = (bf16[512,1408]{1,0:T(8,128)(2,1)}, bf16[512,1408]{1,0:T(8,128)(2,1)}, u32[]{:S(2)}, u32[]{:S(2)}) collective-permute-start(bf16[512,1408]{1,0:T(8,128)(2,1)} %get-tuple-element.63), channel_id=1, source_target_pairs={{0,1},{1,0},{2,3},{3,2},{4,5},{5,4},{6,7},{7,6},{8,9},{9,8},{10,11... | collective-permute-start | bytes 4325384 | tf_op jit(solution)/shard_map/ppermute | solution.py:85
  504.2 58.4 %collective-permute-start.105 = (bf16[512,1024]{1,0:T(8,128)(2,1)}, bf16[512,1024]{1,0:T(8,128)(2,1)}, u32[]{:S(2)}, u32[]{:S(2)}) collective-permute-start(bf16[512,1024]{1,0:T(8,128)(2,1)} %shard_map.260), channel_id=1, source_target_pairs={{0,1},{1,0},{2,3},{3,2},{4,5},{5,4},{6,7},{7,6},{8,9},{9,8},{10,11... | collective-permute-start | bytes 3145736 | tf_op jit(solution)/shard_map/ppermute | solution.py:85
  560.8 63.7 %collective-permute-start.78 = (bf16[512,2048]{1,0:T(8,128)(2,1)S(1)}, bf16[512,2048]{1,0:T(8,128)(2,1)S(1)}, u32[]{:S(2)}, u32[]{:S(2)}) collective-permute-start(bf16[512,2048]{1,0:T(8,128)(2,1)S(1)} %shard_map.254), channel_id=1, source_target_pairs={{0,1},{1,0},{2,3},{3,2},{4,5},{5,4},{6,7},{7,6},{8,9},{9,8},{10,11... | collective-permute-start | bytes 6291464 | tf_op jit(solution)/shard_map/ppermute | solution.py:85
  569.5 92.8 %collective-permute-start.110 = (bf16[256,1408]{1,0:T(8,128)(2,1)}, bf16[256,1408]{1,0:T(8,128)(2,1)}, u32[]{:S(2)}, u32[]{:S(2)}) collective-permute-start(bf16[256,1408]{1,0:T(8,128)(2,1)} %get-tuple-element.75), channel_id=1, source_target_pairs={{8,16},{9,17},{10,18},{11,19},{12,20},{13,21},{14,22},{15,23},{16,... | collective-permute-start | bytes 2162696 | tf_op jit(solution)/shard_map/ppermute | solution.py:85
  579.8 90.9 %collective-permute-start.116 = (bf16[256,1408]{1,0:T(8,128)(2,1)}, bf16[256,1408]{1,0:T(8,128)(2,1)}, u32[]{:S(2)}, u32[]{:S(2)}) collective-permute-start(bf16[256,1408]{1,0:T(8,128)(2,1)} %get-tuple-element.73), channel_id=1, source_target_pairs={{8,16},{9,17},{10,18},{11,19},{12,20},{13,21},{14,22},{15,23},{16,... | collective-permute-start | bytes 2162696 | tf_op jit(solution)/shard_map/ppermute | solution.py:85
  605.6 52.9 %collective-permute-start.107 = (bf16[256,1408]{1,0:T(8,128)(2,1)}, bf16[256,1408]{1,0:T(8,128)(2,1)}, u32[]{:S(2)}, u32[]{:S(2)}) collective-permute-start(bf16[256,1408]{1,0:T(8,128)(2,1)} %get-tuple-element.74), channel_id=1, source_target_pairs={{0,8},{1,9},{2,10},{3,11},{4,12},{5,13},{6,14},{7,15},{8,0},{9,1},... | collective-permute-start | bytes 2162696 | tf_op jit(solution)/shard_map/ppermute | solution.py:85
  620.9 49.3 %collective-permute-start.113 = (bf16[256,1408]{1,0:T(8,128)(2,1)}, bf16[256,1408]{1,0:T(8,128)(2,1)}, u32[]{:S(2)}, u32[]{:S(2)}) collective-permute-start(bf16[256,1408]{1,0:T(8,128)(2,1)} %get-tuple-element.72), channel_id=1, source_target_pairs={{0,8},{1,9},{2,10},{3,11},{4,12},{5,13},{6,14},{7,15},{8,0},{9,1},... | collective-permute-start | bytes 2162696 | tf_op jit(solution)/shard_map/ppermute | solution.py:85
  662.3 45.3 %collective-permute-start.99 = (bf16[1024,512]{1,0:T(8,128)(2,1)}, bf16[1024,512]{1,0:T(8,128)(2,1)}, u32[]{:S(2)}, u32[]{:S(2)}) collective-permute-start(bf16[1024,512]{1,0:T(8,128)(2,1)} %pad_maximum_fusion.4), channel_id=1, source_target_pairs={{0,1},{1,0},{2,3},{3,2},{4,5},{5,4},{6,7},{7,6},{8,9},{9,8},{10,11... | collective-permute-start | bytes 3145736 | tf_op jit(solution)/shard_map/ppermute | solution.py:85
  667.4 46.6 %collective-permute-start.79 = (bf16[512,1536]{1,0:T(8,128)(2,1)}, bf16[512,1536]{1,0:T(8,128)(2,1)}, u32[]{:S(2)}, u32[]{:S(2)}) collective-permute-start(bf16[512,1536]{1,0:T(8,128)(2,1)} %constant_dynamic-slice_fusion.4), channel_id=1, source_target_pairs={{0,1},{1,0},{2,3},{3,2},{4,5},{5,4},{6,7},{7,6},{8,9},{9,8},{10,11... | collective-permute-start | bytes 4718600 | tf_op jit(solution)/shard_map/ppermute | solution.py:85
  670.2 176.1 %collective-permute-start.69 = (bf16[512,2048]{1,0:T(8,128)(2,1)S(1)}, bf16[512,2048]{1,0:T(8,128)(2,1)}, u32[]{:S(2)}, u32[]{:S(2)}) collective-permute-start(bf16[512,2048]{1,0:T(8,128)(2,1)S(1)} %shard_map.253), channel_id=1, source_target_pairs={{0,1},{1,0},{2,3},{3,2},{4,5},{5,4},{6,7},{7,6},{8,9},{9,8},{10,11... | collective-permute-start | bytes 6291464 | tf_op jit(solution)/shard_map/ppermute | solution.py:85
  754.9 53.0 %collective-permute-start.121 = (bf16[256,1408]{1,0:T(8,128)(2,1)S(1)}, bf16[256,1408]{1,0:T(8,128)(2,1)S(1)}, u32[]{:S(2)}, u32[]{:S(2)}) collective-permute-start(bf16[256,1408]{1,0:T(8,128)(2,1)S(1)} %copy-done.62), channel_id=1, source_target_pairs={{0,16},{1,17},{2,18},{3,19},{4,20},{5,21},{6,22},{7,23},{8,24},{9,... | collective-permute-start | bytes 2162696 | tf_op jit(solution)/shard_map/ppermute | solution.py:85
  759.1 52.8 %collective-permute-start.103 = (bf16[256,1024]{1,0:T(8,128)(2,1)S(1)}, bf16[256,1024]{1,0:T(8,128)(2,1)S(1)}, u32[]{:S(2)}, u32[]{:S(2)}) collective-permute-start(bf16[256,1024]{1,0:T(8,128)(2,1)S(1)} %get-tuple-element.81), channel_id=1, source_target_pairs={{8,16},{9,17},{10,18},{11,19},{12,20},{13,21},{14,22},{15,23},{16,... | collective-permute-start | bytes 1572872 | tf_op jit(solution)/shard_map/ppermute | solution.py:85
  760.0 47.8 %collective-permute-start.100 = (bf16[256,1024]{1,0:T(8,128)(2,1)S(1)}, bf16[256,1024]{1,0:T(8,128)(2,1)S(1)}, u32[]{:S(2)}, u32[]{:S(2)}) collective-permute-start(bf16[256,1024]{1,0:T(8,128)(2,1)S(1)} %get-tuple-element.80), channel_id=1, source_target_pairs={{0,8},{1,9},{2,10},{3,11},{4,12},{5,13},{6,14},{7,15},{8,0},{9,1},... | collective-permute-start | bytes 1572872 | tf_op jit(solution)/shard_map/ppermute | solution.py:85
  763.9 64.2 %collective-permute-start.102 = (bf16[256,1024]{1,0:T(8,128)(2,1)S(1)}, bf16[256,1024]{1,0:T(8,128)(2,1)S(1)}, u32[]{:S(2)}, u32[]{:S(2)}) collective-permute-start(bf16[256,1024]{1,0:T(8,128)(2,1)S(1)} %add_convert_fusion.7), channel_id=1, source_target_pairs={{0,16},{1,17},{2,18},{3,19},{4,20},{5,21},{6,22},{7,23},{8,24},{9,... | collective-permute-start | bytes 1572872 | tf_op jit(solution)/shard_map/ppermute | solution.py:85
  857.4 70.8 %collective-permute-start.90 = (bf16[256,384]{0,1:T(8,128)(2,1)S(1)}, bf16[256,384]{0,1:T(8,128)(2,1)S(1)}, u32[]{:S(2)}, u32[]{:S(2)}) collective-permute-start(bf16[256,384]{0,1:T(8,128)(2,1)S(1)} %get-tuple-element.105), channel_id=1, source_target_pairs={{8,16},{9,17},{10,18},{11,19},{12,20},{13,21},{14,22},{15,23},{16,... | collective-permute-start | bytes 589832 | tf_op jit(solution)/shard_map/ppermute | solution.py:85
  866.6 61.5 %collective-permute-start.87 = (bf16[256,384]{0,1:T(8,128)(2,1)S(1)}, bf16[256,384]{0,1:T(8,128)(2,1)S(1)}, u32[]{:S(2)}, u32[]{:S(2)}) collective-permute-start(bf16[256,384]{0,1:T(8,128)(2,1)S(1)} %get-tuple-element.104), channel_id=1, source_target_pairs={{0,8},{1,9},{2,10},{3,11},{4,12},{5,13},{6,14},{7,15},{8,0},{9,1},... | collective-permute-start | bytes 589832 | tf_op jit(solution)/shard_map/ppermute | solution.py:85
  866.7 61.5 %collective-permute-start.89 = (bf16[256,384]{0,1:T(8,128)(2,1)S(1)}, bf16[256,384]{0,1:T(8,128)(2,1)S(1)}, u32[]{:S(2)}, u32[]{:S(2)}) collective-permute-start(bf16[256,384]{0,1:T(8,128)(2,1)S(1)} %add_convert_fusion.13), channel_id=1, source_target_pairs={{0,16},{1,17},{2,18},{3,19},{4,20},{5,21},{6,22},{7,23},{8,24},{9,... | collective-permute-start | bytes 589832 | tf_op jit(solution)/shard_map/ppermute | solution.py:85
  (204 other events, 3494.0 us)

commit v2 on v0

--- a/solution.py
+++ b/solution.py
@@ -1,6 +1,8 @@
 import jax
 import jax.numpy as jnp
 from jax import lax
+from jax.experimental import pallas as pl
+from jax.experimental.pallas import tpu as pltpu
 from jax.sharding import PartitionSpec as P
 
 HD = 256
@@ -8,17 +10,21 @@
 
 EPSILON = 1e-06
 
+AXES = ("dp", "ctx", "tensor")
+BF = jnp.bfloat16
+F32 = jnp.float32
+
+
+def dot(left, right):
+    return jnp.dot(left, right, preferred_element_type=F32)
+
 
 def times_trans(left, right):
-    return lax.dot_general(
-        left, right, (((1,), (1,)), ((), ())), preferred_element_type=jnp.float32
-    )
+    return lax.dot_general(left, right, (((1,), (1,)), ((), ())), preferred_element_type=F32)
 
 
 def trans_times(left, right):
-    return lax.dot_general(
-        left, right, (((0,), (0,)), ((), ())), preferred_element_type=jnp.float32
-    )
+    return lax.dot_general(left, right, (((0,), (0,)), ((), ())), preferred_element_type=F32)
 
 
 def rms_parts(array):
@@ -30,6 +36,1006 @@
     grad_plain = grad_out * gain
     grad_in = inverse * (grad_plain - plain * jnp.mean(grad_plain * plain, axis=-1, keepdims=True))
     return (grad_in, jnp.sum(grad_out * plain, axis=0))
+
+
+def angles_of(places, half):
+    freqs = 10000.0 ** (-jnp.arange(half, dtype=F32) / half)
+    angles = places[:, None] * freqs[None, :]
+    return (jnp.cos(angles), jnp.sin(angles))
+
+
+def turn(array, cosine, sine):
+    half = array.shape[-1] // 2
+    first = array[..., :half]
+    latter = array[..., half:]
+    return jnp.concatenate(
+        [first * cosine - latter * sine, latter * cosine + first * sine], axis=-1
+    )
+
+
+def routes(move):
+    pairs = []
+    for z in range(4):
+        for x in range(2):
+            for y in range(2):
+                for c in range(2):
+                    to = move(z, x, y, c)
+                    if to is not None:
+                        tz, tx, ty, tc = to
+                        pairs.append(
+                            (((z * 2 + x) * 2 + y) * 2 + c, ((tz * 2 + tx) * 2 + ty) * 2 + tc)
+                        )
+    return pairs
+
+
+OVER_X = routes(lambda z, x, y, c: (z, 1 - x, y, c))
+OVER_Y = routes(lambda z, x, y, c: (z, x, 1 - y, c))
+OVER_XY = routes(lambda z, x, y, c: (z, 1 - x, 1 - y, c))
+OVER_YC = routes(lambda z, x, y, c: (z, x, 1 - y, 1 - c))
+OVER_C = routes(lambda z, x, y, c: (z, x, y, 1 - c))
+TRANSPOSE = routes(lambda z, x, y, c: (z, c, y, x) if x != c else None)
+Z_ONE = routes(lambda z, x, y, c: (z ^ 1, x, y, c))
+Z_TWO = routes(lambda z, x, y, c: (z ^ 2, x, y, c))
+Z_THREE = routes(lambda z, x, y, c: (z ^ 3, x, y, c))
+
+
+def send(array, pairs):
+    return lax.ppermute(array, AXES, pairs)
+
+
+def transpose(array, stays):
+    return jnp.where(stays, array, send(array, TRANSPOSE))
+
+
+def after(array, *others):
+    return lax.optimization_barrier((array, *others))[0]
+
+
+def stage(*arrays):
+    return lax.optimization_barrier(arrays)
+
+
+def gather_z(array):
+    return lax.all_gather(array, "dp", axis=0, tiled=True)
+
+
+def reduce_z(slabs):
+    return lax.psum_scatter(slabs, "dp", scatter_dimension=0, tiled=True)
+
+
+def trade_z(slabs):
+    n = slabs.shape[0] // 4
+    return [slabs[:n]] + [
+        send(slabs[k * n : (k + 1) * n], pairs)
+        for k, pairs in ((1, Z_ONE), (2, Z_TWO), (3, Z_THREE))
+    ]
+
+
+WHOLE = pl.BlockSpec(memory_space=pltpu.VMEM)
+HELD = pl.BlockSpec(memory_space=pl.ANY)
+ROOMY = pltpu.CompilerParams(vmem_limit_bytes=56 * 1024 * 1024)
+
+
+def cost(macs, moved, share=1):
+    return pl.CostEstimate(
+        flops=2 * macs // share // 1, bytes_accessed=moved // share // 1, transcendentals=0
+    )
+
+
+def place_copies(plan, numbers, buffers, shape, dtype):
+    def body(numbers_ref, *refs):
+        ins, out_ref, sem = refs[:-2], refs[-2], refs[-1]
+        listed = plan(numbers_ref, ins, out_ref)
+        for i, (condition, source, target) in enumerate(listed):
+            copy = pltpu.make_async_copy(source, target, sem.at[i])
+            if condition is None:
+                copy.start()
+            else:
+                pl.when(condition)(copy.start)
+        for i, (condition, source, target) in enumerate(listed):
+            copy = pltpu.make_async_copy(source, target, sem.at[i])
+            if condition is None:
+                copy.wait()
+            else:
+                pl.when(condition)(copy.wait)
+
+    moved = 2
+    for extent in shape:
+        moved *= extent
+    return pl.pallas_call(
+        body,
+        grid_spec=pltpu.PrefetchScalarGridSpec(
+            num_scalar_prefetch=1,
+            grid=(1,),
+            in_specs=[HELD] * len(buffers),
+            out_specs=pl.BlockSpec(shape, lambda i, numbers_ref: (0, 0)),
+            scratch_shapes=[pltpu.SemaphoreType.DMA((40,))],
+        ),
+        out_shape=jax.ShapeDtypeStruct(shape, dtype),
+        compiler_params=ROOMY,
+        cost_estimate=cost(0, 2 * moved),
+    )(numbers, *buffers)
+
+
+def attention_forward(query_pre, cosine, sine, keys, values, row_info, key_places):
+    rows, width = query_pre.shape
+    heads = width // HD
+    chunk = 256
+    half = HD // 2
+    scale = HD ** (-0.5)
+
+    def body(pre_ref, cos_ref, sin_ref, k_ref, v_ref, info_ref, place_ref, q_ref, o_ref, lse_ref):
+        for i in range(rows // chunk):
+            at = slice(i * chunk, (i + 1) * chunk)
+            first, latter = pre_ref[at, :half], pre_ref[at, half:]
+            co, si = cos_ref[at], sin_ref[at]
+            q = jnp.concatenate([first * co - latter * si, latter * co + first * si], 1).astype(BF)
+            q_ref[at] = q
+            scores = times_trans(q, k_ref[...]) * scale
+            allowed = (place_ref[...] <= info_ref[at, 0:1]) & (place_ref[...] >= info_ref[at, 1:2])
+            scores = jnp.where(allowed, scores, -1e30)
+            largest = jnp.max(scores, axis=-1, keepdims=True)
+            exponent = jnp.exp(scores - largest)
+            totals = jnp.sum(exponent, axis=-1, keepdims=True)
+            soft = (exponent * (1.0 / totals)).astype(BF)
+            o_ref[at] = dot(soft, v_ref[...]).astype(BF)
+            lse_ref[0, at] = largest + jnp.log(totals)
+
+    full = lambda h: (0, 0)
+    by_head = lambda h: (0, h)
+    return pl.pallas_call(
+        body,
+        grid=(heads,),
+        in_specs=[
+            pl.BlockSpec((rows, HD), by_head),
+            pl.BlockSpec((rows, half), full),
+            pl.BlockSpec((rows, half), full),
+            pl.BlockSpec((rows, HD), full),
+            pl.BlockSpec((rows, HD), full),
+            pl.BlockSpec((rows, 2), full),
+            pl.BlockSpec((1, rows), full),
+        ],
+        out_specs=[
+            pl.BlockSpec((rows, HD), by_head),
+            pl.BlockSpec((rows, HD), by_head),
+            pl.BlockSpec((1, rows, 1), lambda h: (h, 0, 0)),
+        ],
+        out_shape=[
+            jax.ShapeDtypeStruct((rows, width), BF),
+            jax.ShapeDtypeStruct((rows, width), BF),
+            jax.ShapeDtypeStruct((heads, rows, 1), F32),
+        ],
+        compiler_params=ROOMY,
+        cost_estimate=cost(4 * rows * rows * width, 6 * rows * width),
+    )(query_pre, cosine, sine, keys, values, row_info, key_places)
+
+
+def attention_backward(query, grad_out, lse, cosine, sine, keys, values, row_info, key_places):
+    rows, width = query.shape
+    heads = width // HD
+    chunk = 256
+    half = HD // 2
+    scale = HD ** (-0.5)
+
+    def body(
+        q_ref, do_ref, lse_ref, cos_ref, sin_ref, k_ref, v_ref, info_ref, place_ref, dq_ref, dk_ref, dv_ref
+    ):
+        @pl.when(pl.program_id(0) == 0)
+        def clear():
+            dk_ref[...] = jnp.zeros_like(dk_ref)
+            dv_ref[...] = jnp.zeros_like(dv_ref)
+
+        for i in range(rows // chunk):
+            at = slice(i * chunk, (i + 1) * chunk)
+            q, do = q_ref[at], do_ref[at]
+            scores = times_trans(q, k_ref[...]) * scale
+            allowed = (place_ref[...] <= info_ref[at, 0:1]) & (place_ref[...] >= info_ref[at, 1:2])
+            soft = jnp.exp(jnp.where(allowed, scores, -1e30) - lse_ref[0, at])
+            grad_soft = times_trans(do, v_ref[...])
+            summed = jnp.sum(soft * grad_soft, axis=-1, keepdims=True)
+            grad_scores = (soft * (grad_soft - summed)).astype(BF)
+            dq = dot(grad_scores, k_ref[...]) * scale
+            first, latter = dq[:, :half], dq[:, half:]
+            co, si = cos_ref[at], sin_ref[at]
+            dq_ref[at] = jnp.concatenate(
+                [first * co + latter * si, latter * co - first * si], 1
+            ).astype(BF)
+            dk_ref[...] += trans_times(grad_scores, q) * scale
+            dv_ref[...] += trans_times(soft.astype(BF), do)
+
+    full = lambda h: (0, 0)
+    by_head = lambda h: (0, h)
+    return pl.pallas_call(
+        body,
+        grid=(heads,),
+        in_specs=[
+            pl.BlockSpec((rows, HD), by_head),
+            pl.BlockSpec((rows, HD), by_head),
+            pl.BlockSpec((1, rows, 1), lambda h: (h, 0, 0)),
+            pl.BlockSpec((rows, half), full),
+            pl.BlockSpec((rows, half), full),
+            pl.BlockSpec((rows, HD), full),
+            pl.BlockSpec((rows, HD), full),
+            pl.BlockSpec((rows, 2), full),
+            pl.BlockSpec((1, rows), full),
+        ],
+        out_specs=[
+            pl.BlockSpec((rows, HD), by_head),
+            pl.BlockSpec((rows, HD), full),
+            pl.BlockSpec((rows, HD), full),
+        ],
+        out_shape=[
+            jax.ShapeDtypeStruct((rows, width), BF),
+            jax.ShapeDtypeStruct((rows, HD), F32),
+            jax.ShapeDtypeStruct((rows, HD), F32),
+        ],
+        compiler_params=ROOMY,
+        cost_estimate=cost(8 * rows * rows * width, 6 * rows * width),
+    )(query, grad_out, lse, cosine, sine, keys, values, row_info, key_places)
+
+
+def product_of_parts(parts, weight):
+    rows = parts[0].shape[0]
+    count = len(parts)
+    width = weight.shape[1]
+
+    def body(*refs):
+        weight_ref, out_ref = refs[count:]
+        for i in range(0, count, 4):
+            left = jnp.concatenate([refs[j][...] for j in range(i, i + 4)], axis=0)
+            out_ref[i * rows : (i + 4) * rows] = dot(left, weight_ref[...]).astype(BF)
+
+    return pl.pallas_call(
+        body,
+        in_specs=[WHOLE] * (count + 1),
+        out_specs=WHOLE,
+        out_shape=jax.ShapeDtypeStruct((count * rows, width), BF),
+        compiler_params=ROOMY,
+        cost_estimate=cost(count * rows * weight.size, 2 * weight.size),
+    )(*parts, weight)
+
+
+def product_pieces(left, weight, extras, got, first_half):
+    rows = left.shape[0] // 2
+    part = rows // 4
+    start = 0 if first_half else rows
+    wide = weight.shape[0]
+    total = wide + sum(e.shape[1] for e in extras)
+    outs = 4 if first_half else 1
+
+    def body(left_ref, weight_ref, *refs):
+        extra_refs = refs[: len(extras)]
+        got_ref = refs[len(extras)] if got is not None else None
+        out_refs = refs[len(refs) - outs :]
+        src = slice(start, start + rows)
+
+        def put(value, cols):
+            if got_ref is not None:
+                value = value + got_ref[:, cols].astype(F32)
+            value = value.astype(BF)
+            if outs == 1:
+                out_refs[0][:, cols] = value
+            else:
+                for f in range(4):
+                    out_refs[f][:, cols] = value[f * part : (f + 1) * part]
+
+        step = 512
+        for col in range(0, wide, step):
+            put(times_trans(left_ref[src], weight_ref[col : col + step]), slice(col, col + step))
+        col = wide
+        for extra_ref in extra_refs:
+            n = extra_ref.shape[1]
+            put(extra_ref[src], slice(col, col + n))
+            col += n
+
+    shapes = [jax.ShapeDtypeStruct((part, total), BF)] * 4
+    if outs == 1:
+        shapes = [jax.ShapeDtypeStruct((rows, total), BF)]
+    arrays = [left, weight, *extras] + ([got] if got is not None else [])
+    return pl.pallas_call(
+        body,
+        in_specs=[WHOLE] * len(arrays),
+        out_specs=[WHOLE] * outs,
+        out_shape=shapes,
+        compiler_params=ROOMY,
+        cost_estimate=cost(rows * wide * left.shape[1], 2 * weight.size + 4 * rows * total),
+    )(*arrays)
+
+
+def tiles_of(width):
+    whole = width // 256
+    return whole, width - whole * 256
+
+
+def ffn_forward(numbers, parts, pairs):
+    part, depth = parts[0].shape
+    rows = part * len(parts)
+    width = pairs[0].shape[1]
+    whole, rest = tiles_of(width)
+
+    def body(numbers_ref, *refs):
+        part_refs, pair_refs = refs[:4], refs[4:6]
+        hid_ref, slope_ref, silu_ref, gate_vm, up_vm, in_vm, sem = refs[6:]
+        gate_copies, up_copies = [], []
+        for i in range(8):
+            to = pl.ds(pl.multiple_of(numbers_ref[i] * 256, 256), 256)
+            ref, at = pair_refs[i // 4], (i % 4) * 512
+            gate_copies.append(
+                pltpu.make_async_copy(ref.at[at : at + 256], gate_vm.at[to], sem.at[i])
+            )
+            up_copies.append(
+                pltpu.make_async_copy(ref.at[at + 256 : at + 512], up_vm.at[to], sem.at[8 + i])
+            )
+        for copy in gate_copies + up_copies:
+            copy.start()
+        for f in range(4):
+            in_vm[f * part : (f + 1) * part] = part_refs[f][...]
+        for copy in gate_copies + up_copies:
+            copy.wait()
+
+        def tile(cols):
+            gate = dot(in_vm[...], gate_vm[:, cols])
+            up = dot(in_vm[...], up_vm[:, cols])
+            sigma = jax.nn.sigmoid(gate)
+            silu = gate * sigma
+            hid_ref[:, cols] = (silu * up).astype(BF)
+            slope_ref[:, cols] = up * sigma * (1.0 + gate * (1.0 - sigma))
+            silu_ref[:, cols] = silu
+
+        @pl.loop(0, whole)
+        def each(i):
+            tile(pl.ds(pl.multiple_of(i * 256, 256), 256))
+
+        if rest:
+            tile(slice(whole * 256, width))
+
+    return pl.pallas_call(
+        body,
+        grid_spec=pltpu.PrefetchScalarGridSpec(
+            num_scalar_prefetch=1,
+            grid=(1,),
+            in_specs=[pl.BlockSpec((part, depth), lambda i, n: (0, 0))] * 4 + [HELD] * 2,
+            out_specs=[pl.BlockSpec((rows, width), lambda i, n: (0, 0))] * 3,
+            scratch_shapes=[
+                pltpu.VMEM((depth, width), BF),
+                pltpu.VMEM((depth, width), BF),
+                pltpu.VMEM((rows, depth), BF),
+                pltpu.SemaphoreType.DMA((16,)),
+            ],
+        ),
+        out_shape=[
+            jax.ShapeDtypeStruct((rows, width), BF),
+            jax.ShapeDtypeStruct((rows, width), F32),
+            jax.ShapeDtypeStruct((rows, width), F32),
+        ],
+        compiler_params=ROOMY,
+        cost_estimate=cost(2 * rows * depth * width, 4 * depth * width),
+    )(numbers, *parts, *pairs)
+
+
+def ffn_backward(numbers, cot, slope, silu, pairs, downs):
+    rows = slope.shape[0]
+    depth = cot.shape[1]
+    part = rows // 4
+    width = slope.shape[1]
+    whole, rest = tiles_of(width)
+
+    def body(numbers_ref, *refs):
+        cot_ref, slope_ref, silu_ref = refs[:3]
+        pair_refs, down_refs = refs[3:5], refs[5:7]
+        gate_out, up_out = refs[7:9]
+        piece_refs = refs[9:13]
+        down_vm, pair_vm, sem = refs[13:]
+        copies, later = [], []
+        for i in range(8):
+            to = pl.ds(pl.multiple_of(numbers_ref[i] * 256, 256), 256)
+            ref, at = down_refs[i // 4], (i % 4) * 256
+            copies.append(
+                pltpu.make_async_copy(ref.at[at : at + 256], down_vm.at[to], sem.at[i])
+            )
+            ref, at = pair_refs[i // 4], (i % 4) * 512
+            later.append(
+                pltpu.make_async_copy(ref.at[at : at + 512], pair_vm.at[i], sem.at[8 + i])
+            )
+        for copy in copies + later:
+            copy.start()
+        for copy in copies:
+            copy.wait()
+
+        def tile(cols):
+            grad = dot(cot_ref[...], down_vm[:, cols])
+            gate_out[:, cols] = (grad * slope_ref[:, cols]).astype(BF)
+            up_out[:, cols] = (grad * silu_ref[:, cols]).astype(BF)
+
+        @pl.loop(0, whole)
+        def each(i):
+            tile(pl.ds(pl.multiple_of(i * 256, 256), 256))
+
+        if rest:
+            tile(slice(whole * 256, width))
+        for copy in later:
+            copy.wait()
+
+        @pl.loop(0, 8)
+        def block(i):
+            cols = pl.ds(pl.multiple_of(numbers_ref[i] * 256, 256), 256)
+            value = times_trans(gate_out[...], pair_vm[i, :256]) + times_trans(
+                up_out[...], pair_vm[i, 256:]
+            )
+            value = value.astype(BF)
+            for f in range(4):
+                piece_refs[f][:, cols] = value[f * part : (f + 1) * part]
+
+    flat = lambda i, n: (0, 0)
+    return pl.pallas_call(
+        body,
+        grid_spec=pltpu.PrefetchScalarGridSpec(
+            num_scalar_prefetch=1,
+            grid=(1,),
+            in_specs=[
+                pl.BlockSpec((rows, depth), flat),
+                pl.BlockSpec((rows, width), flat),
+                pl.BlockSpec((rows, width), flat),
+            ]
+            + [HELD] * 4,
+            out_specs=[pl.BlockSpec((rows, width), flat)] * 2
+            + [pl.BlockSpec((part, depth), flat)] * 4,
+            scratch_shapes=[
+                pltpu.VMEM((depth, width), BF),
+                pltpu.VMEM((8, 512, width), BF),
+                pltpu.SemaphoreType.DMA((16,)),
+            ],
+        ),
+        out_shape=[jax.ShapeDtypeStruct((rows, width), BF)] * 2
+        + [jax.ShapeDtypeStruct((part, depth), BF)] * 4,
+        compiler_params=ROOMY,
+        cost_estimate=cost(3 * rows * depth * width, 6 * depth * width),
+    )(numbers, cot, slope, silu, *pairs, *downs)
+
+
+def ffn_output(numbers, hidden, downs):
+    rows, width = hidden.shape
+    part = rows // 4
+    depth = 2 * downs[0].shape[0]
+
+    def body(numbers_ref, hid_ref, *refs):
+        down_refs, piece_refs = refs[:2], refs[2:6]
+        down_vm, sem = refs[6:]
+        copies = [
+            pltpu.make_async_copy(
+                down_refs[i // 4].at[(i % 4) * 256 : (i % 4 + 1) * 256], down_vm.at[i], sem.at[i]
+            )
+            for i in range(8)
+        ]
+        for copy in copies:
+            copy.start()
+        for copy in copies:
+            copy.wait()
+
+        @pl.loop(0, 8)
+        def block(i):
+            cols = pl.ds(pl.multiple_of(numbers_ref[i] * 256, 256), 256)
+            value = times_trans(hid_ref[...], down_vm[i]).astype(BF)
+            for f in range(4):
+                piece_refs[f][:, cols] = value[f * part : (f + 1) * part]
+
+    flat = lambda i, n: (0, 0)
+    return pl.pallas_call(
+        body,
+        grid_spec=pltpu.PrefetchScalarGridSpec(
+            num_scalar_prefetch=1,
+            grid=(1,),
+            in_specs=[pl.BlockSpec((rows, width), flat)] + [HELD] * 2,
+            out_specs=[pl.BlockSpec((part, depth), flat)] * 4,
+            scratch_shapes=[
+                pltpu.VMEM((8, 256, width), BF),
+                pltpu.SemaphoreType.DMA((8,)),
+            ],
+        ),
+        out_shape=[jax.ShapeDtypeStruct((part, depth), BF)] * 4,
+        compiler_params=ROOMY,
+        cost_estimate=cost(rows * depth * width, 2 * depth * width, 4),
+    )(numbers, hidden, *downs)
+
+
+def weight_grads(numbers, terms, width):
+    lefts, rights, left_specs, right_specs = [], [], [], []
+    shape_of = []
+    for left, block, offset, products in terms:
+        for array in left:
+            lefts.append(array)
+            left_specs.append(
+                pl.BlockSpec((array.shape[0], block), lambda i, n, offset=offset: (0, n[offset + i]))
+            )
+        for place, right in products:
+            for array, start, count, pick in right:
+                rights.append(array)
+                if pick is None:
+                    right_specs.append(pl.BlockSpec(array.shape, lambda i, n: (0, 0)))
+                else:
+                    right_specs.append(
+                        pl.BlockSpec((array.shape[0], width), lambda i, n, pick=pick: (0, n[pick]))
+                    )
+        shape_of.append(block)
+    height = sum(shape_of)
+
+    def body(numbers_ref, *refs):
+        left_refs = refs[: len(lefts)]
+        right_refs = refs[len(lefts) : len(lefts) + len(rights)]
+        out_ref = refs[-1]
+        li, ri, row = 0, 0, 0
+        for left, block, offset, products in terms:
+            pieces = [left_refs[li + j][...] for j in range(len(left))]
+            li += len(left)
+            whole = pieces[0] if len(pieces) == 1 else jnp.concatenate(pieces, axis=0)
+            for place, right in products:
+                value = None
+                at = 0
+                for array, start, count, pick in right:
+                    this = trans_times(
+                        whole[at : at + count], right_refs[ri][start : start + count]
+                    )
+                    value = this if value is None else value + this
+                    at += count
+                    ri += 1
+                value = value.astype(BF)
+                n = value.shape[1]
+                if place is None:
+                    cols = slice(0, n)
+                else:
+                    cols = pl.ds(pl.multiple_of(numbers_ref[place] * n, n), n)
+                out_ref[row : row + block, cols] = value
+
+            row += block
+
+    macs = 4 * height * width * 1024
+    return pl.pallas_call(
+        body,
+        grid_spec=pltpu.PrefetchScalarGridSpec(
+            num_scalar_prefetch=1,
+            grid=(4,),
+            in_specs=left_specs + right_specs,
+            out_specs=pl.BlockSpec((height, width), lambda i, n: (i, 0)),
+        ),
+        out_shape=jax.ShapeDtypeStruct((4 * height, width), BF),
+        compiler_params=ROOMY,
+        cost_estimate=cost(macs, 4 * height * width * 4, 4),
+    )(numbers, *lefts, *rights)
+
+
+def input_gradient(numbers, grad_lat, first_all, grad_mid, tokens, gain):
+    depth = tokens.shape[1]
+    wide = grad_lat.shape[1]
+    part = 128
+
+    def body(numbers_ref, lat_ref, first_ref, mid_ref, tok_ref, gain_ref, out_ref, grad_vm):
+        for col in range(0, depth, 512):
+            cols = slice(col, col + 512)
+            grad_vm[:, cols] = times_trans(lat_ref[...], first_ref[cols]) * gain_ref[:, cols]
+        for i in range(4):
+            at = slice(i * part, (i + 1) * part)
+            plain = tok_ref[at].astype(F32)
+            inverse = lax.rsqrt(jnp.mean(plain * plain, axis=-1, keepdims=True) + EPSILON)
+            plain = plain * inverse
+            grad = grad_vm[at]
+            mean = jnp.mean(grad * plain, axis=-1, keepdims=True)
+            to = pl.ds(pl.multiple_of(numbers_ref[9 + i] * part, part), part)
+            out_ref[to] = mid_ref[at].astype(F32) + inverse * (grad - plain * mean)
+
+    picked = lambda i, n: (n[8], 0)
+    flat = lambda i, n: (0, 0)
+    return pl.pallas_call(
+        body,
+        grid_spec=pltpu.PrefetchScalarGridSpec(
+            num_scalar_prefetch=1,
+            grid=(1,),
+            in_specs=[
+                pl.BlockSpec((4 * part, wide), picked),
+                pl.BlockSpec((depth, wide), flat),
+                pl.BlockSpec((4 * part, depth), picked),
+                pl.BlockSpec((4 * part, depth), picked),
+                pl.BlockSpec((1, depth), flat),
+            ],
+            out_specs=pl.BlockSpec((4 * part, depth), flat),
+            scratch_shapes=[pltpu.VMEM((4 * part, depth), F32)],
+        ),
+        out_shape=jax.ShapeDtypeStruct((4 * part, depth), F32),
+        compiler_params=ROOMY,
+        cost_estimate=cost(4 * part * depth * wide, 2 * depth * wide + 8 * part * depth * 4),
+    )(numbers, grad_lat, first_all, grad_mid, tokens, gain.reshape(1, -1))
+
+
+def first_finish(numbers, quarters, first_w, gain, latent_width):
+    rows, lane = quarters[0].shape
+    wide = first_w.shape[1]
+
+    def body(numbers_ref, *refs):
+        weight_ref, gain_ref, down_ref, key_ref, value_ref, one_ref, all_vm = refs[4:]
+        for i in range(4):
+            cols = pl.ds(pl.multiple_of(numbers_ref[25 + i] * lane, lane), lane)
+            all_vm[:, cols] = refs[i][...].astype(F32)
+        down_ref[...] = all_vm[:, :latent_width]
+        key_ref[...] = all_vm[:, latent_width : latent_width + HD]
+        value_ref[...] = all_vm[:, latent_width + HD :]
+        total = jnp.sum(weight_ref[...].astype(F32) * all_vm[...], axis=1, keepdims=True)
+        one_ref[...] = total / gain_ref[...]
+
+    flat = lambda i, n: (0, 0)
+    extents = [(rows, latent_width), (rows, HD), (rows, wide - latent_width - HD), (rows, 1)]
+    *grads, one = pl.pallas_call(
+        body,
+        grid_spec=pltpu.PrefetchScalarGridSpec(
+            num_scalar_prefetch=1,
+            grid=(1,),
+            in_specs=[pl.BlockSpec((rows, lane), flat)] * 4
+            + [pl.BlockSpec((rows, wide), flat), pl.BlockSpec((rows, 1), flat)],
+            out_specs=[pl.BlockSpec(e, flat) for e in extents],
+            scratch_shapes=[pltpu.VMEM((rows, wide), F32)],
+        ),
+        out_shape=[jax.ShapeDtypeStruct(e, F32) for e in extents],
+        compiler_params=ROOMY,
+        cost_estimate=cost(0, 10 * rows * wide),
+    )(numbers, *quarters, first_w, gain.reshape(-1, 1))
+    return (*grads, one.reshape(-1))
+
+
+def trade(pieces):
+    own, y_piece, x_piece, xy_piece = pieces
+    return [own, send(y_piece, OVER_Y), send(x_piece, OVER_X), send(xy_piece, OVER_XY)]
+
+
+def added(pieces):
+    total = pieces[0].astype(F32)
+    for piece in pieces[1:]:
+        total = total + piece.astype(F32)
+    return total
+
+
+def sum_pieces(pieces):
+    return added(trade(pieces))
+
+
+def spread(part):
+    return [part, send(part, OVER_Y), send(part, OVER_X), send(part, OVER_XY)]
+
+
+def over_core(arrays):
+    return [send(array, OVER_C) for array in arrays]
+
+
+def fast_device(
+    tokens_in,
+    cotangent,
+    seq_lengths,
+    block_order,
+    gain_one,
+    down_q,
+    gain_q,
+    up_q,
+    key_w,
+    value_w,
+    out_w,
+    gain_two,
+    gate_w,
+    up_w,
+    down_w,
+):
+    z = lax.axis_index("dp")
+    x = lax.axis_index("ctx")
+    t = lax.axis_index("tensor")
+    y = t // 2
+    c = t % 2
+    stays = x == c
+    quarter = x * 2 + y
+    rows, depth = tokens_in.shape
+    half = rows // 2
+    part = rows // 4
+    latent_width = down_q.shape[1]
+    cols = up_q.shape[1] // 2
+    ks = jnp.arange(4, dtype=jnp.int32)
+    z_order = z ^ ks
+    numbers = jnp.concatenate(
+        [
+            ks * 2 + c,
+            ks * 2 + (1 - c),
+            jnp.stack([c ^ x]),
+            quarter ^ ks,
+            z_order * 2 + x,
+            z_order * 2 + (1 - x),
+            jnp.stack([c, 1 - c, x, 1 - x, t, t ^ 1, t ^ 2, t ^ 3]),
+        ]
+    ).astype(jnp.int32)
+    at_same, at_quarter, at_x, at_c, at_t = 8, 9, 13, 21, 25
+
+    first_w = jnp.concatenate([down_q, key_w, value_w], axis=1)
+    wide = first_w.shape[1]
+    side = wide // 4
+    mine = lax.dynamic_slice_in_dim(first_w, t * side, side, axis=1)
+    attn_t = transpose(jnp.concatenate([up_q, out_w], axis=0), stays)
+    tok_got = send(rows_at(tokens_in, t * part, part), OVER_X)
+    first_own = stage(mine, send(mine, Z_ONE), send(mine, Z_TWO), send(mine, Z_THREE))
+    first_own = jnp.concatenate(first_own, axis=0)
+    first_blocks = [first_own] + [send(first_own, p) for p in (OVER_Y, OVER_X, OVER_XY)]
+    first_blocks = first_blocks + over_core(first_blocks)
+
+    def first_plan(n, ins, out):
+        listed = []
+        for i in range(8):
+            col = pl.ds(pl.multiple_of(n[at_t + (0, 2, 0, 2, 1, 3, 1, 3)[i]] * side, side), side)
+            for k in range(4):
+                place = n[at_x + (i % 4 // 2) * 4 + k]
+                row = pl.ds(pl.multiple_of(place * 256, 256), 256)
+                listed.append((None, ins[i].at[k * 256 : (k + 1) * 256], out.at[row, col]))
+        return listed
+
+    pair_t = transpose(after(jnp.concatenate([gate_w, up_w], axis=0), first_own, tok_got), stays)
+    first_all = place_copies(first_plan, numbers, first_blocks, (depth, wide), BF)
+
+    def rows_plan(n, ins, out):
+        listed = []
+        for o in range(2):
+            mine_too = (n[at_same] == o)
+            for f in range(4):
+                q = n[at_quarter + f]
+                to = out.at[pl.ds((o * 4 + f) * part, part)]
+                here = pl.ds(pl.multiple_of(q * part, part), part)
+                listed.append((mine_too, ins[0].at[here], to))
+                away = jnp.logical_not(mine_too)
+                for j in range(4):
+                    listed.append((away & (n[at_t + j] == q), ins[1 + j], to))
+        return listed
+
+    def group_rows(array, got):
+        got_y = send(got, OVER_Y)
+        buffers = [array, got, send(got, OVER_C), got_y, send(got_y, OVER_C)]
+        return place_copies(rows_plan, numbers, buffers, (2 * rows, depth), BF)
+
+    tokens = group_rows(tokens_in, tok_got)
+
+    attn_own = gather_z(attn_t)
+    attn_rows = attn_t.shape[0]
+    upq_rows = up_q.shape[0]
+    out_rows = out_w.shape[0]
+
+    def head_plan(start, count):
+        def plan(n, ins, out):
+            listed = []
+            for i in range(8):
+                row = pl.ds(pl.multiple_of(n[i] * count, count), count)
+                col = pl.ds(pl.multiple_of(n[at_c] * cols, cols), cols)
+                at = (i % 4) * attn_rows + start
+                listed.append((None, ins[i // 4].at[at : at + count, col], out.at[row]))
+            return listed
+
+        return plan
+
+
+    cot = group_rows(cotangent, send(rows_at(cotangent, t * part, part), OVER_X))
+
+    places = (
+        block_order[0][:, :, None] * half + jnp.arange(half, dtype=jnp.int32)[None, None, :]
+    ).reshape(2, 4, part)
+    places = jnp.stack(
+        [
+            lax.dynamic_index_in_dim(
+                lax.dynamic_index_in_dim(places, c ^ o, 0, False), quarter ^ f, 0, False
+            )
+            for o in range(2)
+            for f in range(4)
+        ]
+    ).reshape(-1)
+    second = (places >= seq_lengths[0, 0]).astype(jnp.int32)
+    sequence_start = second * seq_lengths[0, 0]
+    cosine, sine = angles_of((places - sequence_start).astype(F32), HD // 2)
+    row_info = jnp.stack([places, sequence_start], axis=1)
+    key_places = places[None, :]
+
+    token_rows = tokens.astype(F32)
+    plain_one, inverse_one = rms_parts(token_rows)
+    normed = (plain_one * gain_one).astype(BF)
+    lat = dot(normed, first_all)
+    pair_own = gather_z(pair_t)
+    down_t = transpose(after(down_w, first_all), stays)
+    attn_own = after(attn_own, lat)
+    attns = [attn_own, send(attn_own, OVER_C)]
+    up_q_all = place_copies(
+        head_plan(0, upq_rows), numbers, attns, (latent_width, cols), BF
+    )
+    out_all = place_copies(
+        head_plan(upq_rows, out_rows), numbers, attns, (depth, cols), BF
+    )
+    latent = lat[:, :latent_width]
+    plain_q, inverse_q = rms_parts(latent)
+    query_in = (plain_q * gain_q).astype(BF)
+    keys = turn(lat[:, latent_width : latent_width + HD], cosine, sine).astype(BF)
+    values = lat[:, latent_width + HD :].astype(BF)
+    query_pre = dot(query_in, up_q_all)
+    query, attended, lse = attention_forward(
+        query_pre, cosine, sine, keys, values, row_info, key_places
+    )
+    (give,) = product_pieces(attended, out_all, [], None, False)
+    pieces = product_pieces(attended, out_all, [], send(give, OVER_C), True)
+    middle, cot = stage(tokens[:part].astype(F32) + sum_pieces(pieces), cot)
+
+    plain_two, inverse_two = rms_parts(middle)
+    two_parts = spread((plain_two * gain_two).astype(BF))
+    *two_parts, pair_own, down_t = stage(*two_parts, pair_own, down_t)
+    down_own = gather_z(down_t)
+    pairs = [pair_own, send(pair_own, OVER_C)]
+    hidden, slope, silu = ffn_forward(numbers, two_parts, pairs)
+
+    def two(array, other):
+        return [(array, 0, rows, None), (other, 0, rows, None)]
+
+    width = down_w.shape[1]
+    (hidden_other,) = over_core([hidden])
+    down_slabs = weight_grads(
+        numbers, [([cot], 256, 0, [(None, two(hidden, hidden_other))])], width
+    )
+    down_slabs, hidden, down_own = stage(down_slabs, hidden, down_own)
+    down_sum = reduce_z(down_slabs)
+    downs = [down_own, send(down_own, OVER_C)]
+    grad_gate, grad_up, *pieces = ffn_backward(
+        numbers, after(cot, down_slabs), slope, silu, pairs, downs
+    )
+
+    gate_other, up_other = over_core([grad_gate, grad_up])
+    two_all = two_parts + over_core(two_parts)
+    pair_slabs = weight_grads(
+        numbers,
+        [
+            (two_all, 256, 0, [(None, two(grad_gate, gate_other))]),
+            (two_all, 256, 0, [(None, two(grad_up, up_other))]),
+        ],
+        width,
+    )
+    *pieces, pair_slabs, hidden = stage(*trade(pieces), pair_slabs, hidden)
+    grad_norm_two = added(pieces)
+    pair_sum = reduce_z(after(pair_slabs, down_sum))
+
+    grad_plain = grad_norm_two * gain_two
+    grad_mid = cot[:part].astype(F32) + inverse_two * (
+        grad_plain - plain_two * jnp.mean(grad_plain * plain_two, axis=-1, keepdims=True)
+    )
+    mid_parts = spread(grad_mid.astype(BF))
+    staged = stage(*mid_parts, *ffn_output(numbers, hidden, downs))
+    mid_parts, out_pieces = list(staged[:4]), staged[4:]
+    mid_parts = mid_parts + over_core(mid_parts)
+
+    def stack_plan(n, ins, out):
+        return [(None, ins[i], out.at[pl.ds(i * part, part)]) for i in range(8)]
+
+    grad_attended = product_of_parts(mid_parts, out_all)
+    grad_query_pre, key_acc, value_acc = attention_backward(
+        query, grad_attended, lse, cosine, sine, keys, values, row_info, key_places
+    )
+    staged = stage(*trade(out_pieces), grad_query_pre, key_acc, value_acc)
+    out_sum, (grad_query_pre, key_acc, value_acc) = staged[:4], staged[4:]
+    extras = [key_acc, value_acc]
+    (give,) = product_pieces(grad_query_pre, up_q_all, extras, None, False)
+    pieces = product_pieces(grad_query_pre, up_q_all, extras, send(give, OVER_C), True)
+    attended_other, query_other = over_core([attended, grad_query_pre])
+    *pieces, attended_other, query_other = stage(*pieces, attended_other, query_other)
+
+    def swapped(array):
+        return [(array, rows, rows, None), (array, 0, rows, None)]
+
+    attn_slabs = weight_grads(
+        numbers,
+        [
+            (
+                [query_in],
+                upq_rows,
+                0,
+                [
+                    (at_c, [(grad_query_pre, 0, 2 * rows, None)]),
+                    (at_c + 1, swapped(query_other)),
+                ],
+            ),
+            (
+                mid_parts,
+                out_rows,
+                0,
+                [
+                    (at_c, [(attended, 0, 2 * rows, None)]),
+                    (at_c + 1, swapped(attended_other)),
+                ],
+            ),
+        ],
+        2 * cols,
+    )
+    out_part = (middle + added(out_sum)).astype(BF)
+    *pieces, attn_slabs, out_part = stage(*trade(pieces), attn_slabs, out_part)
+    three = added(pieces)
+    attn_sum = reduce_z(after(attn_slabs, pair_sum))
+
+    grad_plain = three[:, :latent_width] * gain_q
+    plain_q_mine = plain_q[:part]
+    grad_latent = inverse_q[:part] * (
+        grad_plain - plain_q_mine * jnp.mean(grad_plain * plain_q_mine, axis=-1, keepdims=True)
+    )
+    grad_key_pre = turn(
+        three[:, latent_width : latent_width + HD], cosine[:part], -sine[:part]
+    )
+    lat_parts = spread(
+        jnp.concatenate(
+            [grad_latent, grad_key_pre, three[:, latent_width + HD :]], axis=1
+        ).astype(BF)
+    )
+    down_home = transpose(down_sum, stays)
+    grad_branch = place_copies(stack_plan, numbers, mid_parts, (2 * rows, depth), BF)
+    pair_home = transpose(pair_sum, stays)
+    staged = stage(*lat_parts, down_home, pair_home, grad_branch, out_part)
+    lat_parts, (down_home, pair_home, grad_branch, out_part) = list(staged[:4]), staged[4:]
+    lat_parts = lat_parts + over_core(lat_parts)
+
+    lane = wide // 4
+    first_slabs = weight_grads(
+        numbers,
+        [([normed], 256, at_x, [(None, [(p, 0, part, at_t) for p in lat_parts])])],
+        lane,
+    )
+    out_parts = spread(out_part)
+    out_parts = out_parts + over_core(out_parts)
+    grad_lat = place_copies(stack_plan, numbers, lat_parts, (2 * rows, wide), BF)
+    grad_tokens = input_gradient(numbers, grad_lat, first_all, grad_branch, tokens, gain_one)
+
+    def out_plan(n, ins, out):
+        listed = []
+        for f in range(4):
+            to = out.at[pl.ds(pl.multiple_of(n[at_quarter + f] * part, part), part)]
+            listed.append((n[at_same] == 0, ins[f], to))
+            listed.append((n[at_same] == 1, ins[4 + f], to))
+        return listed
+
+    attn_home = transpose(attn_sum, stays)
+    staged = stage(*trade_z(first_slabs), grad_tokens, attn_home, *out_parts)
+    first_quarter = added(staged[:4]).astype(BF)
+    grad_tokens, attn_home, *out_parts = staged[4:]
+    quarters = [first_quarter] + [send(first_quarter, p) for p in (OVER_C, OVER_Y, OVER_YC)]
+    dev = z * 2 + x
+    block = depth // 8
+    own_one = lax.dynamic_slice_in_dim(gain_one, dev * block, block)
+    grad_down_q, grad_key_w, grad_value_w, grad_gain_one = first_finish(
+        numbers, quarters, first_w, own_one, latent_width
+    )
+    result = place_copies(out_plan, numbers, out_parts, (rows, depth), BF)
+
+    grad_down_w = down_home.astype(F32)
+    pair_home = pair_home.astype(F32)
+    grad_gate_w, grad_up_w = pair_home[:256], pair_home[256:]
+    attn_home = attn_home.astype(F32)
+    grad_up_q, grad_out_w = attn_home[:upq_rows], attn_home[upq_rows:]
+
+    own_two = lax.dynamic_slice_in_dim(gain_two, dev * block, block)
+    own_q = lax.dynamic_slice_in_dim(gain_q, dev * upq_rows, upq_rows)
+    two_sum = jnp.sum(gate_w.astype(F32) * grad_gate_w + up_w.astype(F32) * grad_up_w, axis=1)
+    q_sum = jnp.sum(up_q.astype(F32) * grad_up_q, axis=1)
+    small = jnp.concatenate([two_sum, q_sum]).reshape(3, -1)
+    small = small + send(small, OVER_C) + send(small, OVER_Y) + send(small, OVER_YC)
+    small = small.reshape(-1)
+    grad_gain_two = small[:block] / own_two
+    grad_gain_q = small[block:] / own_q
+
+    return (
+        result,
+        grad_tokens,
+        grad_gain_one,
+        grad_down_q,
+        grad_gain_q,
+        grad_up_q,
+        grad_key_w,
+        grad_value_w,
+        grad_out_w,
+        grad_gain_two,
+        grad_gate_w,
+        grad_up_w,
+        grad_down_w,
+    )
+
+
+def rows_at(array, start, count):
+    return lax.dynamic_slice_in_dim(array, start, count, axis=0)
 
 
 def rotate(array, places):
@@ -305,8 +1311,9 @@
 
 
 def solution(mesh):
+    fast = dict(mesh.shape) == {"dp": 4, "ctx": 2, "tensor": 4}
     return jax.shard_map(
-        per_device,
+        fast_device if fast else per_device,
         mesh=mesh,
         in_specs=(
             P(("dp", "ctx"), None),

time: 2230 us -> 624 us (0.28)
  waiting for transfers between devices: 1810 us -> 253 us
  matrix products: 225 us -> 14.3 us
  Pallas kernels: 0 us -> 184 us
  blocking collectives: 80.5 us -> 0 us
  starting transfers between devices: 1.51 us -> 79.6 us
    reduce_scatter x10 -> x3, waiting for transfers between devices: 1080 us -> 12.1 us  [reduce_z(): return lax.psum_scatter(slabs, 'dp', scatter_dimension=0, tiled=True)]
    all_gather x8 -> x3, waiting for transfers between devices: 472 us -> 22.9 us  [gather_z(): return lax.all_gather(array, 'dp', axis=0, tiled=True)]
    psum x4 -> x0, waiting for transfers between devices: 251 us -> none  [the longest x1 151 us: backward(): lax.psum(times_trans(grad_gate, gate_w) + times_trans(grad_up, up_w), 'te...]
    ppermute x0 -> x83, waiting for transfers between devices: none -> 218 us  [send(): return lax.ppermute(array, AXES, pairs)]
    dot_general x62 -> x2, matrix products: 225 us -> 14.3 us  [dot(): return jnp.dot(left, right, preferred_element_type=F32)]
    pallas_call x0 -> x24, Pallas kernels: none -> 184 us  [the longest x8 37.8 us: place_copies(): pl.pallas_call(body, grid_spec=pltpu.PrefetchScalarGridSpec(num_scalar_pr...]
    ppermute x0 -> x83, starting transfers between devices: none -> 78.3 us  [send(): return lax.ppermute(array, AXES, pairs)]
    unnamed x1 -> x0, blocking collectives: 38.8 us -> none
  transfers between devices with their start and end apart: 22 -> 89, of which waited for: 20 -> 32; matrix products, arithmetic and copies ran while one was open for 9% -> 11% of each run, Pallas kernels for 0% -> 29%
where the time goes in v2:
time: 624 us; the launch traced here: 615 us
  waiting for transfers between devices  253 us (41%)
  Pallas kernels  184 us (29%)
  starting transfers between devices  79.6 us (13%)
  other arithmetic  37.9 us (6%)
  local copies, waits for them, and re-layouts  30.6 us (5%)
  between operations  15.6 us (2%)
  matrix products  14.3 us (2%)
    ppermute x83, waiting for transfers between devices, send(): return lax.ppermute(array, AXES, pairs)  218 us
    ppermute x83, starting transfers between devices, send(): return lax.ppermute(array, AXES, pairs)  78.3 us
    pallas_call x8, Pallas kernels, place_copies(): pl.pallas_call(body, grid_spec=pltpu.PrefetchScalarGridSpec(num_scalar_pr...  37.8 us
    pallas_call x4, Pallas kernels, weight_grads(): pl.pallas_call(body, grid_spec=pltpu.PrefetchScalarGridSpec(num_scalar_pr...  36.5 us
    all_gather x3, waiting for transfers between devices, gather_z(): return lax.all_gather(array, 'dp', axis=0, tiled=True)  22.9 us
    pallas_call x1, Pallas kernels, ffn_backward(): pl.pallas_call(body, grid_spec=pltpu.PrefetchScalarGridSpec(num_scalar_pr...  20.4 us
    pallas_call x4, Pallas kernels, product_pieces(): pl.pallas_call(body, in_specs=[WHOLE] * len(arrays), out_specs=[WHOLE] *...  18.5 us
    pallas_call x1, Pallas kernels, ffn_forward(): pl.pallas_call(body, grid_spec=pltpu.PrefetchScalarGridSpec(num_scalar_pr...  17.6 us
  transfers between devices with their start and end apart: 89, of which 32 were waited for; matrix products, arithmetic and copies ran while one was open for 11% of the time, Pallas kernels for 29%

profile of v2, /device:TPU:0, one launch (start us, length us, event | category | flops | bytes accessed | tf_op | source)
XLA Modules:
  0.0 615.3 jit_solution(14461428959595685673)
XLA Ops:
  27.8 8.3 %collective-permute-done.5 = bf16[256,384]{1,0:T(8,128)(2,1)} collective-permute-done((bf16[256,384]{1,0:T(8,128)(2,1)S(1)}, bf16[256,384]{1,0:T(8,128)(2,1)}, u32[]{:S(2)}, u32[]{:S(2)}) %collective-permute-start.5) | collective-permute-done | bytes 196640 | tf_op jit(solution)/shard_map/ppermute | solution.py:83
  52.0 30.5 %collective-permute-done.7.refs_1_ = bf16[1024,384]{1,0:T(8,128)(2,1)} collective-permute-done((bf16[1024,384]{1,0:T(8,128)(2,1)}, bf16[1024,384]{1,0:T(8,128)(2,1)}, u32[]{:S(2)}, u32[]{:S(2)}) %collective-permute-start.7) | collective-permute-done | bytes 786464 | tf_op jit(solution)/shard_map/ppermute | solution.py:83
  97.9 6.6 %shard_map.247.first_ref = bf16[2048,1536]{1,0:T(8,128)(2,1)} custom-call(s32[29]{0:T(128)} %concatenate.26.numbers_ref, bf16[1024,384]{1,0:T(8,128)(2,1)} %constant_dynamic-update-slice_fusion.3.refs_0_, bf16[1024,384]{1,0:T(8,128)(2,1)} %collective-permute-done.7.refs_1_, bf16[1024,384]{1,0:T(8,128)(2,1)} %collective-permute-done.8.refs_2_, ...), custom_call_target="tpu_custom_call" | custom-call | bytes 12582912 | tf_op jit(solution)/shard_map/pallas_call | solution.py:145
  104.5 10.5 %fusion.17 = f32[1024,1536]{1,0:T(8,128)} fusion(bf16[1024,2048]{1,0:T(8,128)(2,1)S(1)} %fusion.2.refs_0_, bf16[2048,1536]{1,0:T(8,128)(2,1)} %shard_map.247.first_ref), kind=kOutput, calls=%fused_computation.94 | convolution fusion | flops 6442450944 | bytes 16777216 | tf_op jit(solution)/shard_map/dot_general | solution.py:19
  143.4 8.4 %shard_map.249 = (bf16[1024,512]{1,0:T(8,128)(2,1)}, bf16[1024,512]{1,0:T(8,128)(2,1)}, f32[2,1024,1]{2,1,0:T(8,128)}) custom-call(f32[1024,512]{1,0:T(8,128)} %fusion.18.pre_ref, f32[1024,128]{1,0:T(8,128)} %get-tuple-element.243.cos_ref, f32[1024,128]{1,0:T(8,128)} %get-tuple-element.242.sin_ref, bf16[1024,256]{1,0:T(8,128)(2,1)} %pad_maximum_fusion.1.k_ref, ...), custom_call_target="tpu_custom_call" | custom-call | flops 4294967296 | bytes 3145728 | tf_op jit(solution)/shard_map/pallas_call | solution.py:186
  160.0 13.3 %collective-permute-done.20.refs_1_ = bf16[128,2048]{1,0:T(8,128)(2,1)S(1)} collective-permute-done((bf16[128,2048]{1,0:T(8,128)(2,1)S(1)}, bf16[128,2048]{1,0:T(8,128)(2,1)S(1)}, u32[]{:S(2)}, u32[]{:S(2)}) %collective-permute-start.20) | collective-permute-done | bytes 524320 | tf_op jit(solution)/shard_map/ppermute | solution.py:83
  174.9 11.5 %collective-permute-done.22.refs_3_ = bf16[128,2048]{1,0:T(8,128)(2,1)S(1)} collective-permute-done((bf16[128,2048]{1,0:T(8,128)(2,1)S(1)}, bf16[128,2048]{1,0:T(8,128)(2,1)S(1)}, u32[]{:S(2)}, u32[]{:S(2)}) %collective-permute-start.22) | collective-permute-done | bytes 524320 | tf_op jit(solution)/shard_map/ppermute | solution.py:83
  209.4 10.4 %collective-permute-done.19 = bf16[128,2048]{1,0:T(8,128)(2,1)S(1)} collective-permute-done((bf16[128,2048]{1,0:T(8,128)(2,1)}, bf16[128,2048]{1,0:T(8,128)(2,1)S(1)}, u32[]{:S(2)}, u32[]{:S(2)}) %collective-permute-start.19) | collective-permute-done | bytes 524320 | tf_op jit(solution)/shard_map/ppermute | solution.py:83
  227.2 7.9 %collective-permute-done.24.refs_1_.refs_9_ = bf16[128,2048]{1,0:T(8,128)(2,1)S(1)} collective-permute-done((bf16[128,2048]{1,0:T(8,128)(2,1)S(1)}, bf16[128,2048]{1,0:T(8,128)(2,1)S(1)}, u32[]{:S(2)}, u32[]{:S(2)}) %collective-permute-start.24) | collective-permute-done | bytes 524320 | tf_op jit(solution)/shard_map/ppermute | solution.py:83
  235.0 6.4 %collective-permute-done.25.refs_2_.refs_10_ = bf16[128,2048]{1,0:T(8,128)(2,1)S(1)} collective-permute-done((bf16[128,2048]{1,0:T(8,128)(2,1)S(1)}, bf16[128,2048]{1,0:T(8,128)(2,1)S(1)}, u32[]{:S(2)}, u32[]{:S(2)}) %collective-permute-start.25) | collective-permute-done | bytes 524320 | tf_op jit(solution)/shard_map/ppermute | solution.py:83
  241.4 8.6 %collective-permute-done.26.refs_3_.refs_11_ = bf16[128,2048]{1,0:T(8,128)(2,1)S(1)} collective-permute-done((bf16[128,2048]{1,0:T(8,128)(2,1)S(1)}, bf16[128,2048]{1,0:T(8,128)(2,1)S(1)}, u32[]{:S(2)}, u32[]{:S(2)}) %collective-permute-start.26) | collective-permute-done | bytes 524320 | tf_op jit(solution)/shard_map/ppermute | solution.py:83
  250.6 9.2 %collective-permute-done.29.refs_5_.refs_4_ = bf16[2048,1408]{1,0:T(8,128)(2,1)} collective-permute-done((bf16[2048,1408]{1,0:T(8,128)(2,1)}, bf16[2048,1408]{1,0:T(8,128)(2,1)}, u32[]{:S(2)}, u32[]{:S(2)}) %collective-permute-start.29) | collective-permute-done | bytes 5767200 | tf_op jit(solution)/shard_map/ppermute | solution.py:83
  259.8 17.6 %shard_map.254 = (bf16[512,1408]{1,0:T(8,128)(2,1)}, f32[512,1408]{1,0:T(8,128)}, f32[512,1408]{1,0:T(8,128)}) custom-call(s32[29]{0:T(128)} %concatenate.26.numbers_ref, bf16[128,2048]{1,0:T(8,128)(2,1)} %copy-done.6, bf16[128,2048]{1,0:T(8,128)(2,1)} %copy-done.23, bf16[128,2048]{1,0:T(8,128)(2,1)} %copy-done.25, bf16[128,2048]{1,0:T(8,128)(2,1)} %copy-done.27, ...), custom_call_target="tpu_custom_call" | custom-call | flops 5905580032 | bytes 11534336 | tf_op jit(solution)/shard_map/pallas_call | solution.py:392
  282.0 8.0 %shard_map.255 = bf16[1024,1408]{1,0:T(8,128)(2,1)} custom-call(s32[29]{0:T(128)} %concatenate.26.numbers_ref, bf16[1024,2048]{1,0:T(8,128)(2,1)} %shard_map.253.refs_0_, bf16[512,1408]{1,0:T(8,128)(2,1)} %get-tuple-element.157.refs_1_.hid_ref, bf16[512,1408]{1,0:T(8,128)(2,1)} %copy-done.37), custom_call_target="tpu_custom_call" | custom-call | flops 738197504 | bytes 1441792 | tf_op jit(solution)/shard_map/pallas_call | solution.py:592
  290.0 22.2 %all-gather.8.cloned.1.call-done.refs_5_.refs_0_ = bf16[1024,1408]{1,0:T(8,128)(2,1)} async-done(((bf16[256,1408]{1,0:T(8,128)(2,1)}), bf16[1024,1408]{1,0:T(8,128)(2,1)}) %all-gather.8.cloned.1.call-update) | async-done | bytes 2883600 | tf_op jit(solution)/shard_map/all_gather | solution.py:99
  312.4 5.5 collective-permute-done.31.refs_6_.refs_1_
  319.4 20.4 %shard_map.256 = (bf16[512,1408]{1,0:T(8,128)(2,1)}, bf16[512,1408]{1,0:T(8,128)(2,1)}, bf16[128,2048]{1,0:T(8,128)(2,1)}, bf16[128,2048]{1,0:T(8,128)(2,1)}, bf...) custom-call(s32[29]{0:T(128)} %concatenate.26.numbers_ref, bf16[1024,2048]{1,0:T(8,128)(2,1)} %shard_map.253.refs_0_, ...), custom_call_target="tpu_custom_call" | custom-call | flops 8858370048 | bytes 17301504 | tf_op jit(solution)/shard_map/pallas_call | solution.py:470
  350.6 13.3 %shard_map.257 = bf16[2048,1408]{1,0:T(8,128)(2,1)} custom-call(s32[29]{0:T(128)} %concatenate.26.numbers_ref, bf16[128,2048]{1,0:T(8,128)(2,1)} %copy-done.6, bf16[128,2048]{1,0:T(8,128)(2,1)} %copy-done.23, bf16[128,2048]{1,0:T(8,128)(2,1)} %copy-done.25, bf16[128,2048]{1,0:T(8,128)(2,1)} %copy-done.27, bf16[128,2048]{1,0:T(8,128)(2,1)} %copy-done.29, ...), custom_call_target="tpu_custom_call" | custom-call | flops 1476395008 | bytes 2883584 | tf_op jit(solution)/shard_map/pallas_call | solution.py:592
  363.9 9.9 %collective-permute-done.34 = bf16[128,2048]{1,0:T(8,128)(2,1)S(1)} collective-permute-done((bf16[128,2048]{1,0:T(8,128)(2,1)}, bf16[128,2048]{1,0:T(8,128)(2,1)S(1)}, u32[]{:S(2)}, u32[]{:S(2)}) %collective-permute-start.34) | collective-permute-done | bytes 524320 | tf_op jit(solution)/shard_map/ppermute | solution.py:83
  380.8 10.8 %shard_map.258 = (bf16[128,2048]{1,0:T(8,128)(2,1)}, bf16[128,2048]{1,0:T(8,128)(2,1)}, bf16[128,2048]{1,0:T(8,128)(2,1)}, bf16[128,2048]{1,0:T(8,128)(2,1)}) custom-call(s32[29]{0:T(128)} %concatenate.26.numbers_ref, bf16[512,1408]{1,0:T(8,128)(2,1)} %get-tuple-element.157.refs_1_.hid_ref, bf16[1024,1408]{1,0:T(8,128)(2,1)} %all-gather.8.cloned.1.call-done.refs_5_.refs_0_, ...), custom_call_target="tpu_custom_call" | custom-call | flops 738197504 | bytes 1441792 | tf_op jit(solution)/shard_map/pallas_call | solution.py:523
  392.7 10.2 %collective-permute-done.43.refs_3_.refs_4_ = bf16[128,2048]{1,0:T(8,128)(2,1)S(1)} collective-permute-done((bf16[128,2048]{1,0:T(8,128)(2,1)S(1)}, bf16[128,2048]{1,0:T(8,128)(2,1)S(1)}, u32[]{:S(2)}, u32[]{:S(2)}) %collective-permute-start.43) | collective-permute-done | bytes 524320 | tf_op jit(solution)/shard_map/ppermute | solution.py:83
  409.0 6.2 %shard_map.259.do_ref = bf16[1024,512]{1,0:T(8,128)(2,1)} custom-call(bf16[128,2048]{1,0:T(8,128)(2,1)} %copy-done.5, bf16[128,2048]{1,0:T(8,128)(2,1)} %copy-done.16, bf16[128,2048]{1,0:T(8,128)(2,1)} %copy-done.17, bf16[128,2048]{1,0:T(8,128)(2,1)} %copy-done.18, bf16[128,2048]{1,0:T(8,128)(2,1)} %copy-done.19, bf16[128,2048]{1,0:T(8,128)(2,1)} %copy-done.20, ...), custom_call_target="tpu_custom_call" | custom-call | flops 2147483648 | bytes 2097152 | tf_op jit(solution)/shard_map/pallas_call | solution.py:288
  415.2 12.9 %shard_map.260 = (bf16[1024,512]{1,0:T(8,128)(2,1)}, f32[1024,256]{1,0:T(8,128)}, f32[1024,256]{1,0:T(8,128)}) custom-call(bf16[1024,512]{1,0:T(8,128)(2,1)} %get-tuple-element.166.q_ref, bf16[1024,512]{1,0:T(8,128)(2,1)} %shard_map.259.do_ref, f32[2,1024,1]{2,1,0:T(8,128)} %get-tuple-element.171.lse_ref, f32[1024,128]{1,0:T(8,128)} %get-tuple-element.243.cos_ref, ...), custom_call_target="tpu_custom_call" | custom-call | flops 8589934592 | bytes 3145728 | tf_op jit(solution)/shard_map/pallas_call | solution.py:248
  451.5 9.5 %shard_map.263 = bf16[1536,1024]{1,0:T(8,128)(2,1)} custom-call(s32[29]{0:T(128)} %concatenate.26.numbers_ref, bf16[1024,1024]{1,0:T(8,128)(2,1)} %get-tuple-element.232.refs_0_, bf16[128,2048]{1,0:T(8,128)(2,1)} %copy-done.5, bf16[128,2048]{1,0:T(8,128)(2,1)} %copy-done.16, bf16[128,2048]{1,0:T(8,128)(2,1)} %copy-done.17, bf16[128,2048]{1,0:T(8,128)(2,1)} %copy-done.18, ...), custom_call_target="tpu_custom_call" | custom-call | flops 805306368 | bytes 1572864 | tf_op jit(solution)/shard_map/pallas_call | solution.py:592
  461.1 5.5 collective-permute-done.56
  466.6 7.8 %reduce-scatter.6.cloned.1.call-done = bf16[512,1408]{1,0:T(8,128)(2,1)} async-done(((bf16[2048,1408]{1,0:T(8,128)(2,1)}), bf16[512,1408]{1,0:T(8,128)(2,1)}) %reduce-scatter.6.cloned.1.call-update) | async-done | bytes 1441808 | tf_op jit(solution)/shard_map/reduce_scatter | solution.py:103
  486.8 9.5 %collective-permute-start.58 = (bf16[128,1536]{1,0:T(8,128)(2,1)S(1)}, bf16[128,1536]{1,0:T(8,128)(2,1)}, u32[]{:S(2)}, u32[]{:S(2)}) collective-permute-start(bf16[128,1536]{1,0:T(8,128)(2,1)S(1)} %pad_maximum_fusion.2.refs_1_.refs_0_), channel_id=1, source_target_pairs={{0,4},{1,5},{2,6},{3,7},{4,0},{5,1},{6,2},{7,3},{8,12},{9,13},{10,... | collective-permute-start | bytes 1179656 | tf_op jit(solution)/shard_map/ppermute | solution.py:83
  496.5 24.2 %collective-permute-done.58.refs_3_.refs_2_ = bf16[128,1536]{1,0:T(8,128)(2,1)} collective-permute-done((bf16[128,1536]{1,0:T(8,128)(2,1)S(1)}, bf16[128,1536]{1,0:T(8,128)(2,1)}, u32[]{:S(2)}, u32[]{:S(2)}) %collective-permute-start.58) | collective-permute-done | bytes 393248 | tf_op jit(solution)/shard_map/ppermute | solution.py:83
  545.6 5.7 shard_map.265
  556.7 11.8 %shard_map.267 = f32[512,2048]{1,0:T(8,128)} custom-call(s32[29]{0:T(128)} %concatenate.26.numbers_ref, bf16[1024,1536]{1,0:T(8,128)(2,1)} %shard_map.266.lat_ref, bf16[2048,1536]{1,0:T(8,128)(2,1)} %shard_map.247.first_ref, bf16[1024,2048]{1,0:T(8,128)(2,1)} %shard_map.264.mid_ref, bf16[1024,2048]{1,0:T(8,128)(2,1)} %shard_map.246.tok_ref, f32[1,2048]{1,0:T(1,128)} %bitcast.59), custom_call_target="tpu_custom_call" | custom-call | flops 3221225472 | bytes 14680064 | tf_op jit(solution)/shard_map/pallas_call | solution.py:627
  572.4 13.2 %collective-permute-done.67 = bf16[256,384]{1,0:T(8,128)(2,1)S(1)} collective-permute-done((bf16[256,384]{1,0:T(8,128)(2,1)S(1)}, bf16[256,384]{1,0:T(8,128)(2,1)S(1)}, u32[]{:S(2)}, u32[]{:S(2)}) %collective-permute-start.67) | collective-permute-done | bytes 196640 | tf_op jit(solution)/shard_map/ppermute | solution.py:83
  596.8 5.5 collective-permute-done.79.refs_3_
  (414 shorter events, 238.5 us)
Async XLA Ops:
  7.2 107.8 %all-gather.4.cloned.1.call-start = ((), (), s32[]{:S(2)}) async-start(), calls=%async_computation.3 | async-start | bytes 3932160 | tf_op jit(solution)/shard_map/all_gather | solution.py:99
  12.0 24.1 %collective-permute-start = (bf16[128,2048]{1,0:T(8,128)(2,1)}, bf16[128,2048]{1,0:T(8,128)(2,1)}, u32[]{:S(2)}, u32[]{:S(2)}) collective-permute-start(bf16[128,2048]{1,0:T(8,128)(2,1)} %constant_dynamic-slice_fusion.10), channel_id=1, source_target_pairs={{0,4},{1,5},{2,6},{3,7},{4,0},{5,1},{6,2},{7,3},{8,12},{9,13},{10,... | collective-permute-start | bytes 1572872 | tf_op jit(solution)/shard_map/ppermute | solution.py:83
  22.6 204.5 %all-gather.6.cloned.1.call-start = ((), (), s32[]{:S(2)}) async-start(), calls=%async_computation.4 | async-start | bytes 7208960 | tf_op jit(solution)/shard_map/all_gather | solution.py:99
  42.3 40.2 %collective-permute-start.7 = (bf16[1024,384]{1,0:T(8,128)(2,1)}, bf16[1024,384]{1,0:T(8,128)(2,1)}, u32[]{:S(2)}, u32[]{:S(2)}) collective-permute-start(bf16[1024,384]{1,0:T(8,128)(2,1)} %constant_dynamic-update-slice_fusion.3.refs_0_), channel_id=1, source_target_pairs={{0,2},{1,3},{2,0},{3,1},{4,6},{5,7},{6,4},{7,5},{8,10},{9,11},{10,... | collective-permute-start | bytes 2359304 | tf_op jit(solution)/shard_map/ppermute | solution.py:83
  42.8 39.7 %collective-permute-start.8 = (bf16[1024,384]{1,0:T(8,128)(2,1)}, bf16[1024,384]{1,0:T(8,128)(2,1)}, u32[]{:S(2)}, u32[]{:S(2)}) collective-permute-start(bf16[1024,384]{1,0:T(8,128)(2,1)} %constant_dynamic-update-slice_fusion.3.refs_0_), channel_id=1, source_target_pairs={{0,4},{1,5},{2,6},{3,7},{4,0},{5,1},{6,2},{7,3},{8,12},{9,13},{10,... | collective-permute-start | bytes 2359304 | tf_op jit(solution)/shard_map/ppermute | solution.py:83
  42.8 41.5 %collective-permute-start.9 = (bf16[1024,384]{1,0:T(8,128)(2,1)}, bf16[1024,384]{1,0:T(8,128)(2,1)}, u32[]{:S(2)}, u32[]{:S(2)}) collective-permute-start(bf16[1024,384]{1,0:T(8,128)(2,1)} %constant_dynamic-update-slice_fusion.3.refs_0_), channel_id=1, source_target_pairs={{0,6},{1,7},{2,4},{3,5},{4,2},{5,3},{6,0},{7,1},{8,14},{9,15},{10,... | collective-permute-start | bytes 2359304 | tf_op jit(solution)/shard_map/ppermute | solution.py:83
  45.8 40.4 %collective-permute-start.1 = (bf16[128,2048]{1,0:T(8,128)(2,1)}, bf16[128,2048]{1,0:T(8,128)(2,1)}, u32[]{:S(2)}, u32[]{:S(2)}) collective-permute-start(bf16[128,2048]{1,0:T(8,128)(2,1)} %collective-permute-done.refs_1_), channel_id=1, source_target_pairs={{0,1},{1,0},{2,3},{3,2},{4,5},{5,4},{6,7},{7,6},{8,9},{9,8},{10,11... | collective-permute-start | bytes 1572872 | tf_op jit(solution)/shard_map/ppermute | solution.py:83
  51.2 35.0 %collective-permute-start.3 = (bf16[128,2048]{1,0:T(8,128)(2,1)}, bf16[128,2048]{1,0:T(8,128)(2,1)}, u32[]{:S(2)}, u32[]{:S(2)}) collective-permute-start(bf16[128,2048]{1,0:T(8,128)(2,1)} %collective-permute-done.2.refs_3_), channel_id=1, source_target_pairs={{0,1},{1,0},{2,3},{3,2},{4,5},{5,4},{6,7},{7,6},{8,9},{9,8},{10,11... | collective-permute-start | bytes 1572872 | tf_op jit(solution)/shard_map/ppermute | solution.py:83
  82.5 32.7 %collective-permute-start.27 = (bf16[512,1408]{1,0:T(8,128)(2,1)S(1)}, bf16[512,1408]{1,0:T(8,128)(2,1)}, u32[]{:S(2)}, u32[]{:S(2)}) collective-permute-start(bf16[512,1408]{1,0:T(8,128)(2,1)S(1)} %pad_maximum_fusion), channel_id=1, source_target_pairs={{1,4},{3,6},{4,1},{6,3},{9,12},{11,14},{12,9},{14,11},{17,20},{19,... | collective-permute-start | bytes 4325384 | tf_op jit(solution)/shard_map/ppermute | solution.py:83
  116.4 195.8 %all-gather.8.cloned.1.call-start = ((), (), s32[]{:S(2)}) async-start(), calls=%async_computation.5 | async-start | bytes 3604480 | tf_op jit(solution)/shard_map/all_gather | solution.py:99
  156.4 30.0 %collective-permute-start.16 = (bf16[512,2048]{1,0:T(8,128)(2,1)}, bf16[512,2048]{1,0:T(8,128)(2,1)S(1)}, u32[]{:S(2)}, u32[]{:S(2)}) collective-permute-start(bf16[512,2048]{1,0:T(8,128)(2,1)} %shard_map.251), channel_id=1, source_target_pairs={{0,1},{1,0},{2,3},{3,2},{4,5},{5,4},{6,7},{7,6},{8,9},{9,8},{10,11... | collective-permute-start | bytes 6291464 | tf_op jit(solution)/shard_map/ppermute | solution.py:83
  196.0 23.8 %collective-permute-start.19 = (bf16[128,2048]{1,0:T(8,128)(2,1)}, bf16[128,2048]{1,0:T(8,128)(2,1)S(1)}, u32[]{:S(2)}, u32[]{:S(2)}) collective-permute-start(bf16[128,2048]{1,0:T(8,128)(2,1)} %get-tuple-element.129), channel_id=1, source_target_pairs={{0,6},{1,7},{2,4},{3,5},{4,2},{5,3},{6,0},{7,1},{8,14},{9,15},{10,... | collective-permute-start | bytes 1572872 | tf_op jit(solution)/shard_map/ppermute | solution.py:83
  203.1 22.4 %collective-permute-start.28 = (bf16[256,1408]{1,0:T(8,128)(2,1)S(1)}, bf16[256,1408]{1,0:T(8,128)(2,1)S(1)}, u32[]{:S(2)}, u32[]{:S(2)}) collective-permute-start(bf16[256,1408]{1,0:T(8,128)(2,1)S(1)} %copy-done.45), channel_id=1, source_target_pairs={{1,4},{3,6},{4,1},{6,3},{9,12},{11,14},{12,9},{14,11},{17,20},{19,... | collective-permute-start | bytes 2162696 | tf_op jit(solution)/shard_map/ppermute | solution.py:83
  225.5 24.5 %collective-permute-start.26 = (bf16[128,2048]{1,0:T(8,128)(2,1)S(1)}, bf16[128,2048]{1,0:T(8,128)(2,1)S(1)}, u32[]{:S(2)}, u32[]{:S(2)}) collective-permute-start(bf16[128,2048]{1,0:T(8,128)(2,1)S(1)} %multiply_convert_fusion.1.refs_0_.refs_8_), channel_id=1, source_target_pairs={{0,6},{1,7},{2,4},{3,5},{4,2},{5,3},{6,0},{7,1},{8,14},{9,15},{10,... | collective-permute-start | bytes 1572872 | tf_op jit(solution)/shard_map/ppermute | solution.py:83
  250.0 123.7 %reduce-scatter.4.cloned.1.call-start = ((), (), s32[]{:S(2)}) async-start(), calls=%async_computation.6 | async-start | bytes 3604480 | tf_op jit(solution)/shard_map/reduce_scatter | solution.py:103
  312.2 162.1 %reduce-scatter.6.cloned.1.call-start = ((), (), s32[]{:S(2)}) async-start(), calls=%async_computation.7 | async-start | bytes 7208960 | tf_op jit(solution)/shard_map/reduce_scatter | solution.py:103
  349.0 24.7 %collective-permute-start.34 = (bf16[128,2048]{1,0:T(8,128)(2,1)}, bf16[128,2048]{1,0:T(8,128)(2,1)S(1)}, u32[]{:S(2)}, u32[]{:S(2)}) collective-permute-start(bf16[128,2048]{1,0:T(8,128)(2,1)} %get-tuple-element.149), channel_id=1, source_target_pairs={{0,6},{1,7},{2,4},{3,5},{4,2},{5,3},{6,0},{7,1},{8,14},{9,15},{10,... | collective-permute-start | bytes 1572872 | tf_op jit(solution)/shard_map/ppermute | solution.py:83
  373.8 163.6 %reduce-scatter.8.cloned.1.call-start = ((), (), s32[]{:S(2)}) async-start(), calls=%async_computation.8 | async-start | bytes 3932160 | tf_op jit(solution)/shard_map/reduce_scatter | solution.py:103
  379.3 23.5 %collective-permute-start.43 = (bf16[128,2048]{1,0:T(8,128)(2,1)S(1)}, bf16[128,2048]{1,0:T(8,128)(2,1)S(1)}, u32[]{:S(2)}, u32[]{:S(2)}) collective-permute-start(bf16[128,2048]{1,0:T(8,128)(2,1)S(1)} %add_convert_fusion.1.refs_0_.refs_1_), channel_id=1, source_target_pairs={{0,6},{1,7},{2,4},{3,5},{4,2},{5,3},{6,0},{7,1},{8,14},{9,15},{10,... | collective-permute-start | bytes 1572872 | tf_op jit(solution)/shard_map/ppermute | solution.py:83
  403.9 24.2 %collective-permute-start.44 = (bf16[128,2048]{1,0:T(8,128)(2,1)}, bf16[128,2048]{1,0:T(8,128)(2,1)S(1)}, u32[]{:S(2)}, u32[]{:S(2)}) collective-permute-start(bf16[128,2048]{1,0:T(8,128)(2,1)} %get-tuple-element.163), channel_id=1, source_target_pairs={{0,2},{1,3},{2,0},{3,1},{4,6},{5,7},{6,4},{7,5},{8,10},{9,11},{10,... | collective-permute-start | bytes 1572872 | tf_op jit(solution)/shard_map/ppermute | solution.py:83
  404.8 23.3 %collective-permute-start.45 = (bf16[128,2048]{1,0:T(8,128)(2,1)}, bf16[128,2048]{1,0:T(8,128)(2,1)S(1)}, u32[]{:S(2)}, u32[]{:S(2)}) collective-permute-start(bf16[128,2048]{1,0:T(8,128)(2,1)} %get-tuple-element.164), channel_id=1, source_target_pairs={{0,4},{1,5},{2,6},{3,7},{4,0},{5,1},{6,2},{7,3},{8,12},{9,13},{10,... | collective-permute-start | bytes 1572872 | tf_op jit(solution)/shard_map/ppermute | solution.py:83
  406.3 24.2 %collective-permute-start.46 = (bf16[128,2048]{1,0:T(8,128)(2,1)}, bf16[128,2048]{1,0:T(8,128)(2,1)S(1)}, u32[]{:S(2)}, u32[]{:S(2)}) collective-permute-start(bf16[128,2048]{1,0:T(8,128)(2,1)} %get-tuple-element.165), channel_id=1, source_target_pairs={{0,6},{1,7},{2,4},{3,5},{4,2},{5,3},{6,0},{7,1},{8,14},{9,15},{10,... | collective-permute-start | bytes 1572872 | tf_op jit(solution)/shard_map/ppermute | solution.py:83
  486.8 33.9 %collective-permute-start.58 = (bf16[128,1536]{1,0:T(8,128)(2,1)S(1)}, bf16[128,1536]{1,0:T(8,128)(2,1)}, u32[]{:S(2)}, u32[]{:S(2)}) collective-permute-start(bf16[128,1536]{1,0:T(8,128)(2,1)S(1)} %pad_maximum_fusion.2.refs_1_.refs_0_), channel_id=1, source_target_pairs={{0,4},{1,5},{2,6},{3,7},{4,0},{5,1},{6,2},{7,3},{8,12},{9,13},{10,... | collective-permute-start | bytes 1179656 | tf_op jit(solution)/shard_map/ppermute | solution.py:83
  496.3 29.5 %collective-permute-start.59 = (bf16[128,1536]{1,0:T(8,128)(2,1)S(1)}, bf16[128,1536]{1,0:T(8,128)(2,1)}, u32[]{:S(2)}, u32[]{:S(2)}) collective-permute-start(bf16[128,1536]{1,0:T(8,128)(2,1)S(1)} %pad_maximum_fusion.2.refs_1_.refs_0_), channel_id=1, source_target_pairs={{0,6},{1,7},{2,4},{3,5},{4,2},{5,3},{6,0},{7,1},{8,14},{9,15},{10,... | collective-permute-start | bytes 1179656 | tf_op jit(solution)/shard_map/ppermute | solution.py:83
  528.3 24.3 %collective-permute-start.70 = (bf16[128,2048]{1,0:T(8,128)(2,1)}, bf16[128,2048]{1,0:T(8,128)(2,1)}, u32[]{:S(2)}, u32[]{:S(2)}) collective-permute-start(bf16[128,2048]{1,0:T(8,128)(2,1)} %add_convert_fusion.refs_0_), channel_id=1, source_target_pairs={{0,2},{1,3},{2,0},{3,1},{4,6},{5,7},{6,4},{7,5},{8,10},{9,11},{10,... | collective-permute-start | bytes 1572872 | tf_op jit(solution)/shard_map/ppermute | solution.py:83
  530.1 23.6 %collective-permute-start.71 = (bf16[128,2048]{1,0:T(8,128)(2,1)}, bf16[128,2048]{1,0:T(8,128)(2,1)}, u32[]{:S(2)}, u32[]{:S(2)}) collective-permute-start(bf16[128,2048]{1,0:T(8,128)(2,1)} %add_convert_fusion.refs_0_), channel_id=1, source_target_pairs={{0,4},{1,5},{2,6},{3,7},{4,0},{5,1},{6,2},{7,3},{8,12},{9,13},{10,... | collective-permute-start | bytes 1572872 | tf_op jit(solution)/shard_map/ppermute | solution.py:83
  530.4 25.8 %collective-permute-start.72 = (bf16[128,2048]{1,0:T(8,128)(2,1)}, bf16[128,2048]{1,0:T(8,128)(2,1)}, u32[]{:S(2)}, u32[]{:S(2)}) collective-permute-start(bf16[128,2048]{1,0:T(8,128)(2,1)} %add_convert_fusion.refs_0_), channel_id=1, source_target_pairs={{0,6},{1,7},{2,4},{3,5},{4,2},{5,3},{6,0},{7,1},{8,14},{9,15},{10,... | collective-permute-start | bytes 1572872 | tf_op jit(solution)/shard_map/ppermute | solution.py:83
  533.0 23.2 %collective-permute-start.73 = (bf16[128,2048]{1,0:T(8,128)(2,1)}, bf16[128,2048]{1,0:T(8,128)(2,1)}, u32[]{:S(2)}, u32[]{:S(2)}) collective-permute-start(bf16[128,2048]{1,0:T(8,128)(2,1)} %add_convert_fusion.refs_0_), channel_id=1, source_target_pairs={{0,1},{1,0},{2,3},{3,2},{4,5},{5,4},{6,7},{7,6},{8,9},{9,8},{10,11... | collective-permute-start | bytes 1572872 | tf_op jit(solution)/shard_map/ppermute | solution.py:83
  537.3 34.0 %collective-permute-start.69 = (bf16[384,1024]{1,0:T(8,128)(2,1)}, bf16[384,1024]{1,0:T(8,128)(2,1)S(1)}, u32[]{:S(2)}, u32[]{:S(2)}) collective-permute-start(bf16[384,1024]{1,0:T(8,128)(2,1)} %reduce-scatter.8.cloned.1.call-done), channel_id=1, source_target_pairs={{1,4},{3,6},{4,1},{6,3},{9,12},{11,14},{12,9},{14,11},{17,20},{19,... | collective-permute-start | bytes 2359304 | tf_op jit(solution)/shard_map/ppermute | solution.py:83
  553.7 31.9 %collective-permute-start.74 = (bf16[128,2048]{1,0:T(8,128)(2,1)}, bf16[128,2048]{1,0:T(8,128)(2,1)S(1)}, u32[]{:S(2)}, u32[]{:S(2)}) collective-permute-start(bf16[128,2048]{1,0:T(8,128)(2,1)} %collective-permute-done.70.refs_1_), channel_id=1, source_target_pairs={{0,1},{1,0},{2,3},{3,2},{4,5},{5,4},{6,7},{7,6},{8,9},{9,8},{10,11... | collective-permute-start | bytes 1572872 | tf_op jit(solution)/shard_map/ppermute | solution.py:83
  556.2 29.4 %collective-permute-start.75 = (bf16[128,2048]{1,0:T(8,128)(2,1)}, bf16[128,2048]{1,0:T(8,128)(2,1)S(1)}, u32[]{:S(2)}, u32[]{:S(2)}) collective-permute-start(bf16[128,2048]{1,0:T(8,128)(2,1)} %collective-permute-done.71.refs_2_), channel_id=1, source_target_pairs={{0,1},{1,0},{2,3},{3,2},{4,5},{5,4},{6,7},{7,6},{8,9},{9,8},{10,11... | collective-permute-start | bytes 1572872 | tf_op jit(solution)/shard_map/ppermute | solution.py:83
  556.3 29.3 %collective-permute-start.76 = (bf16[128,2048]{1,0:T(8,128)(2,1)}, bf16[128,2048]{1,0:T(8,128)(2,1)S(1)}, u32[]{:S(2)}, u32[]{:S(2)}) collective-permute-start(bf16[128,2048]{1,0:T(8,128)(2,1)} %collective-permute-done.72.refs_3_), channel_id=1, source_target_pairs={{0,1},{1,0},{2,3},{3,2},{4,5},{5,4},{6,7},{7,6},{8,9},{9,8},{10,11... | collective-permute-start | bytes 1572872 | tf_op jit(solution)/shard_map/ppermute | solution.py:83
  (138 other events, 1777.0 us)
Sparse Core Ops, SparseCore 0:
  22.7 72.8 all-gather.3
  116.6 110.5 all-gather.5
  250.2 61.9 all-gather.7
  314.4 54.8 reduce-scatter.3
  373.9 100.4 reduce-scatter.5
  476.5 60.7 reduce-scatter.7

commit v3 on v2

--- a/solution.py
+++ b/solution.py
@@ -753,10 +753,12 @@
     mine = lax.dynamic_slice_in_dim(first_w, t * side, side, axis=1)
     attn_t = transpose(jnp.concatenate([up_q, out_w], axis=0), stays)
     tok_got = send(rows_at(tokens_in, t * part, part), OVER_X)
+    tok_y = send(tok_got, OVER_Y)
     first_own = stage(mine, send(mine, Z_ONE), send(mine, Z_TWO), send(mine, Z_THREE))
+    attn_own = gather_z(after(attn_t, *first_own))
     first_own = jnp.concatenate(first_own, axis=0)
+    pair_t = transpose(after(jnp.concatenate([gate_w, up_w], axis=0), first_own), stays)
     first_blocks = [first_own] + [send(first_own, p) for p in (OVER_Y, OVER_X, OVER_XY)]
-    first_blocks = first_blocks + over_core(first_blocks)
 
     def first_plan(n, ins, out):
         listed = []
@@ -768,7 +770,26 @@
                 listed.append((None, ins[i].at[k * 256 : (k + 1) * 256], out.at[row, col]))
         return listed
 
-    pair_t = transpose(after(jnp.concatenate([gate_w, up_w], axis=0), first_own, tok_got), stays)
+    pair_own = gather_z(after(pair_t, attn_own))
+    first_blocks = first_blocks + over_core(first_blocks)
+
+    def first_plan(n, ins, out):
+        listed = []
+        for i in range(8):
+            col = pl.ds(pl.multiple_of(n[at_t + (0, 2, 0, 2, 1, 3, 1, 3)[i]] * side, side), side)
+            for k in range(4):
+                place = n[at_x + (i % 4 // 2) * 4 + k]
+                row = pl.ds(pl.multiple_of(place * 256, 256), 256)
+                listed.append((None, ins[i].at[k * 256 : (k + 1) * 256], out.at[row, col]))
+        return listed
+
+    ffn_t = transpose(
+        after(jnp.concatenate([gate_w, up_w, down_w], axis=0), first_own), stays
+    )
+    tok_y = send(tok_got, OVER_Y)
+    *first_blocks, ffn_t, tok_got, tok_y = stage(*first_blocks[:4], ffn_t, tok_got, tok_y)
+    ffn_own = gather_z(ffn_t)
+    first_blocks = first_blocks + over_core(first_blocks)
     first_all = place_copies(first_plan, numbers, first_blocks, (depth, wide), BF)
 
     def rows_plan(n, ins, out):
@@ -785,14 +806,12 @@
                     listed.append((away & (n[at_t + j] == q), ins[1 + j], to))
         return listed
 
-    def group_rows(array, got):
-        got_y = send(got, OVER_Y)
+    def group_rows(array, got, got_y):
         buffers = [array, got, send(got, OVER_C), got_y, send(got_y, OVER_C)]
         return place_copies(rows_plan, numbers, buffers, (2 * rows, depth), BF)
 
-    tokens = group_rows(tokens_in, tok_got)
-
-    attn_own = gather_z(attn_t)
+    tokens = group_rows(tokens_in, tok_got, tok_y)
+
     attn_rows = attn_t.shape[0]
     upq_rows = up_q.shape[0]
     out_rows = out_w.shape[0]
@@ -809,8 +828,6 @@
 
         return plan
 
-
-    cot = group_rows(cotangent, send(rows_at(cotangent, t * part, part), OVER_X))
 
     places = (
         block_order[0][:, :, None] * half + jnp.arange(half, dtype=jnp.int32)[None, None, :]
@@ -833,10 +850,10 @@
     token_rows = tokens.astype(F32)
     plain_one, inverse_one = rms_parts(token_rows)
     normed = (plain_one * gain_one).astype(BF)
-    lat = dot(normed, first_all)
-    pair_own = gather_z(pair_t)
-    down_t = transpose(after(down_w, first_all), stays)
-    attn_own = after(attn_own, lat)
+    lat = dot(after(normed, attn_own), first_all)
+    down_t = transpose(after(down_w, lat), stays)
+    cot_got = send(after(rows_at(cotangent, t * part, part), lat), OVER_X)
+    cot_y = send(cot_got, OVER_Y)
     attns = [attn_own, send(attn_own, OVER_C)]
     up_q_all = place_copies(
         head_plan(0, upq_rows), numbers, attns, (latent_width, cols), BF
@@ -853,15 +870,17 @@
     query, attended, lse = attention_forward(
         query_pre, cosine, sine, keys, values, row_info, key_places
     )
+    down_t, cot_got, cot_y, attended = stage(down_t, cot_got, cot_y, attended)
+    cot = group_rows(cotangent, cot_got, cot_y)
     (give,) = product_pieces(attended, out_all, [], None, False)
     pieces = product_pieces(attended, out_all, [], send(give, OVER_C), True)
-    middle, cot = stage(tokens[:part].astype(F32) + sum_pieces(pieces), cot)
+    *pieces, cot, pair_own = stage(*trade(pieces), cot, pair_own)
+    middle = tokens[:part].astype(F32) + added(pieces)
+    down_own = gather_z(after(down_t, pair_own))
+    pairs = [pair_own, send(pair_own, OVER_C)]
 
     plain_two, inverse_two = rms_parts(middle)
     two_parts = spread((plain_two * gain_two).astype(BF))
-    *two_parts, pair_own, down_t = stage(*two_parts, pair_own, down_t)
-    down_own = gather_z(down_t)
-    pairs = [pair_own, send(pair_own, OVER_C)]
     hidden, slope, silu = ffn_forward(numbers, two_parts, pairs)
 
     def two(array, other):
@@ -872,7 +891,10 @@
     down_slabs = weight_grads(
         numbers, [([cot], 256, 0, [(None, two(hidden, hidden_other))])], width
     )
-    down_slabs, hidden, down_own = stage(down_slabs, hidden, down_own)
+    two_other = over_core(two_parts)
+    down_slabs, hidden, down_own, *two_other = stage(
+        down_slabs, hidden, down_own, *two_other
+    )
     down_sum = reduce_z(down_slabs)
     downs = [down_own, send(down_own, OVER_C)]
     grad_gate, grad_up, *pieces = ffn_backward(
@@ -880,7 +902,7 @@
     )
 
     gate_other, up_other = over_core([grad_gate, grad_up])
-    two_all = two_parts + over_core(two_parts)
+    two_all = list(two_parts) + list(two_other)
     pair_slabs = weight_grads(
         numbers,
         [
@@ -909,13 +931,35 @@
     grad_query_pre, key_acc, value_acc = attention_backward(
         query, grad_attended, lse, cosine, sine, keys, values, row_info, key_places
     )
-    staged = stage(*trade(out_pieces), grad_query_pre, key_acc, value_acc)
-    out_sum, (grad_query_pre, key_acc, value_acc) = staged[:4], staged[4:]
+    down_home = transpose(down_sum, stays)
+    grad_branch = place_copies(stack_plan, numbers, mid_parts, (2 * rows, depth), BF)
+    attended_other = send(after(attended, mid_parts[4]), OVER_C)
+    *out_sum, grad_query_pre, key_acc, value_acc, down_home, grad_branch, attended_other = stage(
+        *trade(out_pieces),
+        grad_query_pre,
+        key_acc,
+        value_acc,
+        down_home,
+        grad_branch,
+        attended_other,
+    )
+
+    out_part = (middle + added(out_sum)).astype(BF)
+    out_other = send(out_part, OVER_C)
+    out_mine = jnp.where(stays, out_part, out_other)
+    out_away = rows_at(jnp.where(stays, out_other, out_part), c * (part // 2), part // 2)
     extras = [key_acc, value_acc]
     (give,) = product_pieces(grad_query_pre, up_q_all, extras, None, False)
     pieces = product_pieces(grad_query_pre, up_q_all, extras, send(give, OVER_C), True)
-    attended_other, query_other = over_core([attended, grad_query_pre])
-    *pieces, attended_other, query_other = stage(*pieces, attended_other, query_other)
+    staged = stage(
+        *pieces,
+        out_mine,
+        send(rows_at(out_mine, c * (part // 2), part // 2), OVER_Y),
+        send(out_away, OVER_X),
+        send(out_away, OVER_XY),
+    )
+    pieces, out_parts = staged[:4], list(staged[4:])
+    query_other = send(grad_query_pre, OVER_C)
 
     def swapped(array):
         return [(array, rows, rows, None), (array, 0, rows, None)]
@@ -944,8 +988,7 @@
         ],
         2 * cols,
     )
-    out_part = (middle + added(out_sum)).astype(BF)
-    *pieces, attn_slabs, out_part = stage(*trade(pieces), attn_slabs, out_part)
+    *pieces, attn_slabs = stage(*trade(pieces), attn_slabs)
     three = added(pieces)
     attn_sum = reduce_z(after(attn_slabs, pair_sum))
 
@@ -962,11 +1005,8 @@
             [grad_latent, grad_key_pre, three[:, latent_width + HD :]], axis=1
         ).astype(BF)
     )
-    down_home = transpose(down_sum, stays)
-    grad_branch = place_copies(stack_plan, numbers, mid_parts, (2 * rows, depth), BF)
+    *lat_parts, pair_sum = stage(*lat_parts, pair_sum)
     pair_home = transpose(pair_sum, stays)
-    staged = stage(*lat_parts, down_home, pair_home, grad_branch, out_part)
-    lat_parts, (down_home, pair_home, grad_branch, out_part) = list(staged[:4]), staged[4:]
     lat_parts = lat_parts + over_core(lat_parts)
 
     lane = wide // 4
@@ -975,24 +1015,30 @@
         [([normed], 256, at_x, [(None, [(p, 0, part, at_t) for p in lat_parts])])],
         lane,
     )
-    out_parts = spread(out_part)
-    out_parts = out_parts + over_core(out_parts)
+    first_slabs, pair_home, *lat_parts = stage(first_slabs, pair_home, *lat_parts)
     grad_lat = place_copies(stack_plan, numbers, lat_parts, (2 * rows, wide), BF)
     grad_tokens = input_gradient(numbers, grad_lat, first_all, grad_branch, tokens, gain_one)
+
+    out_parts = out_parts + over_core(out_parts[1:])
 
     def out_plan(n, ins, out):
         listed = []
         for f in range(4):
-            to = out.at[pl.ds(pl.multiple_of(n[at_quarter + f] * part, part), part)]
-            listed.append((n[at_same] == 0, ins[f], to))
-            listed.append((n[at_same] == 1, ins[4 + f], to))
+            row = n[at_quarter + f] * part
+            if f == 0:
+                to = out.at[pl.ds(pl.multiple_of(row, part), part)]
+                listed.append((None, ins[0], to))
+                continue
+            for j in range(2):
+                at = pl.multiple_of(row + n[at_c + j] * (part // 2), part // 2)
+                listed.append((None, ins[f + 3 * j], out.at[pl.ds(at, part // 2)]))
         return listed
 
-    attn_home = transpose(attn_sum, stays)
-    staged = stage(*trade_z(first_slabs), grad_tokens, attn_home, *out_parts)
-    first_quarter = added(staged[:4]).astype(BF)
-    grad_tokens, attn_home, *out_parts = staged[4:]
+    *first_got, grad_tokens = stage(*trade_z(first_slabs), grad_tokens)
+    first_quarter = added(first_got).astype(BF)
     quarters = [first_quarter] + [send(first_quarter, p) for p in (OVER_C, OVER_Y, OVER_YC)]
+    quarters = stage(*quarters)
+    attn_home = transpose(after(attn_sum, *quarters), stays)
     dev = z * 2 + x
     block = depth // 8
     own_one = lax.dynamic_slice_in_dim(gain_one, dev * block, block)

time: 624 us -> 578 us (0.926)
  waiting for transfers between devices: 253 us -> 200 us
  starting transfers between devices: 79.6 us -> 88.7 us
    all_gather x3, waiting for transfers between devices: 22.9 us -> 0.02 us  [gather_z(): return lax.all_gather(array, 'dp', axis=0, tiled=True)]
    ppermute x83, waiting for transfers between devices: 218 us -> 199 us  [send(): return lax.ppermute(array, AXES, pairs)]
    reduce_scatter x3, waiting for transfers between devices: 12.1 us -> 0.88 us  [reduce_z(): return lax.psum_scatter(slabs, 'dp', scatter_dimension=0, tiled=True)]
    ppermute x83, starting transfers between devices: 78.3 us -> 88 us  [send(): return lax.ppermute(array, AXES, pairs)]
    unnamed x166 -> x156, local copies, waits for them, and re-layouts: 17 us -> 22 us
  transfers between devices with their start and end apart: 89 -> 89, of which waited for: 32 -> 33; matrix products, arithmetic and copies ran while one was open for 11% -> 10% of each run, Pallas kernels for 29% -> 33%
where the time goes in v3:
time: 578 us; the launch traced here: 570 us
  waiting for transfers between devices  200 us (35%)
  Pallas kernels  188 us (33%)
  starting transfers between devices  88.7 us (15%)
  other arithmetic  33.1 us (6%)
  local copies, waits for them, and re-layouts  33 us (6%)
  between operations  15.5 us (3%)
  matrix products  12.5 us (2%)
    ppermute x83, waiting for transfers between devices, send(): return lax.ppermute(array, AXES, pairs)  199 us
    ppermute x83, starting transfers between devices, send(): return lax.ppermute(array, AXES, pairs)  88 us
    pallas_call x8, Pallas kernels, place_copies(): pl.pallas_call(body, grid_spec=pltpu.PrefetchScalarGridSpec(num_scalar_pr...  40.1 us
    pallas_call x4, Pallas kernels, weight_grads(): pl.pallas_call(body, grid_spec=pltpu.PrefetchScalarGridSpec(num_scalar_pr...  36.5 us
    unnamed x156, local copies, waits for them, and re-layouts  22 us
    pallas_call x1, Pallas kernels, ffn_backward(): pl.pallas_call(body, grid_spec=pltpu.PrefetchScalarGridSpec(num_scalar_pr...  20.4 us
    pallas_call x4, Pallas kernels, product_pieces(): pl.pallas_call(body, in_specs=[WHOLE] * len(arrays), out_specs=[WHOLE] *...  18.3 us
    pallas_call x1, Pallas kernels, ffn_forward(): pl.pallas_call(body, grid_spec=pltpu.PrefetchScalarGridSpec(num_scalar_pr...  17.6 us
  transfers between devices with their start and end apart: 89, of which 33 were waited for; matrix products, arithmetic and copies ran while one was open for 10% of the time, Pallas kernels for 33%

profile of v3, /device:TPU:0, one launch (start us, length us, event | category | flops | bytes accessed | tf_op | source)
XLA Modules:
  0.0 570.5 jit_solution(3340565981491392638)
XLA Ops:
  13.9 5.1 collective-permute-start.2
  23.7 12.5 %collective-permute-done.1 = bf16[256,384]{1,0:T(8,128)(2,1)S(1)} collective-permute-done((bf16[256,384]{1,0:T(8,128)(2,1)S(1)}, bf16[256,384]{1,0:T(8,128)(2,1)S(1)}, u32[]{:S(2)}, u32[]{:S(2)}) %collective-permute-start.1) | collective-permute-done | bytes 196640 | tf_op jit(solution)/shard_map/ppermute | solution.py:83
  57.3 39.0 %collective-permute-done.5.refs_3_ = bf16[1024,384]{1,0:T(8,128)(2,1)} collective-permute-done((bf16[1024,384]{1,0:T(8,128)(2,1)}, bf16[1024,384]{1,0:T(8,128)(2,1)}, u32[]{:S(2)}, u32[]{:S(2)}) %collective-permute-start.5) | collective-permute-done | bytes 786464 | tf_op jit(solution)/shard_map/ppermute | solution.py:83
  96.3 7.4 %collective-permute-done.4.refs_2_ = bf16[1024,384]{1,0:T(8,128)(2,1)} collective-permute-done((bf16[1024,384]{1,0:T(8,128)(2,1)}, bf16[1024,384]{1,0:T(8,128)(2,1)}, u32[]{:S(2)}, u32[]{:S(2)}) %collective-permute-start.4) | collective-permute-done | bytes 786464 | tf_op jit(solution)/shard_map/ppermute | solution.py:83
  107.7 5.2 shard_map.246.tok_ref
  118.8 9.1 %shard_map.247.first_ref = bf16[2048,1536]{1,0:T(8,128)(2,1)} custom-call(s32[29]{0:T(128)} %concatenate.27.numbers_ref, bf16[1024,384]{1,0:T(8,128)(2,1)} %constant_dynamic-update-slice_fusion.3.refs_0_, bf16[1024,384]{1,0:T(8,128)(2,1)} %collective-permute-done.3.refs_1_, bf16[1024,384]{1,0:T(8,128)(2,1)} %collective-permute-done.4.refs_2_, ...), custom_call_target="tpu_custom_call" | custom-call | bytes 12582912 | tf_op jit(solution)/shard_map/pallas_call | solution.py:145
  128.3 8.7 %fusion.17 = f32[1024,1536]{1,0:T(8,128)S(1)} fusion(bf16[1024,2048]{1,0:T(8,128)(2,1)S(1)} %fusion.2.refs_0_, bf16[2048,1536]{1,0:T(8,128)(2,1)} %shard_map.247.first_ref), kind=kOutput, calls=%fused_computation.97 | convolution fusion | flops 6442450944 | bytes 16777216 | tf_op jit(solution)/shard_map/dot_general | solution.py:19
  161.0 8.4 %shard_map.249 = (bf16[1024,512]{1,0:T(8,128)(2,1)}, bf16[1024,512]{1,0:T(8,128)(2,1)}, f32[2,1024,1]{2,1,0:T(8,128)}) custom-call(f32[1024,512]{1,0:T(8,128)} %fusion.18.pre_ref, f32[1024,128]{1,0:T(8,128)} %get-tuple-element.293.cos_ref, f32[1024,128]{1,0:T(8,128)} %get-tuple-element.292.sin_ref, bf16[1024,256]{1,0:T(8,128)(2,1)} %pad_maximum_fusion.1.k_ref, ...), custom_call_target="tpu_custom_call" | custom-call | flops 4294967296 | bytes 3145728 | tf_op jit(solution)/shard_map/pallas_call | solution.py:186
  177.8 6.4 %collective-permute-start.19 = (bf16[512,2048]{1,0:T(8,128)(2,1)}, bf16[512,2048]{1,0:T(8,128)(2,1)S(1)}, u32[]{:S(2)}, u32[]{:S(2)}) collective-permute-start(bf16[512,2048]{1,0:T(8,128)(2,1)} %shard_map.251), channel_id=1, source_target_pairs={{0,1},{1,0},{2,3},{3,2},{4,5},{5,4},{6,7},{7,6},{8,9},{9,8},{10,11... | collective-permute-start | bytes 6291464 | tf_op jit(solution)/shard_map/ppermute | solution.py:83
  199.7 5.1 shard_map.253.refs_0_
  211.1 10.3 %collective-permute-done.22 = bf16[128,2048]{1,0:T(8,128)(2,1)S(1)} collective-permute-done((bf16[128,2048]{1,0:T(8,128)(2,1)}, bf16[128,2048]{1,0:T(8,128)(2,1)S(1)}, u32[]{:S(2)}, u32[]{:S(2)}) %collective-permute-start.22) | collective-permute-done | bytes 524320 | tf_op jit(solution)/shard_map/ppermute | solution.py:83
  227.2 12.2 %collective-permute-done.28.refs_3_.refs_11_ = bf16[128,2048]{1,0:T(8,128)(2,1)S(1)} collective-permute-done((bf16[128,2048]{1,0:T(8,128)(2,1)S(1)}, bf16[128,2048]{1,0:T(8,128)(2,1)S(1)}, u32[]{:S(2)}, u32[]{:S(2)}) %collective-permute-start.28) | collective-permute-done | bytes 524320 | tf_op jit(solution)/shard_map/ppermute | solution.py:83
  239.4 10.9 %collective-permute-done.27.refs_2_.refs_10_ = bf16[128,2048]{1,0:T(8,128)(2,1)S(1)} collective-permute-done((bf16[128,2048]{1,0:T(8,128)(2,1)S(1)}, bf16[128,2048]{1,0:T(8,128)(2,1)S(1)}, u32[]{:S(2)}, u32[]{:S(2)}) %collective-permute-start.27) | collective-permute-done | bytes 524320 | tf_op jit(solution)/shard_map/ppermute | solution.py:83
  251.2 17.6 %shard_map.254 = (bf16[512,1408]{1,0:T(8,128)(2,1)}, f32[512,1408]{1,0:T(8,128)}, f32[512,1408]{1,0:T(8,128)}) custom-call(s32[29]{0:T(128)} %concatenate.27.numbers_ref, bf16[128,2048]{1,0:T(8,128)(2,1)} %copy-done.7, bf16[128,2048]{1,0:T(8,128)(2,1)} %copy-done.27, bf16[128,2048]{1,0:T(8,128)(2,1)} %copy-done.26, bf16[128,2048]{1,0:T(8,128)(2,1)} %copy-done.25, ...), custom_call_target="tpu_custom_call" | custom-call | flops 5905580032 | bytes 11534336 | tf_op jit(solution)/shard_map/pallas_call | solution.py:392
  273.4 7.9 %shard_map.255 = bf16[1024,1408]{1,0:T(8,128)(2,1)} custom-call(s32[29]{0:T(128)} %concatenate.27.numbers_ref, bf16[1024,2048]{1,0:T(8,128)(2,1)} %shard_map.253.refs_0_, bf16[512,1408]{1,0:T(8,128)(2,1)} %get-tuple-element.197.refs_1_.hid_ref, bf16[512,1408]{1,0:T(8,128)(2,1)} %copy-done.41), custom_call_target="tpu_custom_call" | custom-call | flops 738197504 | bytes 1441792 | tf_op jit(solution)/shard_map/pallas_call | solution.py:592
  281.7 5.4 collective-permute-done.35.refs_6_.refs_1_
  288.7 20.4 %shard_map.256 = (bf16[512,1408]{1,0:T(8,128)(2,1)}, bf16[512,1408]{1,0:T(8,128)(2,1)}, bf16[128,2048]{1,0:T(8,128)(2,1)}, bf16[128,2048]{1,0:T(8,128)(2,1)}, bf...) custom-call(s32[29]{0:T(128)} %concatenate.27.numbers_ref, bf16[1024,2048]{1,0:T(8,128)(2,1)} %shard_map.253.refs_0_, ...), custom_call_target="tpu_custom_call" | custom-call | flops 8858370048 | bytes 17301504 | tf_op jit(solution)/shard_map/pallas_call | solution.py:470
  315.8 13.3 %shard_map.257 = bf16[2048,1408]{1,0:T(8,128)(2,1)} custom-call(s32[29]{0:T(128)} %concatenate.27.numbers_ref, bf16[128,2048]{1,0:T(8,128)(2,1)} %copy-done.7, bf16[128,2048]{1,0:T(8,128)(2,1)} %copy-done.27, bf16[128,2048]{1,0:T(8,128)(2,1)} %copy-done.26, bf16[128,2048]{1,0:T(8,128)(2,1)} %copy-done.25, bf16[128,2048]{1,0:T(8,128)(2,1)} %copy-done.28, ...), custom_call_target="tpu_custom_call" | custom-call | flops 1476395008 | bytes 2883584 | tf_op jit(solution)/shard_map/pallas_call | solution.py:592
  329.1 7.2 %collective-permute-done.38 = bf16[128,2048]{1,0:T(8,128)(2,1)S(1)} collective-permute-done((bf16[128,2048]{1,0:T(8,128)(2,1)}, bf16[128,2048]{1,0:T(8,128)(2,1)S(1)}, u32[]{:S(2)}, u32[]{:S(2)}) %collective-permute-start.38) | collective-permute-done | bytes 524320 | tf_op jit(solution)/shard_map/ppermute | solution.py:83
  343.0 11.4 %shard_map.258 = (bf16[128,2048]{1,0:T(8,128)(2,1)}, bf16[128,2048]{1,0:T(8,128)(2,1)}, bf16[128,2048]{1,0:T(8,128)(2,1)}, bf16[128,2048]{1,0:T(8,128)(2,1)}) custom-call(s32[29]{0:T(128)} %concatenate.27.numbers_ref, bf16[512,1408]{1,0:T(8,128)(2,1)} %get-tuple-element.197.refs_1_.hid_ref, bf16[1024,1408]{1,0:T(8,128)(2,1)} %all-gather.8.cloned.1.call-done.refs_5_.refs_0_, ...), custom_call_target="tpu_custom_call" | custom-call | flops 738197504 | bytes 1441792 | tf_op jit(solution)/shard_map/pallas_call | solution.py:523
  355.3 9.8 %collective-permute-done.42.refs_2_.refs_3_ = bf16[128,2048]{1,0:T(8,128)(2,1)S(1)} collective-permute-done((bf16[128,2048]{1,0:T(8,128)(2,1)S(1)}, bf16[128,2048]{1,0:T(8,128)(2,1)S(1)}, u32[]{:S(2)}, u32[]{:S(2)}) %collective-permute-start.42) | collective-permute-done | bytes 524320 | tf_op jit(solution)/shard_map/ppermute | solution.py:83
  371.7 5.1 shard_map.261.mid_ref
  376.9 6.2 %shard_map.259.do_ref = bf16[1024,512]{1,0:T(8,128)(2,1)} custom-call(bf16[128,2048]{1,0:T(8,128)(2,1)} %copy-done.6, bf16[128,2048]{1,0:T(8,128)(2,1)} %copy-done.20, bf16[128,2048]{1,0:T(8,128)(2,1)} %copy-done.19, bf16[128,2048]{1,0:T(8,128)(2,1)} %copy-done.18, bf16[128,2048]{1,0:T(8,128)(2,1)} %copy-done.21, bf16[128,2048]{1,0:T(8,128)(2,1)} %copy-done.22, ...), custom_call_target="tpu_custom_call" | custom-call | flops 2147483648 | bytes 2097152 | tf_op jit(solution)/shard_map/pallas_call | solution.py:288
  384.0 13.0 %shard_map.260 = (bf16[1024,512]{1,0:T(8,128)(2,1)}, f32[1024,256]{1,0:T(8,128)}, f32[1024,256]{1,0:T(8,128)}) custom-call(bf16[1024,512]{1,0:T(8,128)(2,1)} %get-tuple-element.206.q_ref, bf16[1024,512]{1,0:T(8,128)(2,1)} %shard_map.259.do_ref, f32[2,1024,1]{2,1,0:T(8,128)} %get-tuple-element.211.lse_ref, f32[1024,128]{1,0:T(8,128)} %get-tuple-element.293.cos_ref, ...), custom_call_target="tpu_custom_call" | custom-call | flops 8589934592 | bytes 3145728 | tf_op jit(solution)/shard_map/pallas_call | solution.py:248
  428.0 9.6 %shard_map.265 = bf16[1536,1024]{1,0:T(8,128)(2,1)} custom-call(s32[29]{0:T(128)} %concatenate.27.numbers_ref, bf16[1024,1024]{1,0:T(8,128)(2,1)} %get-tuple-element.282.refs_0_, bf16[128,2048]{1,0:T(8,128)(2,1)} %copy-done.6, bf16[128,2048]{1,0:T(8,128)(2,1)} %copy-done.20, bf16[128,2048]{1,0:T(8,128)(2,1)} %copy-done.19, bf16[128,2048]{1,0:T(8,128)(2,1)} %copy-done.18, ...), custom_call_target="tpu_custom_call" | custom-call | flops 805306368 | bytes 1572864 | tf_op jit(solution)/shard_map/pallas_call | solution.py:592
  437.7 6.1 %collective-permute-done.63 = bf16[128,1536]{1,0:T(8,128)(2,1)S(1)} collective-permute-done((bf16[128,1536]{1,0:T(8,128)(2,1)}, bf16[128,1536]{1,0:T(8,128)(2,1)S(1)}, u32[]{:S(2)}, u32[]{:S(2)}) %collective-permute-start.63) | collective-permute-done | bytes 393248 | tf_op jit(solution)/shard_map/ppermute | solution.py:83
  451.1 9.5 %collective-permute-done.67.refs_4_.refs_3_ = bf16[128,1536]{1,0:T(8,128)(2,1)S(1)} collective-permute-done((bf16[128,1536]{1,0:T(8,128)(2,1)S(1)}, bf16[128,1536]{1,0:T(8,128)(2,1)S(1)}, u32[]{:S(2)}, u32[]{:S(2)}) %collective-permute-start.67) | collective-permute-done | bytes 393248 | tf_op jit(solution)/shard_map/ppermute | solution.py:83
  460.6 5.3 collective-permute-done.66.refs_3_.refs_2_
  474.2 5.7 shard_map.266
  490.2 12.0 %shard_map.268 = f32[512,2048]{1,0:T(8,128)} custom-call(s32[29]{0:T(128)} %concatenate.27.numbers_ref, bf16[1024,1536]{1,0:T(8,128)(2,1)} %shard_map.267.lat_ref, bf16[2048,1536]{1,0:T(8,128)(2,1)} %shard_map.247.first_ref, bf16[1024,2048]{1,0:T(8,128)(2,1)} %shard_map.261.mid_ref, bf16[1024,2048]{1,0:T(8,128)(2,1)} %shard_map.246.tok_ref, f32[1,2048]{1,0:T(1,128)} %bitcast.57), custom_call_target="tpu_custom_call" | custom-call | flops 3221225472 | bytes 14680064 | tf_op jit(solution)/shard_map/pallas_call | solution.py:627
  502.2 17.0 %collective-permute-done.74 = bf16[256,384]{1,0:T(8,128)(2,1)S(1)} collective-permute-done((bf16[256,384]{1,0:T(8,128)(2,1)S(1)}, bf16[256,384]{1,0:T(8,128)(2,1)S(1)}, u32[]{:S(2)}, u32[]{:S(2)}) %collective-permute-start.74) | collective-permute-done | bytes 196640 | tf_op jit(solution)/shard_map/ppermute | solution.py:83
  541.8 6.7 %collective-permute-start.82 = (f32[3,128]{1,0:T(4,128)S(1)}, f32[3,128]{1,0:T(4,128)S(1)}, u32[]{:S(2)}, u32[]{:S(2)}) collective-permute-start(f32[3,128]{1,0:T(4,128)S(1)} %maximum_bitcast_fusion), channel_id=1, source_target_pairs={{0,3},{1,2},{2,1},{3,0},{4,7},{5,6},{6,5},{7,4},{8,11},{9,10},{10,... | collective-permute-start | bytes 4616 | tf_op jit(solution)/shard_map/ppermute | solution.py:83
  (405 shorter events, 225.4 us)
Async XLA Ops:
  7.2 107.0 %all-gather.4.cloned.1.call-start = ((), (), s32[]{:S(2)}) async-start(), calls=%async_computation.3 | async-start | bytes 3932160 | tf_op jit(solution)/shard_map/all_gather | solution.py:99
  9.3 26.9 %collective-permute-start.10 = (bf16[384,1024]{1,0:T(8,128)(2,1)S(1)}, bf16[384,1024]{1,0:T(8,128)(2,1)}, u32[]{:S(2)}, u32[]{:S(2)}) collective-permute-start(bf16[384,1024]{1,0:T(8,128)(2,1)S(1)} %constant_dynamic-update-slice_fusion.7), channel_id=1, source_target_pairs={{1,4},{3,6},{4,1},{6,3},{9,12},{11,14},{12,9},{14,11},{17,20},{19,... | collective-permute-start | bytes 2359304 | tf_op jit(solution)/shard_map/ppermute | solution.py:83
  37.2 184.2 %all-gather.6.cloned.1.call-start = ((), (), s32[]{:S(2)}) async-start(), calls=%async_computation.4 | async-start | bytes 7208960 | tf_op jit(solution)/shard_map/all_gather | solution.py:99
  44.6 68.3 %collective-permute-start.25 = (bf16[512,1408]{1,0:T(8,128)(2,1)S(1)}, bf16[512,1408]{1,0:T(8,128)(2,1)S(1)}, u32[]{:S(2)}, u32[]{:S(2)}) collective-permute-start(bf16[512,1408]{1,0:T(8,128)(2,1)S(1)} %pad_maximum_fusion), channel_id=1, source_target_pairs={{1,4},{3,6},{4,1},{6,3},{9,12},{11,14},{12,9},{14,11},{17,20},{19,... | collective-permute-start | bytes 4325384 | tf_op jit(solution)/shard_map/ppermute | solution.py:83
  45.5 50.8 %collective-permute-start.5 = (bf16[1024,384]{1,0:T(8,128)(2,1)}, bf16[1024,384]{1,0:T(8,128)(2,1)}, u32[]{:S(2)}, u32[]{:S(2)}) collective-permute-start(bf16[1024,384]{1,0:T(8,128)(2,1)} %constant_dynamic-update-slice_fusion.3.refs_0_), channel_id=1, source_target_pairs={{0,6},{1,7},{2,4},{3,5},{4,2},{5,3},{6,0},{7,1},{8,14},{9,15},{10,... | collective-permute-start | bytes 2359304 | tf_op jit(solution)/shard_map/ppermute | solution.py:83
  48.7 55.0 %collective-permute-start.4 = (bf16[1024,384]{1,0:T(8,128)(2,1)}, bf16[1024,384]{1,0:T(8,128)(2,1)}, u32[]{:S(2)}, u32[]{:S(2)}) collective-permute-start(bf16[1024,384]{1,0:T(8,128)(2,1)} %constant_dynamic-update-slice_fusion.3.refs_0_), channel_id=1, source_target_pairs={{0,4},{1,5},{2,6},{3,7},{4,0},{5,1},{6,2},{7,3},{8,12},{9,13},{10,... | collective-permute-start | bytes 2359304 | tf_op jit(solution)/shard_map/ppermute | solution.py:83
  48.7 55.0 %collective-permute-start.3 = (bf16[1024,384]{1,0:T(8,128)(2,1)}, bf16[1024,384]{1,0:T(8,128)(2,1)}, u32[]{:S(2)}, u32[]{:S(2)}) collective-permute-start(bf16[1024,384]{1,0:T(8,128)(2,1)} %constant_dynamic-update-slice_fusion.3.refs_0_), channel_id=1, source_target_pairs={{0,2},{1,3},{2,0},{3,1},{4,6},{5,7},{6,4},{7,5},{8,10},{9,11},{10,... | collective-permute-start | bytes 2359304 | tf_op jit(solution)/shard_map/ppermute | solution.py:83
  54.1 49.6 %collective-permute-start.7 = (bf16[128,2048]{1,0:T(8,128)(2,1)}, bf16[128,2048]{1,0:T(8,128)(2,1)S(1)}, u32[]{:S(2)}, u32[]{:S(2)}) collective-permute-start(bf16[128,2048]{1,0:T(8,128)(2,1)} %collective-permute-done.6.refs_1_), channel_id=1, source_target_pairs={{0,2},{1,3},{2,0},{3,1},{4,6},{5,7},{6,4},{7,5},{8,10},{9,11},{10,... | collective-permute-start | bytes 1572872 | tf_op jit(solution)/shard_map/ppermute | solution.py:83
  114.2 167.3 %all-gather.8.cloned.1.call-start = ((), (), s32[]{:S(2)}) async-start(), calls=%async_computation.5 | async-start | bytes 3604480 | tf_op jit(solution)/shard_map/all_gather | solution.py:99
  127.9 25.9 %collective-permute-start.18 = (bf16[1536,1024]{1,0:T(8,128)(2,1)S(1)}, bf16[1536,1024]{1,0:T(8,128)(2,1)}, u32[]{:S(2)}, u32[]{:S(2)}) collective-permute-start(bf16[1536,1024]{1,0:T(8,128)(2,1)S(1)} %copy-done.2), channel_id=1, source_target_pairs={{0,1},{1,0},{2,3},{3,2},{4,5},{5,4},{6,7},{7,6},{8,9},{9,8},{10,11... | collective-permute-start | bytes 9437192 | tf_op jit(solution)/shard_map/ppermute | solution.py:83
  196.6 24.8 %collective-permute-start.22 = (bf16[128,2048]{1,0:T(8,128)(2,1)}, bf16[128,2048]{1,0:T(8,128)(2,1)S(1)}, u32[]{:S(2)}, u32[]{:S(2)}) collective-permute-start(bf16[128,2048]{1,0:T(8,128)(2,1)} %get-tuple-element.163), channel_id=1, source_target_pairs={{0,6},{1,7},{2,4},{3,5},{4,2},{5,3},{6,0},{7,1},{8,14},{9,15},{10,... | collective-permute-start | bytes 1572872 | tf_op jit(solution)/shard_map/ppermute | solution.py:83
  221.4 28.8 %collective-permute-start.29 = (bf16[2048,1408]{1,0:T(8,128)(2,1)}, bf16[2048,1408]{1,0:T(8,128)(2,1)}, u32[]{:S(2)}, u32[]{:S(2)}) collective-permute-start(bf16[2048,1408]{1,0:T(8,128)(2,1)} %all-gather.6.cloned.1.call-done.refs_4_.refs_3_), channel_id=1, source_target_pairs={{0,1},{1,0},{2,3},{3,2},{4,5},{5,4},{6,7},{7,6},{8,9},{9,8},{10,11... | collective-permute-start | bytes 17301512 | tf_op jit(solution)/shard_map/ppermute | solution.py:83
  221.5 115.7 %reduce-scatter.4.cloned.1.call-start = ((), (), s32[]{:S(2)}) async-start(), calls=%async_computation.6 | async-start | bytes 3604480 | tf_op jit(solution)/shard_map/reduce_scatter | solution.py:103
  225.0 25.3 %collective-permute-start.27 = (bf16[128,2048]{1,0:T(8,128)(2,1)S(1)}, bf16[128,2048]{1,0:T(8,128)(2,1)S(1)}, u32[]{:S(2)}, u32[]{:S(2)}) collective-permute-start(bf16[128,2048]{1,0:T(8,128)(2,1)S(1)} %multiply_convert_fusion.1.refs_0_.refs_8_), channel_id=1, source_target_pairs={{0,4},{1,5},{2,6},{3,7},{4,0},{5,1},{6,2},{7,3},{8,12},{9,13},{10,... | collective-permute-start | bytes 1572872 | tf_op jit(solution)/shard_map/ppermute | solution.py:83
  226.7 23.6 %collective-permute-start.26 = (bf16[128,2048]{1,0:T(8,128)(2,1)S(1)}, bf16[128,2048]{1,0:T(8,128)(2,1)S(1)}, u32[]{:S(2)}, u32[]{:S(2)}) collective-permute-start(bf16[128,2048]{1,0:T(8,128)(2,1)S(1)} %multiply_convert_fusion.1.refs_0_.refs_8_), channel_id=1, source_target_pairs={{0,2},{1,3},{2,0},{3,1},{4,6},{5,7},{6,4},{7,5},{8,10},{9,11},{10,... | collective-permute-start | bytes 1572872 | tf_op jit(solution)/shard_map/ppermute | solution.py:83
  281.5 162.3 %reduce-scatter.6.cloned.1.call-start = ((), (), s32[]{:S(2)}) async-start(), calls=%async_computation.7 | async-start | bytes 7208960 | tf_op jit(solution)/shard_map/reduce_scatter | solution.py:103
  309.7 19.4 %collective-permute-start.36 = (bf16[128,2048]{1,0:T(8,128)(2,1)}, bf16[128,2048]{1,0:T(8,128)(2,1)S(1)}, u32[]{:S(2)}, u32[]{:S(2)}) collective-permute-start(bf16[128,2048]{1,0:T(8,128)(2,1)} %get-tuple-element.183), channel_id=1, source_target_pairs={{0,2},{1,3},{2,0},{3,1},{4,6},{5,7},{6,4},{7,5},{8,10},{9,11},{10,... | collective-permute-start | bytes 1572872 | tf_op jit(solution)/shard_map/ppermute | solution.py:83
  310.9 18.2 %collective-permute-start.37 = (bf16[128,2048]{1,0:T(8,128)(2,1)}, bf16[128,2048]{1,0:T(8,128)(2,1)S(1)}, u32[]{:S(2)}, u32[]{:S(2)}) collective-permute-start(bf16[128,2048]{1,0:T(8,128)(2,1)} %get-tuple-element.184), channel_id=1, source_target_pairs={{0,4},{1,5},{2,6},{3,7},{4,0},{5,1},{6,2},{7,3},{8,12},{9,13},{10,... | collective-permute-start | bytes 1572872 | tf_op jit(solution)/shard_map/ppermute | solution.py:83
  311.2 25.1 %collective-permute-start.38 = (bf16[128,2048]{1,0:T(8,128)(2,1)}, bf16[128,2048]{1,0:T(8,128)(2,1)S(1)}, u32[]{:S(2)}, u32[]{:S(2)}) collective-permute-start(bf16[128,2048]{1,0:T(8,128)(2,1)} %get-tuple-element.185), channel_id=1, source_target_pairs={{0,6},{1,7},{2,4},{3,5},{4,2},{5,3},{6,0},{7,1},{8,14},{9,15},{10,... | collective-permute-start | bytes 1572872 | tf_op jit(solution)/shard_map/ppermute | solution.py:83
  337.2 194.7 %reduce-scatter.8.cloned.1.call-start = ((), (), s32[]{:S(2)}) async-start(), calls=%async_computation.8 | async-start | bytes 3932160 | tf_op jit(solution)/shard_map/reduce_scatter | solution.py:103
  341.8 23.3 %collective-permute-start.42 = (bf16[128,2048]{1,0:T(8,128)(2,1)S(1)}, bf16[128,2048]{1,0:T(8,128)(2,1)S(1)}, u32[]{:S(2)}, u32[]{:S(2)}) collective-permute-start(bf16[128,2048]{1,0:T(8,128)(2,1)S(1)} %add_convert_fusion.1.refs_0_.refs_1_), channel_id=1, source_target_pairs={{0,4},{1,5},{2,6},{3,7},{4,0},{5,1},{6,2},{7,3},{8,12},{9,13},{10,... | collective-permute-start | bytes 1572872 | tf_op jit(solution)/shard_map/ppermute | solution.py:83
  342.4 22.8 %collective-permute-start.41 = (bf16[128,2048]{1,0:T(8,128)(2,1)S(1)}, bf16[128,2048]{1,0:T(8,128)(2,1)S(1)}, u32[]{:S(2)}, u32[]{:S(2)}) collective-permute-start(bf16[128,2048]{1,0:T(8,128)(2,1)S(1)} %add_convert_fusion.1.refs_0_.refs_1_), channel_id=1, source_target_pairs={{0,2},{1,3},{2,0},{3,1},{4,6},{5,7},{6,4},{7,5},{8,10},{9,11},{10,... | collective-permute-start | bytes 1572872 | tf_op jit(solution)/shard_map/ppermute | solution.py:83
  366.2 30.9 %collective-permute-start.44 = (bf16[128,2048]{1,0:T(8,128)(2,1)}, bf16[128,2048]{1,0:T(8,128)(2,1)S(1)}, u32[]{:S(2)}, u32[]{:S(2)}) collective-permute-start(bf16[128,2048]{1,0:T(8,128)(2,1)} %get-tuple-element.203), channel_id=1, source_target_pairs={{0,2},{1,3},{2,0},{3,1},{4,6},{5,7},{6,4},{7,5},{8,10},{9,11},{10,... | collective-permute-start | bytes 1572872 | tf_op jit(solution)/shard_map/ppermute | solution.py:83
  367.6 29.6 %collective-permute-start.45 = (bf16[128,2048]{1,0:T(8,128)(2,1)}, bf16[128,2048]{1,0:T(8,128)(2,1)}, u32[]{:S(2)}, u32[]{:S(2)}) collective-permute-start(bf16[128,2048]{1,0:T(8,128)(2,1)} %get-tuple-element.204), channel_id=1, source_target_pairs={{0,4},{1,5},{2,6},{3,7},{4,0},{5,1},{6,2},{7,3},{8,12},{9,13},{10,... | collective-permute-start | bytes 1572872 | tf_op jit(solution)/shard_map/ppermute | solution.py:83
  369.0 28.1 %collective-permute-start.46 = (bf16[128,2048]{1,0:T(8,128)(2,1)}, bf16[128,2048]{1,0:T(8,128)(2,1)}, u32[]{:S(2)}, u32[]{:S(2)}) collective-permute-start(bf16[128,2048]{1,0:T(8,128)(2,1)} %get-tuple-element.205), channel_id=1, source_target_pairs={{0,6},{1,7},{2,4},{3,5},{4,2},{5,3},{6,0},{7,1},{8,14},{9,15},{10,... | collective-permute-start | bytes 1572872 | tf_op jit(solution)/shard_map/ppermute | solution.py:83
  370.1 27.1 %collective-permute-start.52 = (bf16[1024,512]{1,0:T(8,128)(2,1)S(1)}, bf16[1024,512]{1,0:T(8,128)(2,1)S(1)}, u32[]{:S(2)}, u32[]{:S(2)}) collective-permute-start(bf16[1024,512]{1,0:T(8,128)(2,1)S(1)} %copy-done.3), channel_id=1, source_target_pairs={{0,1},{1,0},{2,3},{3,2},{4,5},{5,4},{6,7},{7,6},{8,9},{9,8},{10,11... | collective-permute-start | bytes 3145736 | tf_op jit(solution)/shard_map/ppermute | solution.py:83
  407.0 20.0 %collective-permute-start.64 = (bf16[1024,512]{1,0:T(8,128)(2,1)S(1)}, bf16[1024,512]{1,0:T(8,128)(2,1)S(1)}, u32[]{:S(2)}, u32[]{:S(2)}) collective-permute-start(bf16[1024,512]{1,0:T(8,128)(2,1)S(1)} %copy-done.4), channel_id=1, source_target_pairs={{0,1},{1,0},{2,3},{3,2},{4,5},{5,4},{6,7},{7,6},{8,9},{9,8},{10,11... | collective-permute-start | bytes 3145736 | tf_op jit(solution)/shard_map/ppermute | solution.py:83
  481.1 21.1 %collective-permute-start.75 = (bf16[256,384]{1,0:T(8,128)(2,1)S(1)}, bf16[256,384]{1,0:T(8,128)(2,1)S(1)}, u32[]{:S(2)}, u32[]{:S(2)}) collective-permute-start(bf16[256,384]{1,0:T(8,128)(2,1)S(1)} %get-tuple-element.288), channel_id=1, source_target_pairs={{0,24},{1,25},{2,26},{3,27},{4,28},{5,29},{6,30},{7,31},{8,16},{9,... | collective-permute-start | bytes 589832 | tf_op jit(solution)/shard_map/ppermute | solution.py:83
  483.6 35.6 %collective-permute-start.74 = (bf16[256,384]{1,0:T(8,128)(2,1)S(1)}, bf16[256,384]{1,0:T(8,128)(2,1)S(1)}, u32[]{:S(2)}, u32[]{:S(2)}) collective-permute-start(bf16[256,384]{1,0:T(8,128)(2,1)S(1)} %get-tuple-element.289), channel_id=1, source_target_pairs={{0,16},{1,17},{2,18},{3,19},{4,20},{5,21},{6,22},{7,23},{8,24},{9,... | collective-permute-start | bytes 589832 | tf_op jit(solution)/shard_map/ppermute | solution.py:83
  483.6 35.6 %collective-permute-start.73 = (bf16[256,384]{1,0:T(8,128)(2,1)S(1)}, bf16[256,384]{1,0:T(8,128)(2,1)S(1)}, u32[]{:S(2)}, u32[]{:S(2)}) collective-permute-start(bf16[256,384]{1,0:T(8,128)(2,1)S(1)} %get-tuple-element.290), channel_id=1, source_target_pairs={{0,8},{1,9},{2,10},{3,11},{4,12},{5,13},{6,14},{7,15},{8,0},{9,1},... | collective-permute-start | bytes 589832 | tf_op jit(solution)/shard_map/ppermute | solution.py:83
  541.8 20.3 %collective-permute-start.81 = (f32[3,128]{1,0:T(4,128)S(1)}, f32[3,128]{1,0:T(4,128)S(1)}, u32[]{:S(2)}, u32[]{:S(2)}) collective-permute-start(f32[3,128]{1,0:T(4,128)S(1)} %maximum_bitcast_fusion), channel_id=1, source_target_pairs={{0,2},{1,3},{2,0},{3,1},{4,6},{5,7},{6,4},{7,5},{8,10},{9,11},{10,... | collective-permute-start | bytes 4616 | tf_op jit(solution)/shard_map/ppermute | solution.py:83
  541.8 20.3 %collective-permute-start.82 = (f32[3,128]{1,0:T(4,128)S(1)}, f32[3,128]{1,0:T(4,128)S(1)}, u32[]{:S(2)}, u32[]{:S(2)}) collective-permute-start(f32[3,128]{1,0:T(4,128)S(1)} %maximum_bitcast_fusion), channel_id=1, source_target_pairs={{0,3},{1,2},{2,1},{3,0},{4,7},{5,6},{6,5},{7,4},{8,11},{9,10},{10,... | collective-permute-start | bytes 4616 | tf_op jit(solution)/shard_map/ppermute | solution.py:83
  (133 other events, 1797.7 us)
Sparse Core Ops, SparseCore 0:
  37.3 64.3 all-gather.3
  114.3 105.9 all-gather.5
  222.4 57.6 all-gather.7
  282.3 54.8 reduce-scatter.3
  339.3 102.1 reduce-scatter.5
  443.9 72.5 reduce-scatter.7

commit v4 on v3

--- a/solution.py
+++ b/solution.py
@@ -771,26 +771,6 @@
         return listed
 
     pair_own = gather_z(after(pair_t, attn_own))
-    first_blocks = first_blocks + over_core(first_blocks)
-
-    def first_plan(n, ins, out):
-        listed = []
-        for i in range(8):
-            col = pl.ds(pl.multiple_of(n[at_t + (0, 2, 0, 2, 1, 3, 1, 3)[i]] * side, side), side)
-            for k in range(4):
-                place = n[at_x + (i % 4 // 2) * 4 + k]
-                row = pl.ds(pl.multiple_of(place * 256, 256), 256)
-                listed.append((None, ins[i].at[k * 256 : (k + 1) * 256], out.at[row, col]))
-        return listed
-
-    ffn_t = transpose(
-        after(jnp.concatenate([gate_w, up_w, down_w], axis=0), first_own), stays
-    )
-    tok_y = send(tok_got, OVER_Y)
-    *first_blocks, ffn_t, tok_got, tok_y = stage(*first_blocks[:4], ffn_t, tok_got, tok_y)
-    ffn_own = gather_z(ffn_t)
-    first_blocks = first_blocks + over_core(first_blocks)
-    first_all = place_copies(first_plan, numbers, first_blocks, (depth, wide), BF)
 
     def rows_plan(n, ins, out):
         listed = []
@@ -850,7 +830,29 @@
     token_rows = tokens.astype(F32)
     plain_one, inverse_one = rms_parts(token_rows)
     normed = (plain_one * gain_one).astype(BF)
-    lat = dot(after(normed, attn_own), first_all)
+    *first_blocks, attn_own, normed = stage(*first_blocks, attn_own, normed)
+    first_blocks = first_blocks + over_core(first_blocks)
+
+    def first_plan(n, ins, out):
+        listed = []
+        for i in range(8):
+            col = pl.ds(pl.multiple_of(n[at_t + (0, 2, 0, 2, 1, 3, 1, 3)[i]] * side, side), side)
+            for k in range(4):
+                place = n[at_x + (i % 4 // 2) * 4 + k]
+                row = pl.ds(pl.multiple_of(place * 256, 256), 256)
+                listed.append((None, ins[i].at[k * 256 : (k + 1) * 256], out.at[row, col]))
+        return listed
+
+    ffn_t = transpose(
+        after(jnp.concatenate([gate_w, up_w, down_w], axis=0), first_own), stays
+    )
+    tok_y = send(tok_got, OVER_Y)
+    *first_blocks, ffn_t, tok_got, tok_y = stage(*first_blocks[:4], ffn_t, tok_got, tok_y)
+    ffn_own = gather_z(ffn_t)
+    first_blocks = first_blocks + over_core(first_blocks)
+    first_all = place_copies(first_plan, numbers, first_blocks, (depth, wide), BF)
+
+    lat = dot(normed, first_all)
     down_t = transpose(after(down_w, lat), stays)
     cot_got = send(after(rows_at(cotangent, t * part, part), lat), OVER_X)
     cot_y = send(cot_got, OVER_Y)
@@ -1034,32 +1036,33 @@
                 listed.append((None, ins[f + 3 * j], out.at[pl.ds(at, part // 2)]))
         return listed
 
-    *first_got, grad_tokens = stage(*trade_z(first_slabs), grad_tokens)
-    first_quarter = added(first_got).astype(BF)
-    quarters = [first_quarter] + [send(first_quarter, p) for p in (OVER_C, OVER_Y, OVER_YC)]
-    quarters = stage(*quarters)
-    attn_home = transpose(after(attn_sum, *quarters), stays)
-    dev = z * 2 + x
-    block = depth // 8
-    own_one = lax.dynamic_slice_in_dim(gain_one, dev * block, block)
-    grad_down_q, grad_key_w, grad_value_w, grad_gain_one = first_finish(
-        numbers, quarters, first_w, own_one, latent_width
-    )
     result = place_copies(out_plan, numbers, out_parts, (rows, depth), BF)
-
     grad_down_w = down_home.astype(F32)
     pair_home = pair_home.astype(F32)
     grad_gate_w, grad_up_w = pair_home[:256], pair_home[256:]
+
+    two_sum = jnp.sum(gate_w.astype(F32) * grad_gate_w + up_w.astype(F32) * grad_up_w, axis=1)
+    *first_got, grad_tokens, result, two_sum, grad_gate_w, grad_up_w, grad_down_w = stage(
+        *trade_z(first_slabs), grad_tokens, result, two_sum, grad_gate_w, grad_up_w, grad_down_w
+    )
+    first_quarter = added(first_got).astype(BF)
+    quarters = [first_quarter] + [send(first_quarter, p) for p in (OVER_C, OVER_Y, OVER_YC)]
+    attn_home = transpose(after(attn_sum, first_quarter), stays)
+    *quarters, attn_home = stage(*quarters, attn_home)
     attn_home = attn_home.astype(F32)
     grad_up_q, grad_out_w = attn_home[:upq_rows], attn_home[upq_rows:]
-
-    own_two = lax.dynamic_slice_in_dim(gain_two, dev * block, block)
-    own_q = lax.dynamic_slice_in_dim(gain_q, dev * upq_rows, upq_rows)
-    two_sum = jnp.sum(gate_w.astype(F32) * grad_gate_w + up_w.astype(F32) * grad_up_w, axis=1)
     q_sum = jnp.sum(up_q.astype(F32) * grad_up_q, axis=1)
     small = jnp.concatenate([two_sum, q_sum]).reshape(3, -1)
     small = small + send(small, OVER_C) + send(small, OVER_Y) + send(small, OVER_YC)
     small = small.reshape(-1)
+    dev = z * 2 + x
+    block = depth // 8
+    own_one = lax.dynamic_slice_in_dim(gain_one, dev * block, block)
+    own_two = lax.dynamic_slice_in_dim(gain_two, dev * block, block)
+    own_q = lax.dynamic_slice_in_dim(gain_q, dev * upq_rows, upq_rows)
+    grad_down_q, grad_key_w, grad_value_w, grad_gain_one = first_finish(
+        numbers, quarters, first_w, own_one, latent_width
+    )
     grad_gain_two = small[:block] / own_two
     grad_gain_q = small[block:] / own_q
 

time: 578 us -> 556 us (0.962)
  waiting for transfers between devices: 200 us -> 184 us
    ppermute x83, waiting for transfers between devices: 199 us -> 163 us  [send(): return lax.ppermute(array, AXES, pairs)]
    all_gather x3, waiting for transfers between devices: 0.02 us -> 20.1 us  [gather_z(): return lax.all_gather(array, 'dp', axis=0, tiled=True)]
    unnamed x156 -> x160, local copies, waits for them, and re-layouts: 22 us -> 20.5 us
  transfers between devices with their start and end apart: 89 -> 89, of which waited for: 33 -> 37; matrix products, arithmetic and copies ran while one was open for 10% -> 11% of each run, Pallas kernels for 33% -> 34%
where the time goes in v4:
time: 556 us; the launch traced here: 548 us
  Pallas kernels  185 us (33%)
  waiting for transfers between devices  184 us (33%)
  starting transfers between devices  83.5 us (15%)
  other arithmetic  36.1 us (6%)
  local copies, waits for them, and re-layouts  31.8 us (6%)
  between operations  15.6 us (3%)
  matrix products  12.6 us (2%)
    ppermute x83, waiting for transfers between devices, send(): return lax.ppermute(array, AXES, pairs)  163 us
    ppermute x83, starting transfers between devices, send(): return lax.ppermute(array, AXES, pairs)  82.8 us
    pallas_call x8, Pallas kernels, place_copies(): pl.pallas_call(body, grid_spec=pltpu.PrefetchScalarGridSpec(num_scalar_pr...  37.7 us
    pallas_call x4, Pallas kernels, weight_grads(): pl.pallas_call(body, grid_spec=pltpu.PrefetchScalarGridSpec(num_scalar_pr...  36.5 us
    unnamed x160, local copies, waits for them, and re-layouts  20.5 us
    pallas_call x1, Pallas kernels, ffn_backward(): pl.pallas_call(body, grid_spec=pltpu.PrefetchScalarGridSpec(num_scalar_pr...  20.4 us
    all_gather x3, waiting for transfers between devices, gather_z(): return lax.all_gather(array, 'dp', axis=0, tiled=True)  20.1 us
    pallas_call x4, Pallas kernels, product_pieces(): pl.pallas_call(body, in_specs=[WHOLE] * len(arrays), out_specs=[WHOLE] *...  18.2 us
  transfers between devices with their start and end apart: 89, of which 37 were waited for; matrix products, arithmetic and copies ran while one was open for 11% of the time, Pallas kernels for 34%

profile of v4, /device:TPU:0, one launch (start us, length us, event | category | flops | bytes accessed | tf_op | source)
XLA Modules:
  0.0 548.1 jit_solution(11270011166439241027)
XLA Ops:
  23.7 12.5 %collective-permute-done.1 = bf16[256,384]{1,0:T(8,128)(2,1)S(1)} collective-permute-done((bf16[256,384]{1,0:T(8,128)(2,1)S(1)}, bf16[256,384]{1,0:T(8,128)(2,1)S(1)}, u32[]{:S(2)}, u32[]{:S(2)}) %collective-permute-start.1) | collective-permute-done | bytes 196640 | tf_op jit(solution)/shard_map/ppermute | solution.py:83
  42.2 10.9 %collective-permute-done.7.refs_1_ = bf16[128,2048]{1,0:T(8,128)(2,1)} collective-permute-done((bf16[128,2048]{1,0:T(8,128)(2,1)S(1)}, bf16[128,2048]{1,0:T(8,128)(2,1)}, u32[]{:S(2)}, u32[]{:S(2)}) %collective-permute-start.7) | collective-permute-done | bytes 524320 | tf_op jit(solution)/shard_map/ppermute | solution.py:83
  59.5 8.2 %collective-permute-done.9.refs_3_ = bf16[128,2048]{1,0:T(8,128)(2,1)S(1)} collective-permute-done((bf16[128,2048]{1,0:T(8,128)(2,1)}, bf16[128,2048]{1,0:T(8,128)(2,1)S(1)}, u32[]{:S(2)}, u32[]{:S(2)}) %collective-permute-start.9) | collective-permute-done | bytes 524320 | tf_op jit(solution)/shard_map/ppermute | solution.py:83
  72.1 5.2 shard_map.246.tok_ref
  81.7 20.1 %all-gather.4.cloned.1.call-done.refs_0_ = bf16[1536,1024]{1,0:T(8,128)(2,1)} async-done(((bf16[384,1024]{1,0:T(8,128)(2,1)}), bf16[1536,1024]{1,0:T(8,128)(2,1)}) %all-gather.4.cloned.1.call-update) | async-done | bytes 3145744 | tf_op jit(solution)/shard_map/all_gather | solution.py:99
  101.9 5.4 fusion.2.refs_0_
  116.7 6.6 %shard_map.247.first_ref = bf16[2048,1536]{1,0:T(8,128)(2,1)} custom-call(s32[29]{0:T(128)} %concatenate.27.numbers_ref, bf16[1024,384]{1,0:T(8,128)(2,1)} %constant_dynamic-update-slice_fusion.3.refs_0_, bf16[1024,384]{1,0:T(8,128)(2,1)} %collective-permute-done.3.refs_1_, bf16[1024,384]{1,0:T(8,128)(2,1)} %collective-permute-done.4.refs_2_, ...), custom_call_target="tpu_custom_call" | custom-call | bytes 12582912 | tf_op jit(solution)/shard_map/pallas_call | solution.py:145
  123.3 8.8 %fusion.18 = f32[1024,1536]{1,0:T(8,128)S(1)} fusion(bf16[1024,2048]{1,0:T(8,128)(2,1)S(1)} %copy-done, bf16[2048,1536]{1,0:T(8,128)(2,1)} %shard_map.247.first_ref), kind=kOutput, calls=%fused_computation.98 | convolution fusion | flops 6442450944 | bytes 16777216 | tf_op jit(solution)/shard_map/dot_general | solution.py:19
  154.9 8.4 %shard_map.249 = (bf16[1024,512]{1,0:T(8,128)(2,1)}, bf16[1024,512]{1,0:T(8,128)(2,1)}, f32[2,1024,1]{2,1,0:T(8,128)}) custom-call(f32[1024,512]{1,0:T(8,128)} %fusion.19.pre_ref, f32[1024,128]{1,0:T(8,128)} %get-tuple-element.310.cos_ref, f32[1024,128]{1,0:T(8,128)} %get-tuple-element.309.sin_ref, bf16[1024,256]{1,0:T(8,128)(2,1)} %pad_maximum_fusion.1.k_ref, ...), custom_call_target="tpu_custom_call" | custom-call | flops 4294967296 | bytes 3145728 | tf_op jit(solution)/shard_map/pallas_call | solution.py:186
  171.7 7.4 %collective-permute-start.19 = (bf16[512,2048]{1,0:T(8,128)(2,1)}, bf16[512,2048]{1,0:T(8,128)(2,1)S(1)}, u32[]{:S(2)}, u32[]{:S(2)}) collective-permute-start(bf16[512,2048]{1,0:T(8,128)(2,1)} %shard_map.251), channel_id=1, source_target_pairs={{0,1},{1,0},{2,3},{3,2},{4,5},{5,4},{6,7},{7,6},{8,9},{9,8},{10,11... | collective-permute-start | bytes 6291464 | tf_op jit(solution)/shard_map/ppermute | solution.py:83
  194.6 5.1 shard_map.253.refs_0_
  204.9 11.4 %collective-permute-done.22 = bf16[128,2048]{1,0:T(8,128)(2,1)S(1)} collective-permute-done((bf16[128,2048]{1,0:T(8,128)(2,1)}, bf16[128,2048]{1,0:T(8,128)(2,1)S(1)}, u32[]{:S(2)}, u32[]{:S(2)}) %collective-permute-start.22) | collective-permute-done | bytes 524320 | tf_op jit(solution)/shard_map/ppermute | solution.py:83
  222.1 12.2 %collective-permute-done.28.refs_3_.refs_11_ = bf16[128,2048]{1,0:T(8,128)(2,1)S(1)} collective-permute-done((bf16[128,2048]{1,0:T(8,128)(2,1)S(1)}, bf16[128,2048]{1,0:T(8,128)(2,1)S(1)}, u32[]{:S(2)}, u32[]{:S(2)}) %collective-permute-start.28) | collective-permute-done | bytes 524320 | tf_op jit(solution)/shard_map/ppermute | solution.py:83
  234.3 9.8 %collective-permute-done.27.refs_2_.refs_10_ = bf16[128,2048]{1,0:T(8,128)(2,1)S(1)} collective-permute-done((bf16[128,2048]{1,0:T(8,128)(2,1)S(1)}, bf16[128,2048]{1,0:T(8,128)(2,1)S(1)}, u32[]{:S(2)}, u32[]{:S(2)}) %collective-permute-start.27) | collective-permute-done | bytes 524320 | tf_op jit(solution)/shard_map/ppermute | solution.py:83
  245.9 17.6 %shard_map.254 = (bf16[512,1408]{1,0:T(8,128)(2,1)}, f32[512,1408]{1,0:T(8,128)}, f32[512,1408]{1,0:T(8,128)}) custom-call(s32[29]{0:T(128)} %concatenate.27.numbers_ref, bf16[128,2048]{1,0:T(8,128)(2,1)} %copy-done.6, bf16[128,2048]{1,0:T(8,128)(2,1)} %copy-done.27, bf16[128,2048]{1,0:T(8,128)(2,1)} %copy-done.26, bf16[128,2048]{1,0:T(8,128)(2,1)} %copy-done.25, ...), custom_call_target="tpu_custom_call" | custom-call | flops 5905580032 | bytes 11534336 | tf_op jit(solution)/shard_map/pallas_call | solution.py:392
  268.1 7.9 %shard_map.255 = bf16[1024,1408]{1,0:T(8,128)(2,1)} custom-call(s32[29]{0:T(128)} %concatenate.27.numbers_ref, bf16[1024,2048]{1,0:T(8,128)(2,1)} %shard_map.253.refs_0_, bf16[512,1408]{1,0:T(8,128)(2,1)} %get-tuple-element.209.refs_1_.hid_ref, bf16[512,1408]{1,0:T(8,128)(2,1)} %copy-done.41), custom_call_target="tpu_custom_call" | custom-call | flops 738197504 | bytes 1441792 | tf_op jit(solution)/shard_map/pallas_call | solution.py:592
  276.4 5.3 collective-permute-done.35.refs_6_.refs_1_
  283.3 20.4 %shard_map.256 = (bf16[512,1408]{1,0:T(8,128)(2,1)}, bf16[512,1408]{1,0:T(8,128)(2,1)}, bf16[128,2048]{1,0:T(8,128)(2,1)}, bf16[128,2048]{1,0:T(8,128)(2,1)}, bf...) custom-call(s32[29]{0:T(128)} %concatenate.27.numbers_ref, bf16[1024,2048]{1,0:T(8,128)(2,1)} %shard_map.253.refs_0_, ...), custom_call_target="tpu_custom_call" | custom-call | flops 8858370048 | bytes 17301504 | tf_op jit(solution)/shard_map/pallas_call | solution.py:470
  310.4 13.3 %shard_map.257 = bf16[2048,1408]{1,0:T(8,128)(2,1)} custom-call(s32[29]{0:T(128)} %concatenate.27.numbers_ref, bf16[128,2048]{1,0:T(8,128)(2,1)} %copy-done.6, bf16[128,2048]{1,0:T(8,128)(2,1)} %copy-done.27, bf16[128,2048]{1,0:T(8,128)(2,1)} %copy-done.26, bf16[128,2048]{1,0:T(8,128)(2,1)} %copy-done.25, bf16[128,2048]{1,0:T(8,128)(2,1)} %copy-done.28, ...), custom_call_target="tpu_custom_call" | custom-call | flops 1476395008 | bytes 2883584 | tf_op jit(solution)/shard_map/pallas_call | solution.py:592
  323.8 7.1 %collective-permute-done.38 = bf16[128,2048]{1,0:T(8,128)(2,1)S(1)} collective-permute-done((bf16[128,2048]{1,0:T(8,128)(2,1)}, bf16[128,2048]{1,0:T(8,128)(2,1)S(1)}, u32[]{:S(2)}, u32[]{:S(2)}) %collective-permute-start.38) | collective-permute-done | bytes 524320 | tf_op jit(solution)/shard_map/ppermute | solution.py:83
  337.6 11.3 %shard_map.258 = (bf16[128,2048]{1,0:T(8,128)(2,1)}, bf16[128,2048]{1,0:T(8,128)(2,1)}, bf16[128,2048]{1,0:T(8,128)(2,1)}, bf16[128,2048]{1,0:T(8,128)(2,1)}) custom-call(s32[29]{0:T(128)} %concatenate.27.numbers_ref, bf16[512,1408]{1,0:T(8,128)(2,1)} %get-tuple-element.209.refs_1_.hid_ref, bf16[1024,1408]{1,0:T(8,128)(2,1)} %all-gather.8.cloned.1.call-done.refs_5_.refs_0_, ...), custom_call_target="tpu_custom_call" | custom-call | flops 738197504 | bytes 1441792 | tf_op jit(solution)/shard_map/pallas_call | solution.py:523
  349.9 9.1 %collective-permute-done.42.refs_2_.refs_3_ = bf16[128,2048]{1,0:T(8,128)(2,1)S(1)} collective-permute-done((bf16[128,2048]{1,0:T(8,128)(2,1)S(1)}, bf16[128,2048]{1,0:T(8,128)(2,1)S(1)}, u32[]{:S(2)}, u32[]{:S(2)}) %collective-permute-start.42) | collective-permute-done | bytes 524320 | tf_op jit(solution)/shard_map/ppermute | solution.py:83
  365.7 5.1 shard_map.261.mid_ref
  370.8 6.2 %shard_map.259.do_ref = bf16[1024,512]{1,0:T(8,128)(2,1)} custom-call(bf16[128,2048]{1,0:T(8,128)(2,1)} %copy-done.5, bf16[128,2048]{1,0:T(8,128)(2,1)} %copy-done.20, bf16[128,2048]{1,0:T(8,128)(2,1)} %copy-done.19, bf16[128,2048]{1,0:T(8,128)(2,1)} %copy-done.18, bf16[128,2048]{1,0:T(8,128)(2,1)} %copy-done.21, bf16[128,2048]{1,0:T(8,128)(2,1)} %copy-done.22, ...), custom_call_target="tpu_custom_call" | custom-call | flops 2147483648 | bytes 2097152 | tf_op jit(solution)/shard_map/pallas_call | solution.py:288
  377.9 13.1 %shard_map.260 = (bf16[1024,512]{1,0:T(8,128)(2,1)}, f32[1024,256]{1,0:T(8,128)}, f32[1024,256]{1,0:T(8,128)}) custom-call(bf16[1024,512]{1,0:T(8,128)(2,1)} %get-tuple-element.218.q_ref, bf16[1024,512]{1,0:T(8,128)(2,1)} %shard_map.259.do_ref, f32[2,1024,1]{2,1,0:T(8,128)} %get-tuple-element.223.lse_ref, f32[1024,128]{1,0:T(8,128)} %get-tuple-element.310.cos_ref, ...), custom_call_target="tpu_custom_call" | custom-call | flops 8589934592 | bytes 3145728 | tf_op jit(solution)/shard_map/pallas_call | solution.py:248
  422.0 9.5 %shard_map.264 = bf16[1536,1024]{1,0:T(8,128)(2,1)} custom-call(s32[29]{0:T(128)} %concatenate.27.numbers_ref, bf16[1024,1024]{1,0:T(8,128)(2,1)} %get-tuple-element.297.refs_0_, bf16[128,2048]{1,0:T(8,128)(2,1)} %copy-done.5, bf16[128,2048]{1,0:T(8,128)(2,1)} %copy-done.20, bf16[128,2048]{1,0:T(8,128)(2,1)} %copy-done.19, bf16[128,2048]{1,0:T(8,128)(2,1)} %copy-done.18, ...), custom_call_target="tpu_custom_call" | custom-call | flops 805306368 | bytes 1572864 | tf_op jit(solution)/shard_map/pallas_call | solution.py:592
  431.5 6.2 %collective-permute-done.60 = bf16[128,1536]{1,0:T(8,128)(2,1)S(1)} collective-permute-done((bf16[128,1536]{1,0:T(8,128)(2,1)}, bf16[128,1536]{1,0:T(8,128)(2,1)S(1)}, u32[]{:S(2)}, u32[]{:S(2)}) %collective-permute-start.60) | collective-permute-done | bytes 393248 | tf_op jit(solution)/shard_map/ppermute | solution.py:83
  445.0 9.5 %collective-permute-done.64.refs_4_.refs_3_ = bf16[128,1536]{1,0:T(8,128)(2,1)S(1)} collective-permute-done((bf16[128,1536]{1,0:T(8,128)(2,1)S(1)}, bf16[128,1536]{1,0:T(8,128)(2,1)S(1)}, u32[]{:S(2)}, u32[]{:S(2)}) %collective-permute-start.64) | collective-permute-done | bytes 393248 | tf_op jit(solution)/shard_map/ppermute | solution.py:83
  454.5 5.3 collective-permute-done.63.refs_3_.refs_2_
  473.8 5.7 %shard_map.265 = bf16[1024,384]{1,0:T(8,128)(2,1)} custom-call(s32[29]{0:T(128)} %concatenate.27.numbers_ref, bf16[1024,2048]{1,0:T(8,128)(2,1)} %fusion.2.refs_0_, bf16[128,1536]{1,0:T(8,128)(2,1)} %copy-done.9, bf16[128,1536]{1,0:T(8,128)(2,1)} %copy-done.36, bf16[128,1536]{1,0:T(8,128)(2,1)} %copy-done.35, bf16[128,1536]{1,0:T(8,128)(2,1)} %copy-done.34, ...), custom_call_target="tpu_custom_call" | custom-call | flops 201326592 | bytes 393216 | tf_op jit(solution)/shard_map/pallas_call | solution.py:592
  490.0 11.8 %shard_map.267 = f32[512,2048]{1,0:T(8,128)} custom-call(s32[29]{0:T(128)} %concatenate.27.numbers_ref, bf16[1024,1536]{1,0:T(8,128)(2,1)} %shard_map.266.lat_ref, bf16[2048,1536]{1,0:T(8,128)(2,1)} %shard_map.247.first_ref, bf16[1024,2048]{1,0:T(8,128)(2,1)} %shard_map.261.mid_ref, bf16[1024,2048]{1,0:T(8,128)(2,1)} %shard_map.246.tok_ref, f32[1,2048]{1,0:T(1,128)} %bitcast.57), custom_call_target="tpu_custom_call" | custom-call | flops 3221225472 | bytes 14680064 | tf_op jit(solution)/shard_map/pallas_call | solution.py:627
  504.2 10.2 %collective-permute-done.71 = bf16[256,384]{1,0:T(8,128)(2,1)S(1)} collective-permute-done((bf16[256,384]{1,0:T(8,128)(2,1)S(1)}, bf16[256,384]{1,0:T(8,128)(2,1)S(1)}, u32[]{:S(2)}, u32[]{:S(2)}) %collective-permute-start.71) | collective-permute-done | bytes 196640 | tf_op jit(solution)/shard_map/ppermute | solution.py:83
  (411 shorter events, 225.7 us)
Async XLA Ops:
  7.2 94.6 %all-gather.4.cloned.1.call-start = ((), (), s32[]{:S(2)}) async-start(), calls=%async_computation.3 | async-start | bytes 3932160 | tf_op jit(solution)/shard_map/all_gather | solution.py:99
  9.3 26.9 %collective-permute-start.6 = (bf16[384,1024]{1,0:T(8,128)(2,1)S(1)}, bf16[384,1024]{1,0:T(8,128)(2,1)}, u32[]{:S(2)}, u32[]{:S(2)}) collective-permute-start(bf16[384,1024]{1,0:T(8,128)(2,1)S(1)} %constant_dynamic-update-slice_fusion.7), channel_id=1, source_target_pairs={{1,4},{3,6},{4,1},{6,3},{9,12},{11,14},{12,9},{14,11},{17,20},{19,... | collective-permute-start | bytes 2359304 | tf_op jit(solution)/shard_map/ppermute | solution.py:83
  19.1 17.2 %collective-permute-start = (bf16[256,384]{1,0:T(8,128)(2,1)S(1)}, bf16[256,384]{1,0:T(8,128)(2,1)S(1)}, u32[]{:S(2)}, u32[]{:S(2)}) collective-permute-start(bf16[256,384]{1,0:T(8,128)(2,1)S(1)} %constant_dynamic-slice_fusion.11), channel_id=1, source_target_pairs={{0,8},{1,9},{2,10},{3,11},{4,12},{5,13},{6,14},{7,15},{8,0},{9,1},... | collective-permute-start | bytes 589832 | tf_op jit(solution)/shard_map/ppermute | solution.py:83
  37.2 179.1 %all-gather.6.cloned.1.call-start = ((), (), s32[]{:S(2)}) async-start(), calls=%async_computation.4 | async-start | bytes 7208960 | tf_op jit(solution)/shard_map/all_gather | solution.py:99
  56.0 24.4 %collective-permute-start.25 = (bf16[512,1408]{1,0:T(8,128)(2,1)S(1)}, bf16[512,1408]{1,0:T(8,128)(2,1)S(1)}, u32[]{:S(2)}, u32[]{:S(2)}) collective-permute-start(bf16[512,1408]{1,0:T(8,128)(2,1)S(1)} %pad_maximum_fusion), channel_id=1, source_target_pairs={{1,4},{3,6},{4,1},{6,3},{9,12},{11,14},{12,9},{14,11},{17,20},{19,... | collective-permute-start | bytes 4325384 | tf_op jit(solution)/shard_map/ppermute | solution.py:83
  68.6 38.7 %collective-permute-start.5 = (bf16[1024,384]{1,0:T(8,128)(2,1)}, bf16[1024,384]{1,0:T(8,128)(2,1)}, u32[]{:S(2)}, u32[]{:S(2)}) collective-permute-start(bf16[1024,384]{1,0:T(8,128)(2,1)} %constant_dynamic-update-slice_fusion.3.refs_0_), channel_id=1, source_target_pairs={{0,6},{1,7},{2,4},{3,5},{4,2},{5,3},{6,0},{7,1},{8,14},{9,15},{10,... | collective-permute-start | bytes 2359304 | tf_op jit(solution)/shard_map/ppermute | solution.py:83
  69.1 41.6 %collective-permute-start.4 = (bf16[1024,384]{1,0:T(8,128)(2,1)}, bf16[1024,384]{1,0:T(8,128)(2,1)}, u32[]{:S(2)}, u32[]{:S(2)}) collective-permute-start(bf16[1024,384]{1,0:T(8,128)(2,1)} %constant_dynamic-update-slice_fusion.3.refs_0_), channel_id=1, source_target_pairs={{0,4},{1,5},{2,6},{3,7},{4,0},{5,1},{6,2},{7,3},{8,12},{9,13},{10,... | collective-permute-start | bytes 2359304 | tf_op jit(solution)/shard_map/ppermute | solution.py:83
  71.6 39.1 %collective-permute-start.3 = (bf16[1024,384]{1,0:T(8,128)(2,1)}, bf16[1024,384]{1,0:T(8,128)(2,1)}, u32[]{:S(2)}, u32[]{:S(2)}) collective-permute-start(bf16[1024,384]{1,0:T(8,128)(2,1)} %constant_dynamic-update-slice_fusion.3.refs_0_), channel_id=1, source_target_pairs={{0,2},{1,3},{2,0},{3,1},{4,6},{5,7},{6,4},{7,5},{8,10},{9,11},{10,... | collective-permute-start | bytes 2359304 | tf_op jit(solution)/shard_map/ppermute | solution.py:83
  101.8 174.3 %all-gather.8.cloned.1.call-start = ((), (), s32[]{:S(2)}) async-start(), calls=%async_computation.5 | async-start | bytes 3604480 | tf_op jit(solution)/shard_map/all_gather | solution.py:99
  114.1 33.6 %collective-permute-start.18 = (bf16[1536,1024]{1,0:T(8,128)(2,1)S(1)}, bf16[1536,1024]{1,0:T(8,128)(2,1)}, u32[]{:S(2)}, u32[]{:S(2)}) collective-permute-start(bf16[1536,1024]{1,0:T(8,128)(2,1)S(1)} %copy-done.1), channel_id=1, source_target_pairs={{0,1},{1,0},{2,3},{3,2},{4,5},{5,4},{6,7},{7,6},{8,9},{9,8},{10,11... | collective-permute-start | bytes 9437192 | tf_op jit(solution)/shard_map/ppermute | solution.py:83
  190.5 25.8 %collective-permute-start.22 = (bf16[128,2048]{1,0:T(8,128)(2,1)}, bf16[128,2048]{1,0:T(8,128)(2,1)S(1)}, u32[]{:S(2)}, u32[]{:S(2)}) collective-permute-start(bf16[128,2048]{1,0:T(8,128)(2,1)} %get-tuple-element.175), channel_id=1, source_target_pairs={{0,6},{1,7},{2,4},{3,5},{4,2},{5,3},{6,0},{7,1},{8,14},{9,15},{10,... | collective-permute-start | bytes 1572872 | tf_op jit(solution)/shard_map/ppermute | solution.py:83
  216.3 28.8 %collective-permute-start.29 = (bf16[2048,1408]{1,0:T(8,128)(2,1)}, bf16[2048,1408]{1,0:T(8,128)(2,1)}, u32[]{:S(2)}, u32[]{:S(2)}) collective-permute-start(bf16[2048,1408]{1,0:T(8,128)(2,1)} %all-gather.6.cloned.1.call-done.refs_4_.refs_3_), channel_id=1, source_target_pairs={{0,1},{1,0},{2,3},{3,2},{4,5},{5,4},{6,7},{7,6},{8,9},{9,8},{10,11... | collective-permute-start | bytes 17301512 | tf_op jit(solution)/shard_map/ppermute | solution.py:83
  216.3 114.8 %reduce-scatter.4.cloned.1.call-start = ((), (), s32[]{:S(2)}) async-start(), calls=%async_computation.6 | async-start | bytes 3604480 | tf_op jit(solution)/shard_map/reduce_scatter | solution.py:103
  218.8 25.2 %collective-permute-start.27 = (bf16[128,2048]{1,0:T(8,128)(2,1)S(1)}, bf16[128,2048]{1,0:T(8,128)(2,1)S(1)}, u32[]{:S(2)}, u32[]{:S(2)}) collective-permute-start(bf16[128,2048]{1,0:T(8,128)(2,1)S(1)} %multiply_convert_fusion.1.refs_0_.refs_8_), channel_id=1, source_target_pairs={{0,4},{1,5},{2,6},{3,7},{4,0},{5,1},{6,2},{7,3},{8,12},{9,13},{10,... | collective-permute-start | bytes 1572872 | tf_op jit(solution)/shard_map/ppermute | solution.py:83
  220.5 24.6 %collective-permute-start.26 = (bf16[128,2048]{1,0:T(8,128)(2,1)S(1)}, bf16[128,2048]{1,0:T(8,128)(2,1)S(1)}, u32[]{:S(2)}, u32[]{:S(2)}) collective-permute-start(bf16[128,2048]{1,0:T(8,128)(2,1)S(1)} %multiply_convert_fusion.1.refs_0_.refs_8_), channel_id=1, source_target_pairs={{0,2},{1,3},{2,0},{3,1},{4,6},{5,7},{6,4},{7,5},{8,10},{9,11},{10,... | collective-permute-start | bytes 1572872 | tf_op jit(solution)/shard_map/ppermute | solution.py:83
  276.1 161.6 %reduce-scatter.6.cloned.1.call-start = ((), (), s32[]{:S(2)}) async-start(), calls=%async_computation.7 | async-start | bytes 7208960 | tf_op jit(solution)/shard_map/reduce_scatter | solution.py:103
  304.3 19.4 %collective-permute-start.36 = (bf16[128,2048]{1,0:T(8,128)(2,1)}, bf16[128,2048]{1,0:T(8,128)(2,1)S(1)}, u32[]{:S(2)}, u32[]{:S(2)}) collective-permute-start(bf16[128,2048]{1,0:T(8,128)(2,1)} %get-tuple-element.195), channel_id=1, source_target_pairs={{0,2},{1,3},{2,0},{3,1},{4,6},{5,7},{6,4},{7,5},{8,10},{9,11},{10,... | collective-permute-start | bytes 1572872 | tf_op jit(solution)/shard_map/ppermute | solution.py:83
  305.1 18.6 %collective-permute-start.37 = (bf16[128,2048]{1,0:T(8,128)(2,1)}, bf16[128,2048]{1,0:T(8,128)(2,1)S(1)}, u32[]{:S(2)}, u32[]{:S(2)}) collective-permute-start(bf16[128,2048]{1,0:T(8,128)(2,1)} %get-tuple-element.196), channel_id=1, source_target_pairs={{0,4},{1,5},{2,6},{3,7},{4,0},{5,1},{6,2},{7,3},{8,12},{9,13},{10,... | collective-permute-start | bytes 1572872 | tf_op jit(solution)/shard_map/ppermute | solution.py:83
  305.4 25.5 %collective-permute-start.38 = (bf16[128,2048]{1,0:T(8,128)(2,1)}, bf16[128,2048]{1,0:T(8,128)(2,1)S(1)}, u32[]{:S(2)}, u32[]{:S(2)}) collective-permute-start(bf16[128,2048]{1,0:T(8,128)(2,1)} %get-tuple-element.197), channel_id=1, source_target_pairs={{0,6},{1,7},{2,4},{3,5},{4,2},{5,3},{6,0},{7,1},{8,14},{9,15},{10,... | collective-permute-start | bytes 1572872 | tf_op jit(solution)/shard_map/ppermute | solution.py:83
  331.1 183.4 %reduce-scatter.8.cloned.1.call-start = ((), (), s32[]{:S(2)}) async-start(), calls=%async_computation.8 | async-start | bytes 3932160 | tf_op jit(solution)/shard_map/reduce_scatter | solution.py:103
  335.7 23.3 %collective-permute-start.42 = (bf16[128,2048]{1,0:T(8,128)(2,1)S(1)}, bf16[128,2048]{1,0:T(8,128)(2,1)S(1)}, u32[]{:S(2)}, u32[]{:S(2)}) collective-permute-start(bf16[128,2048]{1,0:T(8,128)(2,1)S(1)} %add_convert_fusion.1.refs_0_.refs_1_), channel_id=1, source_target_pairs={{0,4},{1,5},{2,6},{3,7},{4,0},{5,1},{6,2},{7,3},{8,12},{9,13},{10,... | collective-permute-start | bytes 1572872 | tf_op jit(solution)/shard_map/ppermute | solution.py:83
  336.4 22.7 %collective-permute-start.41 = (bf16[128,2048]{1,0:T(8,128)(2,1)S(1)}, bf16[128,2048]{1,0:T(8,128)(2,1)S(1)}, u32[]{:S(2)}, u32[]{:S(2)}) collective-permute-start(bf16[128,2048]{1,0:T(8,128)(2,1)S(1)} %add_convert_fusion.1.refs_0_.refs_1_), channel_id=1, source_target_pairs={{0,2},{1,3},{2,0},{3,1},{4,6},{5,7},{6,4},{7,5},{8,10},{9,11},{10,... | collective-permute-start | bytes 1572872 | tf_op jit(solution)/shard_map/ppermute | solution.py:83
  360.2 30.9 %collective-permute-start.44 = (bf16[128,2048]{1,0:T(8,128)(2,1)}, bf16[128,2048]{1,0:T(8,128)(2,1)S(1)}, u32[]{:S(2)}, u32[]{:S(2)}) collective-permute-start(bf16[128,2048]{1,0:T(8,128)(2,1)} %get-tuple-element.215), channel_id=1, source_target_pairs={{0,2},{1,3},{2,0},{3,1},{4,6},{5,7},{6,4},{7,5},{8,10},{9,11},{10,... | collective-permute-start | bytes 1572872 | tf_op jit(solution)/shard_map/ppermute | solution.py:83
  361.5 29.6 %collective-permute-start.45 = (bf16[128,2048]{1,0:T(8,128)(2,1)}, bf16[128,2048]{1,0:T(8,128)(2,1)}, u32[]{:S(2)}, u32[]{:S(2)}) collective-permute-start(bf16[128,2048]{1,0:T(8,128)(2,1)} %get-tuple-element.216), channel_id=1, source_target_pairs={{0,4},{1,5},{2,6},{3,7},{4,0},{5,1},{6,2},{7,3},{8,12},{9,13},{10,... | collective-permute-start | bytes 1572872 | tf_op jit(solution)/shard_map/ppermute | solution.py:83
  363.0 28.1 %collective-permute-start.46 = (bf16[128,2048]{1,0:T(8,128)(2,1)}, bf16[128,2048]{1,0:T(8,128)(2,1)}, u32[]{:S(2)}, u32[]{:S(2)}) collective-permute-start(bf16[128,2048]{1,0:T(8,128)(2,1)} %get-tuple-element.217), channel_id=1, source_target_pairs={{0,6},{1,7},{2,4},{3,5},{4,2},{5,3},{6,0},{7,1},{8,14},{9,15},{10,... | collective-permute-start | bytes 1572872 | tf_op jit(solution)/shard_map/ppermute | solution.py:83
  364.1 27.1 %collective-permute-start.52 = (bf16[1024,512]{1,0:T(8,128)(2,1)S(1)}, bf16[1024,512]{1,0:T(8,128)(2,1)S(1)}, u32[]{:S(2)}, u32[]{:S(2)}) collective-permute-start(bf16[1024,512]{1,0:T(8,128)(2,1)S(1)} %copy-done.2), channel_id=1, source_target_pairs={{0,1},{1,0},{2,3},{3,2},{4,5},{5,4},{6,7},{7,6},{8,9},{9,8},{10,11... | collective-permute-start | bytes 3145736 | tf_op jit(solution)/shard_map/ppermute | solution.py:83
  401.0 20.0 %collective-permute-start.61 = (bf16[1024,512]{1,0:T(8,128)(2,1)S(1)}, bf16[1024,512]{1,0:T(8,128)(2,1)S(1)}, u32[]{:S(2)}, u32[]{:S(2)}) collective-permute-start(bf16[1024,512]{1,0:T(8,128)(2,1)S(1)} %copy-done.3), channel_id=1, source_target_pairs={{0,1},{1,0},{2,3},{3,2},{4,5},{5,4},{6,7},{7,6},{8,9},{9,8},{10,11... | collective-permute-start | bytes 3145736 | tf_op jit(solution)/shard_map/ppermute | solution.py:83
  420.4 17.3 %collective-permute-start.60 = (bf16[128,1536]{1,0:T(8,128)(2,1)}, bf16[128,1536]{1,0:T(8,128)(2,1)S(1)}, u32[]{:S(2)}, u32[]{:S(2)}) collective-permute-start(bf16[128,1536]{1,0:T(8,128)(2,1)} %get-tuple-element.242), channel_id=1, source_target_pairs={{0,6},{1,7},{2,4},{3,5},{4,2},{5,3},{6,0},{7,1},{8,14},{9,15},{10,... | collective-permute-start | bytes 1179656 | tf_op jit(solution)/shard_map/ppermute | solution.py:83
  460.1 19.5 %collective-permute-start.69 = (bf16[512,1408]{1,0:T(8,128)(2,1)S(1)}, bf16[512,1408]{1,0:T(8,128)(2,1)S(1)}, u32[]{:S(2)}, u32[]{:S(2)}) collective-permute-start(bf16[512,1408]{1,0:T(8,128)(2,1)S(1)} %copy-done.42), channel_id=1, source_target_pairs={{1,4},{3,6},{4,1},{6,3},{9,12},{11,14},{12,9},{14,11},{17,20},{19,... | collective-permute-start | bytes 4325384 | tf_op jit(solution)/shard_map/ppermute | solution.py:83
  480.8 23.4 %collective-permute-start.72 = (bf16[256,384]{1,0:T(8,128)(2,1)S(1)}, bf16[256,384]{1,0:T(8,128)(2,1)S(1)}, u32[]{:S(2)}, u32[]{:S(2)}) collective-permute-start(bf16[256,384]{1,0:T(8,128)(2,1)S(1)} %get-tuple-element.305), channel_id=1, source_target_pairs={{0,24},{1,25},{2,26},{3,27},{4,28},{5,29},{6,30},{7,31},{8,16},{9,... | collective-permute-start | bytes 589832 | tf_op jit(solution)/shard_map/ppermute | solution.py:83
  483.3 31.2 %collective-permute-start.71 = (bf16[256,384]{1,0:T(8,128)(2,1)S(1)}, bf16[256,384]{1,0:T(8,128)(2,1)S(1)}, u32[]{:S(2)}, u32[]{:S(2)}) collective-permute-start(bf16[256,384]{1,0:T(8,128)(2,1)S(1)} %get-tuple-element.306), channel_id=1, source_target_pairs={{0,16},{1,17},{2,18},{3,19},{4,20},{5,21},{6,22},{7,23},{8,24},{9,... | collective-permute-start | bytes 589832 | tf_op jit(solution)/shard_map/ppermute | solution.py:83
  483.3 31.2 %collective-permute-start.70 = (bf16[256,384]{1,0:T(8,128)(2,1)S(1)}, bf16[256,384]{1,0:T(8,128)(2,1)S(1)}, u32[]{:S(2)}, u32[]{:S(2)}) collective-permute-start(bf16[256,384]{1,0:T(8,128)(2,1)S(1)} %get-tuple-element.307), channel_id=1, source_target_pairs={{0,8},{1,9},{2,10},{3,11},{4,12},{5,13},{6,14},{7,15},{8,0},{9,1},... | collective-permute-start | bytes 589832 | tf_op jit(solution)/shard_map/ppermute | solution.py:83
  (135 other events, 1727.8 us)
Sparse Core Ops, SparseCore 0:
  37.4 64.3 all-gather.3
  103.9 105.3 all-gather.5
  216.5 57.5 all-gather.7
  276.2 54.8 reduce-scatter.3
  333.3 102.0 reduce-scatter.5
  437.9 71.3 reduce-scatter.7

commit v5 on v4

--- a/solution.py
+++ b/solution.py
@@ -853,9 +853,9 @@
     first_all = place_copies(first_plan, numbers, first_blocks, (depth, wide), BF)
 
     lat = dot(normed, first_all)
-    down_t = transpose(after(down_w, lat), stays)
-    cot_got = send(after(rows_at(cotangent, t * part, part), lat), OVER_X)
-    cot_y = send(cot_got, OVER_Y)
+    down_t = transpose(after(down_w, first_blocks[4]), stays)
+    cot_got = send(after(rows_at(cotangent, t * part, part), first_blocks[4]), OVER_X)
+    cot_y = send(after(cot_got, lat), OVER_Y)
     attns = [attn_own, send(attn_own, OVER_C)]
     up_q_all = place_copies(
         head_plan(0, upq_rows), numbers, attns, (latent_width, cols), BF

time: 556 us -> 549 us (0.987)
    ppermute x83, waiting for transfers between devices: 163 us -> 157 us  [send(): return lax.ppermute(array, AXES, pairs)]
  transfers between devices with their start and end apart: 89 -> 89, of which waited for: 37 -> 33; matrix products, arithmetic and copies ran while one was open for 11% -> 11% of each run, Pallas kernels for 34% -> 34%
where the time goes in v5:
time: 549 us; the launch traced here: 543 us
  Pallas kernels  185 us (34%)
  waiting for transfers between devices  183 us (33%)
  starting transfers between devices  79.8 us (15%)
  other arithmetic  36.2 us (7%)
  local copies, waits for them, and re-layouts  31.2 us (6%)
  between operations  15.6 us (3%)
  matrix products  12.6 us (2%)
    ppermute x83, waiting for transfers between devices, send(): return lax.ppermute(array, AXES, pairs)  157 us
    ppermute x83, starting transfers between devices, send(): return lax.ppermute(array, AXES, pairs)  79.4 us
    pallas_call x8, Pallas kernels, place_copies(): pl.pallas_call(body, grid_spec=pltpu.PrefetchScalarGridSpec(num_scalar_pr...  37.7 us
    pallas_call x4, Pallas kernels, weight_grads(): pl.pallas_call(body, grid_spec=pltpu.PrefetchScalarGridSpec(num_scalar_pr...  36.4 us
    all_gather x3, waiting for transfers between devices, gather_z(): return lax.all_gather(array, 'dp', axis=0, tiled=True)  23.4 us
    pallas_call x1, Pallas kernels, ffn_backward(): pl.pallas_call(body, grid_spec=pltpu.PrefetchScalarGridSpec(num_scalar_pr...  20.3 us
    unnamed x160, local copies, waits for them, and re-layouts  19.9 us
    pallas_call x4, Pallas kernels, product_pieces(): pl.pallas_call(body, in_specs=[WHOLE] * len(arrays), out_specs=[WHOLE] *...  18.2 us
  transfers between devices with their start and end apart: 89, of which 33 were waited for; matrix products, arithmetic and copies ran while one was open for 11% of the time, Pallas kernels for 34%

profile of v5, /device:TPU:0, one launch (start us, length us, event | category | flops | bytes accessed | tf_op | source)
XLA Modules:
  0.0 543.0 jit_solution(1477282246207899643)
XLA Ops:
  13.9 5.1 collective-permute-start.2
  23.7 12.5 %collective-permute-done.1 = bf16[256,384]{1,0:T(8,128)(2,1)S(1)} collective-permute-done((bf16[256,384]{1,0:T(8,128)(2,1)S(1)}, bf16[256,384]{1,0:T(8,128)(2,1)S(1)}, u32[]{:S(2)}, u32[]{:S(2)}) %collective-permute-start.1) | collective-permute-done | bytes 196640 | tf_op jit(solution)/shard_map/ppermute | solution.py:83
  42.2 10.9 %collective-permute-done.7.refs_1_ = bf16[128,2048]{1,0:T(8,128)(2,1)} collective-permute-done((bf16[128,2048]{1,0:T(8,128)(2,1)S(1)}, bf16[128,2048]{1,0:T(8,128)(2,1)}, u32[]{:S(2)}, u32[]{:S(2)}) %collective-permute-start.7) | collective-permute-done | bytes 524320 | tf_op jit(solution)/shard_map/ppermute | solution.py:83
  59.5 8.2 %collective-permute-done.9.refs_3_ = bf16[128,2048]{1,0:T(8,128)(2,1)S(1)} collective-permute-done((bf16[128,2048]{1,0:T(8,128)(2,1)}, bf16[128,2048]{1,0:T(8,128)(2,1)S(1)}, u32[]{:S(2)}, u32[]{:S(2)}) %collective-permute-start.9) | collective-permute-done | bytes 524320 | tf_op jit(solution)/shard_map/ppermute | solution.py:83
  72.1 5.2 shard_map.246.tok_ref
  81.7 20.1 %all-gather.4.cloned.1.call-done.refs_0_ = bf16[1536,1024]{1,0:T(8,128)(2,1)} async-done(((bf16[384,1024]{1,0:T(8,128)(2,1)}), bf16[1536,1024]{1,0:T(8,128)(2,1)}) %all-gather.4.cloned.1.call-update) | async-done | bytes 3145744 | tf_op jit(solution)/shard_map/all_gather | solution.py:99
  101.9 5.4 fusion.2.refs_0_
  116.7 6.6 %shard_map.247.first_ref = bf16[2048,1536]{1,0:T(8,128)(2,1)} custom-call(s32[29]{0:T(128)} %concatenate.27.numbers_ref, bf16[1024,384]{1,0:T(8,128)(2,1)} %constant_dynamic-update-slice_fusion.3.refs_0_, bf16[1024,384]{1,0:T(8,128)(2,1)} %collective-permute-done.3.refs_1_, bf16[1024,384]{1,0:T(8,128)(2,1)} %collective-permute-done.4.refs_2_, ...), custom_call_target="tpu_custom_call" | custom-call | bytes 12582912 | tf_op jit(solution)/shard_map/pallas_call | solution.py:145
  123.3 8.8 %fusion.18 = f32[1024,1536]{1,0:T(8,128)S(1)} fusion(bf16[1024,2048]{1,0:T(8,128)(2,1)S(1)} %copy-done, bf16[2048,1536]{1,0:T(8,128)(2,1)} %shard_map.247.first_ref), kind=kOutput, calls=%fused_computation.98 | convolution fusion | flops 6442450944 | bytes 16777216 | tf_op jit(solution)/shard_map/dot_general | solution.py:19
  149.3 8.4 %shard_map.249 = (bf16[1024,512]{1,0:T(8,128)(2,1)}, bf16[1024,512]{1,0:T(8,128)(2,1)}, f32[2,1024,1]{2,1,0:T(8,128)}) custom-call(f32[1024,512]{1,0:T(8,128)} %fusion.19.pre_ref, f32[1024,128]{1,0:T(8,128)} %get-tuple-element.312.cos_ref, f32[1024,128]{1,0:T(8,128)} %get-tuple-element.311.sin_ref, bf16[1024,256]{1,0:T(8,128)(2,1)} %pad_maximum_fusion.1.k_ref, ...), custom_call_target="tpu_custom_call" | custom-call | flops 4294967296 | bytes 3145728 | tf_op jit(solution)/shard_map/pallas_call | solution.py:186
  184.2 5.1 shard_map.253.refs_0_
  195.6 10.3 %collective-permute-done.22 = bf16[128,2048]{1,0:T(8,128)(2,1)S(1)} collective-permute-done((bf16[128,2048]{1,0:T(8,128)(2,1)}, bf16[128,2048]{1,0:T(8,128)(2,1)S(1)}, u32[]{:S(2)}, u32[]{:S(2)}) %collective-permute-start.22) | collective-permute-done | bytes 524320 | tf_op jit(solution)/shard_map/ppermute | solution.py:83
  214.9 12.2 %collective-permute-done.28.refs_3_.refs_11_ = bf16[128,2048]{1,0:T(8,128)(2,1)S(1)} collective-permute-done((bf16[128,2048]{1,0:T(8,128)(2,1)S(1)}, bf16[128,2048]{1,0:T(8,128)(2,1)S(1)}, u32[]{:S(2)}, u32[]{:S(2)}) %collective-permute-start.28) | collective-permute-done | bytes 524320 | tf_op jit(solution)/shard_map/ppermute | solution.py:83
  227.1 10.8 %collective-permute-done.27.refs_2_.refs_10_ = bf16[128,2048]{1,0:T(8,128)(2,1)S(1)} collective-permute-done((bf16[128,2048]{1,0:T(8,128)(2,1)S(1)}, bf16[128,2048]{1,0:T(8,128)(2,1)S(1)}, u32[]{:S(2)}, u32[]{:S(2)}) %collective-permute-start.27) | collective-permute-done | bytes 524320 | tf_op jit(solution)/shard_map/ppermute | solution.py:83
  238.9 17.6 %shard_map.254 = (bf16[512,1408]{1,0:T(8,128)(2,1)}, f32[512,1408]{1,0:T(8,128)}, f32[512,1408]{1,0:T(8,128)}) custom-call(s32[29]{0:T(128)} %concatenate.27.numbers_ref, bf16[128,2048]{1,0:T(8,128)(2,1)} %copy-done.6, bf16[128,2048]{1,0:T(8,128)(2,1)} %copy-done.27, bf16[128,2048]{1,0:T(8,128)(2,1)} %copy-done.26, bf16[128,2048]{1,0:T(8,128)(2,1)} %copy-done.25, ...), custom_call_target="tpu_custom_call" | custom-call | flops 5905580032 | bytes 11534336 | tf_op jit(solution)/shard_map/pallas_call | solution.py:392
  261.1 7.9 %shard_map.255 = bf16[1024,1408]{1,0:T(8,128)(2,1)} custom-call(s32[29]{0:T(128)} %concatenate.27.numbers_ref, bf16[1024,2048]{1,0:T(8,128)(2,1)} %shard_map.253.refs_0_, bf16[512,1408]{1,0:T(8,128)(2,1)} %get-tuple-element.211.refs_1_.hid_ref, bf16[512,1408]{1,0:T(8,128)(2,1)} %copy-done.41), custom_call_target="tpu_custom_call" | custom-call | flops 738197504 | bytes 1441792 | tf_op jit(solution)/shard_map/pallas_call | solution.py:592
  269.4 5.4 collective-permute-done.35.refs_6_.refs_1_
  276.4 20.3 %shard_map.256 = (bf16[512,1408]{1,0:T(8,128)(2,1)}, bf16[512,1408]{1,0:T(8,128)(2,1)}, bf16[128,2048]{1,0:T(8,128)(2,1)}, bf16[128,2048]{1,0:T(8,128)(2,1)}, bf...) custom-call(s32[29]{0:T(128)} %concatenate.27.numbers_ref, bf16[1024,2048]{1,0:T(8,128)(2,1)} %shard_map.253.refs_0_, ...), custom_call_target="tpu_custom_call" | custom-call | flops 8858370048 | bytes 17301504 | tf_op jit(solution)/shard_map/pallas_call | solution.py:470
  303.4 13.2 %shard_map.257 = bf16[2048,1408]{1,0:T(8,128)(2,1)} custom-call(s32[29]{0:T(128)} %concatenate.27.numbers_ref, bf16[128,2048]{1,0:T(8,128)(2,1)} %copy-done.6, bf16[128,2048]{1,0:T(8,128)(2,1)} %copy-done.27, bf16[128,2048]{1,0:T(8,128)(2,1)} %copy-done.26, bf16[128,2048]{1,0:T(8,128)(2,1)} %copy-done.25, bf16[128,2048]{1,0:T(8,128)(2,1)} %copy-done.28, ...), custom_call_target="tpu_custom_call" | custom-call | flops 1476395008 | bytes 2883584 | tf_op jit(solution)/shard_map/pallas_call | solution.py:592
  316.6 7.3 %collective-permute-done.38 = bf16[128,2048]{1,0:T(8,128)(2,1)S(1)} collective-permute-done((bf16[128,2048]{1,0:T(8,128)(2,1)}, bf16[128,2048]{1,0:T(8,128)(2,1)S(1)}, u32[]{:S(2)}, u32[]{:S(2)}) %collective-permute-start.38) | collective-permute-done | bytes 524320 | tf_op jit(solution)/shard_map/ppermute | solution.py:83
  331.7 11.5 %shard_map.258 = (bf16[128,2048]{1,0:T(8,128)(2,1)}, bf16[128,2048]{1,0:T(8,128)(2,1)}, bf16[128,2048]{1,0:T(8,128)(2,1)}, bf16[128,2048]{1,0:T(8,128)(2,1)}) custom-call(s32[29]{0:T(128)} %concatenate.27.numbers_ref, bf16[512,1408]{1,0:T(8,128)(2,1)} %get-tuple-element.211.refs_1_.hid_ref, bf16[1024,1408]{1,0:T(8,128)(2,1)} %all-gather.8.cloned.1.call-done.refs_5_.refs_0_, ...), custom_call_target="tpu_custom_call" | custom-call | flops 738197504 | bytes 1441792 | tf_op jit(solution)/shard_map/pallas_call | solution.py:523
  344.0 9.9 %collective-permute-done.42.refs_2_.refs_3_ = bf16[128,2048]{1,0:T(8,128)(2,1)S(1)} collective-permute-done((bf16[128,2048]{1,0:T(8,128)(2,1)S(1)}, bf16[128,2048]{1,0:T(8,128)(2,1)S(1)}, u32[]{:S(2)}, u32[]{:S(2)}) %collective-permute-start.42) | collective-permute-done | bytes 524320 | tf_op jit(solution)/shard_map/ppermute | solution.py:83
  360.6 5.1 shard_map.261.mid_ref
  365.7 6.2 %shard_map.259.do_ref = bf16[1024,512]{1,0:T(8,128)(2,1)} custom-call(bf16[128,2048]{1,0:T(8,128)(2,1)} %copy-done.5, bf16[128,2048]{1,0:T(8,128)(2,1)} %copy-done.20, bf16[128,2048]{1,0:T(8,128)(2,1)} %copy-done.19, bf16[128,2048]{1,0:T(8,128)(2,1)} %copy-done.18, bf16[128,2048]{1,0:T(8,128)(2,1)} %copy-done.21, bf16[128,2048]{1,0:T(8,128)(2,1)} %copy-done.22, ...), custom_call_target="tpu_custom_call" | custom-call | flops 2147483648 | bytes 2097152 | tf_op jit(solution)/shard_map/pallas_call | solution.py:288
  373.1 13.0 %shard_map.260 = (bf16[1024,512]{1,0:T(8,128)(2,1)}, f32[1024,256]{1,0:T(8,128)}, f32[1024,256]{1,0:T(8,128)}) custom-call(bf16[1024,512]{1,0:T(8,128)(2,1)} %get-tuple-element.220.q_ref, bf16[1024,512]{1,0:T(8,128)(2,1)} %shard_map.259.do_ref, f32[2,1024,1]{2,1,0:T(8,128)} %get-tuple-element.225.lse_ref, f32[1024,128]{1,0:T(8,128)} %get-tuple-element.312.cos_ref, ...), custom_call_target="tpu_custom_call" | custom-call | flops 8589934592 | bytes 3145728 | tf_op jit(solution)/shard_map/pallas_call | solution.py:248
  416.9 9.5 %shard_map.264 = bf16[1536,1024]{1,0:T(8,128)(2,1)} custom-call(s32[29]{0:T(128)} %concatenate.27.numbers_ref, bf16[1024,1024]{1,0:T(8,128)(2,1)} %get-tuple-element.299.refs_0_, bf16[128,2048]{1,0:T(8,128)(2,1)} %copy-done.5, bf16[128,2048]{1,0:T(8,128)(2,1)} %copy-done.20, bf16[128,2048]{1,0:T(8,128)(2,1)} %copy-done.19, bf16[128,2048]{1,0:T(8,128)(2,1)} %copy-done.18, ...), custom_call_target="tpu_custom_call" | custom-call | flops 805306368 | bytes 1572864 | tf_op jit(solution)/shard_map/pallas_call | solution.py:592
  426.4 6.2 %collective-permute-done.60 = bf16[128,1536]{1,0:T(8,128)(2,1)S(1)} collective-permute-done((bf16[128,1536]{1,0:T(8,128)(2,1)}, bf16[128,1536]{1,0:T(8,128)(2,1)S(1)}, u32[]{:S(2)}, u32[]{:S(2)}) %collective-permute-start.60) | collective-permute-done | bytes 393248 | tf_op jit(solution)/shard_map/ppermute | solution.py:83
  439.9 9.5 %collective-permute-done.64.refs_4_.refs_3_ = bf16[128,1536]{1,0:T(8,128)(2,1)S(1)} collective-permute-done((bf16[128,1536]{1,0:T(8,128)(2,1)S(1)}, bf16[128,1536]{1,0:T(8,128)(2,1)S(1)}, u32[]{:S(2)}, u32[]{:S(2)}) %collective-permute-start.64) | collective-permute-done | bytes 393248 | tf_op jit(solution)/shard_map/ppermute | solution.py:83
  449.4 5.3 collective-permute-done.63.refs_3_.refs_2_
  468.7 5.7 %shard_map.265 = bf16[1024,384]{1,0:T(8,128)(2,1)} custom-call(s32[29]{0:T(128)} %concatenate.27.numbers_ref, bf16[1024,2048]{1,0:T(8,128)(2,1)} %fusion.2.refs_0_, bf16[128,1536]{1,0:T(8,128)(2,1)} %copy-done.9, bf16[128,1536]{1,0:T(8,128)(2,1)} %copy-done.36, bf16[128,1536]{1,0:T(8,128)(2,1)} %copy-done.35, bf16[128,1536]{1,0:T(8,128)(2,1)} %copy-done.34, ...), custom_call_target="tpu_custom_call" | custom-call | flops 201326592 | bytes 393216 | tf_op jit(solution)/shard_map/pallas_call | solution.py:592
  484.9 11.8 %shard_map.267 = f32[512,2048]{1,0:T(8,128)} custom-call(s32[29]{0:T(128)} %concatenate.27.numbers_ref, bf16[1024,1536]{1,0:T(8,128)(2,1)} %shard_map.266.lat_ref, bf16[2048,1536]{1,0:T(8,128)(2,1)} %shard_map.247.first_ref, bf16[1024,2048]{1,0:T(8,128)(2,1)} %shard_map.261.mid_ref, bf16[1024,2048]{1,0:T(8,128)(2,1)} %shard_map.246.tok_ref, f32[1,2048]{1,0:T(1,128)} %bitcast.57), custom_call_target="tpu_custom_call" | custom-call | flops 3221225472 | bytes 14680064 | tf_op jit(solution)/shard_map/pallas_call | solution.py:627
  499.0 10.3 %collective-permute-done.71 = bf16[256,384]{1,0:T(8,128)(2,1)S(1)} collective-permute-done((bf16[256,384]{1,0:T(8,128)(2,1)S(1)}, bf16[256,384]{1,0:T(8,128)(2,1)S(1)}, u32[]{:S(2)}, u32[]{:S(2)}) %collective-permute-start.71) | collective-permute-done | bytes 196640 | tf_op jit(solution)/shard_map/ppermute | solution.py:83
  (411 shorter events, 222.1 us)
Async XLA Ops:
  7.2 94.6 %all-gather.4.cloned.1.call-start = ((), (), s32[]{:S(2)}) async-start(), calls=%async_computation.3 | async-start | bytes 3932160 | tf_op jit(solution)/shard_map/all_gather | solution.py:99
  9.3 26.9 %collective-permute-start.6 = (bf16[384,1024]{1,0:T(8,128)(2,1)S(1)}, bf16[384,1024]{1,0:T(8,128)(2,1)}, u32[]{:S(2)}, u32[]{:S(2)}) collective-permute-start(bf16[384,1024]{1,0:T(8,128)(2,1)S(1)} %constant_dynamic-update-slice_fusion.7), channel_id=1, source_target_pairs={{1,4},{3,6},{4,1},{6,3},{9,12},{11,14},{12,9},{14,11},{17,20},{19,... | collective-permute-start | bytes 2359304 | tf_op jit(solution)/shard_map/ppermute | solution.py:83
  37.2 172.0 %all-gather.6.cloned.1.call-start = ((), (), s32[]{:S(2)}) async-start(), calls=%async_computation.4 | async-start | bytes 7208960 | tf_op jit(solution)/shard_map/all_gather | solution.py:99
  56.0 24.4 %collective-permute-start.25 = (bf16[512,1408]{1,0:T(8,128)(2,1)S(1)}, bf16[512,1408]{1,0:T(8,128)(2,1)S(1)}, u32[]{:S(2)}, u32[]{:S(2)}) collective-permute-start(bf16[512,1408]{1,0:T(8,128)(2,1)S(1)} %pad_maximum_fusion), channel_id=1, source_target_pairs={{1,4},{3,6},{4,1},{6,3},{9,12},{11,14},{12,9},{14,11},{17,20},{19,... | collective-permute-start | bytes 4325384 | tf_op jit(solution)/shard_map/ppermute | solution.py:83
  68.6 38.7 %collective-permute-start.5 = (bf16[1024,384]{1,0:T(8,128)(2,1)}, bf16[1024,384]{1,0:T(8,128)(2,1)}, u32[]{:S(2)}, u32[]{:S(2)}) collective-permute-start(bf16[1024,384]{1,0:T(8,128)(2,1)} %constant_dynamic-update-slice_fusion.3.refs_0_), channel_id=1, source_target_pairs={{0,6},{1,7},{2,4},{3,5},{4,2},{5,3},{6,0},{7,1},{8,14},{9,15},{10,... | collective-permute-start | bytes 2359304 | tf_op jit(solution)/shard_map/ppermute | solution.py:83
  69.1 41.6 %collective-permute-start.4 = (bf16[1024,384]{1,0:T(8,128)(2,1)}, bf16[1024,384]{1,0:T(8,128)(2,1)}, u32[]{:S(2)}, u32[]{:S(2)}) collective-permute-start(bf16[1024,384]{1,0:T(8,128)(2,1)} %constant_dynamic-update-slice_fusion.3.refs_0_), channel_id=1, source_target_pairs={{0,4},{1,5},{2,6},{3,7},{4,0},{5,1},{6,2},{7,3},{8,12},{9,13},{10,... | collective-permute-start | bytes 2359304 | tf_op jit(solution)/shard_map/ppermute | solution.py:83
  71.6 39.1 %collective-permute-start.3 = (bf16[1024,384]{1,0:T(8,128)(2,1)}, bf16[1024,384]{1,0:T(8,128)(2,1)}, u32[]{:S(2)}, u32[]{:S(2)}) collective-permute-start(bf16[1024,384]{1,0:T(8,128)(2,1)} %constant_dynamic-update-slice_fusion.3.refs_0_), channel_id=1, source_target_pairs={{0,2},{1,3},{2,0},{3,1},{4,6},{5,7},{6,4},{7,5},{8,10},{9,11},{10,... | collective-permute-start | bytes 2359304 | tf_op jit(solution)/shard_map/ppermute | solution.py:83
  101.8 167.3 %all-gather.8.cloned.1.call-start = ((), (), s32[]{:S(2)}) async-start(), calls=%async_computation.5 | async-start | bytes 3604480 | tf_op jit(solution)/shard_map/all_gather | solution.py:99
  114.1 27.9 %collective-permute-start.18 = (bf16[1536,1024]{1,0:T(8,128)(2,1)S(1)}, bf16[1536,1024]{1,0:T(8,128)(2,1)}, u32[]{:S(2)}, u32[]{:S(2)}) collective-permute-start(bf16[1536,1024]{1,0:T(8,128)(2,1)S(1)} %copy-done.1), channel_id=1, source_target_pairs={{0,1},{1,0},{2,3},{3,2},{4,5},{5,4},{6,7},{7,6},{8,9},{9,8},{10,11... | collective-permute-start | bytes 9437192 | tf_op jit(solution)/shard_map/ppermute | solution.py:83
  114.2 26.3 %collective-permute-start.16 = (bf16[128,2048]{1,0:T(8,128)(2,1)S(1)}, bf16[128,2048]{1,0:T(8,128)(2,1)}, u32[]{:S(2)}, u32[]{:S(2)}) collective-permute-start(bf16[128,2048]{1,0:T(8,128)(2,1)S(1)} %constant_dynamic-slice_fusion.9), channel_id=1, source_target_pairs={{0,4},{1,5},{2,6},{3,7},{4,0},{5,1},{6,2},{7,3},{8,12},{9,13},{10,... | collective-permute-start | bytes 1572872 | tf_op jit(solution)/shard_map/ppermute | solution.py:83
  114.7 26.2 %collective-permute-start.15 = (bf16[256,1408]{1,0:T(8,128)(2,1)}, bf16[256,1408]{1,0:T(8,128)(2,1)}, u32[]{:S(2)}, u32[]{:S(2)}) collective-permute-start(bf16[256,1408]{1,0:T(8,128)(2,1)} %param.29), channel_id=1, source_target_pairs={{1,4},{3,6},{4,1},{6,3},{9,12},{11,14},{12,9},{14,11},{17,20},{19,... | collective-permute-start | bytes 2162696 | tf_op jit(solution)/shard_map/ppermute | solution.py:83
  181.4 24.6 %collective-permute-start.22 = (bf16[128,2048]{1,0:T(8,128)(2,1)}, bf16[128,2048]{1,0:T(8,128)(2,1)S(1)}, u32[]{:S(2)}, u32[]{:S(2)}) collective-permute-start(bf16[128,2048]{1,0:T(8,128)(2,1)} %get-tuple-element.177), channel_id=1, source_target_pairs={{0,6},{1,7},{2,4},{3,5},{4,2},{5,3},{6,0},{7,1},{8,14},{9,15},{10,... | collective-permute-start | bytes 1572872 | tf_op jit(solution)/shard_map/ppermute | solution.py:83
  209.3 28.6 %collective-permute-start.29 = (bf16[2048,1408]{1,0:T(8,128)(2,1)}, bf16[2048,1408]{1,0:T(8,128)(2,1)}, u32[]{:S(2)}, u32[]{:S(2)}) collective-permute-start(bf16[2048,1408]{1,0:T(8,128)(2,1)} %all-gather.6.cloned.1.call-done.refs_4_.refs_3_), channel_id=1, source_target_pairs={{0,1},{1,0},{2,3},{3,2},{4,5},{5,4},{6,7},{7,6},{8,9},{9,8},{10,11... | collective-permute-start | bytes 17301512 | tf_op jit(solution)/shard_map/ppermute | solution.py:83
  209.4 116.6 %reduce-scatter.4.cloned.1.call-start = ((), (), s32[]{:S(2)}) async-start(), calls=%async_computation.6 | async-start | bytes 3604480 | tf_op jit(solution)/shard_map/reduce_scatter | solution.py:103
  213.8 24.1 %collective-permute-start.27 = (bf16[128,2048]{1,0:T(8,128)(2,1)S(1)}, bf16[128,2048]{1,0:T(8,128)(2,1)S(1)}, u32[]{:S(2)}, u32[]{:S(2)}) collective-permute-start(bf16[128,2048]{1,0:T(8,128)(2,1)S(1)} %multiply_convert_fusion.1.refs_0_.refs_8_), channel_id=1, source_target_pairs={{0,4},{1,5},{2,6},{3,7},{4,0},{5,1},{6,2},{7,3},{8,12},{9,13},{10,... | collective-permute-start | bytes 1572872 | tf_op jit(solution)/shard_map/ppermute | solution.py:83
  214.4 23.5 %collective-permute-start.26 = (bf16[128,2048]{1,0:T(8,128)(2,1)S(1)}, bf16[128,2048]{1,0:T(8,128)(2,1)S(1)}, u32[]{:S(2)}, u32[]{:S(2)}) collective-permute-start(bf16[128,2048]{1,0:T(8,128)(2,1)S(1)} %multiply_convert_fusion.1.refs_0_.refs_8_), channel_id=1, source_target_pairs={{0,2},{1,3},{2,0},{3,1},{4,6},{5,7},{6,4},{7,5},{8,10},{9,11},{10,... | collective-permute-start | bytes 1572872 | tf_op jit(solution)/shard_map/ppermute | solution.py:83
  269.1 163.5 %reduce-scatter.6.cloned.1.call-start = ((), (), s32[]{:S(2)}) async-start(), calls=%async_computation.7 | async-start | bytes 7208960 | tf_op jit(solution)/shard_map/reduce_scatter | solution.py:103
  297.3 19.3 %collective-permute-start.36 = (bf16[128,2048]{1,0:T(8,128)(2,1)}, bf16[128,2048]{1,0:T(8,128)(2,1)S(1)}, u32[]{:S(2)}, u32[]{:S(2)}) collective-permute-start(bf16[128,2048]{1,0:T(8,128)(2,1)} %get-tuple-element.197), channel_id=1, source_target_pairs={{0,2},{1,3},{2,0},{3,1},{4,6},{5,7},{6,4},{7,5},{8,10},{9,11},{10,... | collective-permute-start | bytes 1572872 | tf_op jit(solution)/shard_map/ppermute | solution.py:83
  298.6 18.1 %collective-permute-start.37 = (bf16[128,2048]{1,0:T(8,128)(2,1)}, bf16[128,2048]{1,0:T(8,128)(2,1)S(1)}, u32[]{:S(2)}, u32[]{:S(2)}) collective-permute-start(bf16[128,2048]{1,0:T(8,128)(2,1)} %get-tuple-element.198), channel_id=1, source_target_pairs={{0,4},{1,5},{2,6},{3,7},{4,0},{5,1},{6,2},{7,3},{8,12},{9,13},{10,... | collective-permute-start | bytes 1572872 | tf_op jit(solution)/shard_map/ppermute | solution.py:83
  300.1 23.8 %collective-permute-start.38 = (bf16[128,2048]{1,0:T(8,128)(2,1)}, bf16[128,2048]{1,0:T(8,128)(2,1)S(1)}, u32[]{:S(2)}, u32[]{:S(2)}) collective-permute-start(bf16[128,2048]{1,0:T(8,128)(2,1)} %get-tuple-element.199), channel_id=1, source_target_pairs={{0,6},{1,7},{2,4},{3,5},{4,2},{5,3},{6,0},{7,1},{8,14},{9,15},{10,... | collective-permute-start | bytes 1572872 | tf_op jit(solution)/shard_map/ppermute | solution.py:83
  326.0 183.4 %reduce-scatter.8.cloned.1.call-start = ((), (), s32[]{:S(2)}) async-start(), calls=%async_computation.8 | async-start | bytes 3932160 | tf_op jit(solution)/shard_map/reduce_scatter | solution.py:103
  330.6 23.3 %collective-permute-start.42 = (bf16[128,2048]{1,0:T(8,128)(2,1)S(1)}, bf16[128,2048]{1,0:T(8,128)(2,1)S(1)}, u32[]{:S(2)}, u32[]{:S(2)}) collective-permute-start(bf16[128,2048]{1,0:T(8,128)(2,1)S(1)} %add_convert_fusion.1.refs_0_.refs_1_), channel_id=1, source_target_pairs={{0,4},{1,5},{2,6},{3,7},{4,0},{5,1},{6,2},{7,3},{8,12},{9,13},{10,... | collective-permute-start | bytes 1572872 | tf_op jit(solution)/shard_map/ppermute | solution.py:83
  331.2 22.8 %collective-permute-start.41 = (bf16[128,2048]{1,0:T(8,128)(2,1)S(1)}, bf16[128,2048]{1,0:T(8,128)(2,1)S(1)}, u32[]{:S(2)}, u32[]{:S(2)}) collective-permute-start(bf16[128,2048]{1,0:T(8,128)(2,1)S(1)} %add_convert_fusion.1.refs_0_.refs_1_), channel_id=1, source_target_pairs={{0,2},{1,3},{2,0},{3,1},{4,6},{5,7},{6,4},{7,5},{8,10},{9,11},{10,... | collective-permute-start | bytes 1572872 | tf_op jit(solution)/shard_map/ppermute | solution.py:83
  355.1 31.1 %collective-permute-start.44 = (bf16[128,2048]{1,0:T(8,128)(2,1)}, bf16[128,2048]{1,0:T(8,128)(2,1)S(1)}, u32[]{:S(2)}, u32[]{:S(2)}) collective-permute-start(bf16[128,2048]{1,0:T(8,128)(2,1)} %get-tuple-element.217), channel_id=1, source_target_pairs={{0,2},{1,3},{2,0},{3,1},{4,6},{5,7},{6,4},{7,5},{8,10},{9,11},{10,... | collective-permute-start | bytes 1572872 | tf_op jit(solution)/shard_map/ppermute | solution.py:83
  356.4 29.8 %collective-permute-start.45 = (bf16[128,2048]{1,0:T(8,128)(2,1)}, bf16[128,2048]{1,0:T(8,128)(2,1)}, u32[]{:S(2)}, u32[]{:S(2)}) collective-permute-start(bf16[128,2048]{1,0:T(8,128)(2,1)} %get-tuple-element.218), channel_id=1, source_target_pairs={{0,4},{1,5},{2,6},{3,7},{4,0},{5,1},{6,2},{7,3},{8,12},{9,13},{10,... | collective-permute-start | bytes 1572872 | tf_op jit(solution)/shard_map/ppermute | solution.py:83
  357.9 28.3 %collective-permute-start.46 = (bf16[128,2048]{1,0:T(8,128)(2,1)}, bf16[128,2048]{1,0:T(8,128)(2,1)}, u32[]{:S(2)}, u32[]{:S(2)}) collective-permute-start(bf16[128,2048]{1,0:T(8,128)(2,1)} %get-tuple-element.219), channel_id=1, source_target_pairs={{0,6},{1,7},{2,4},{3,5},{4,2},{5,3},{6,0},{7,1},{8,14},{9,15},{10,... | collective-permute-start | bytes 1572872 | tf_op jit(solution)/shard_map/ppermute | solution.py:83
  359.0 27.3 %collective-permute-start.52 = (bf16[1024,512]{1,0:T(8,128)(2,1)S(1)}, bf16[1024,512]{1,0:T(8,128)(2,1)S(1)}, u32[]{:S(2)}, u32[]{:S(2)}) collective-permute-start(bf16[1024,512]{1,0:T(8,128)(2,1)S(1)} %copy-done.2), channel_id=1, source_target_pairs={{0,1},{1,0},{2,3},{3,2},{4,5},{5,4},{6,7},{7,6},{8,9},{9,8},{10,11... | collective-permute-start | bytes 3145736 | tf_op jit(solution)/shard_map/ppermute | solution.py:83
  395.9 20.0 %collective-permute-start.61 = (bf16[1024,512]{1,0:T(8,128)(2,1)S(1)}, bf16[1024,512]{1,0:T(8,128)(2,1)S(1)}, u32[]{:S(2)}, u32[]{:S(2)}) collective-permute-start(bf16[1024,512]{1,0:T(8,128)(2,1)S(1)} %copy-done.3), channel_id=1, source_target_pairs={{0,1},{1,0},{2,3},{3,2},{4,5},{5,4},{6,7},{7,6},{8,9},{9,8},{10,11... | collective-permute-start | bytes 3145736 | tf_op jit(solution)/shard_map/ppermute | solution.py:83
  455.0 19.4 %collective-permute-start.69 = (bf16[512,1408]{1,0:T(8,128)(2,1)S(1)}, bf16[512,1408]{1,0:T(8,128)(2,1)S(1)}, u32[]{:S(2)}, u32[]{:S(2)}) collective-permute-start(bf16[512,1408]{1,0:T(8,128)(2,1)S(1)} %copy-done.42), channel_id=1, source_target_pairs={{1,4},{3,6},{4,1},{6,3},{9,12},{11,14},{12,9},{14,11},{17,20},{19,... | collective-permute-start | bytes 4325384 | tf_op jit(solution)/shard_map/ppermute | solution.py:83
  475.6 23.4 %collective-permute-start.72 = (bf16[256,384]{1,0:T(8,128)(2,1)S(1)}, bf16[256,384]{1,0:T(8,128)(2,1)S(1)}, u32[]{:S(2)}, u32[]{:S(2)}) collective-permute-start(bf16[256,384]{1,0:T(8,128)(2,1)S(1)} %get-tuple-element.307), channel_id=1, source_target_pairs={{0,24},{1,25},{2,26},{3,27},{4,28},{5,29},{6,30},{7,31},{8,16},{9,... | collective-permute-start | bytes 589832 | tf_op jit(solution)/shard_map/ppermute | solution.py:83
  478.1 31.2 %collective-permute-start.71 = (bf16[256,384]{1,0:T(8,128)(2,1)S(1)}, bf16[256,384]{1,0:T(8,128)(2,1)S(1)}, u32[]{:S(2)}, u32[]{:S(2)}) collective-permute-start(bf16[256,384]{1,0:T(8,128)(2,1)S(1)} %get-tuple-element.308), channel_id=1, source_target_pairs={{0,16},{1,17},{2,18},{3,19},{4,20},{5,21},{6,22},{7,23},{8,24},{9,... | collective-permute-start | bytes 589832 | tf_op jit(solution)/shard_map/ppermute | solution.py:83
  478.1 31.2 %collective-permute-start.70 = (bf16[256,384]{1,0:T(8,128)(2,1)S(1)}, bf16[256,384]{1,0:T(8,128)(2,1)S(1)}, u32[]{:S(2)}, u32[]{:S(2)}) collective-permute-start(bf16[256,384]{1,0:T(8,128)(2,1)S(1)} %get-tuple-element.309), channel_id=1, source_target_pairs={{0,8},{1,9},{2,10},{3,11},{4,12},{5,13},{6,14},{7,15},{8,0},{9,1},... | collective-permute-start | bytes 589832 | tf_op jit(solution)/shard_map/ppermute | solution.py:83
  (135 other events, 1723.4 us)
Sparse Core Ops, SparseCore 0:
  37.4 64.3 all-gather.3
  103.9 105.3 all-gather.5
  211.4 57.4 all-gather.7
  271.1 54.8 reduce-scatter.3
  328.1 102.1 reduce-scatter.5
  432.8 71.3 reduce-scatter.7

commit v6 on v5

--- a/solution.py
+++ b/solution.py
@@ -1042,6 +1042,12 @@
     grad_gate_w, grad_up_w = pair_home[:256], pair_home[256:]
 
     two_sum = jnp.sum(gate_w.astype(F32) * grad_gate_w + up_w.astype(F32) * grad_up_w, axis=1)
+    dev = z * 2 + x
+    block = depth // 8
+    own_one = lax.dynamic_slice_in_dim(gain_one, dev * block, block).reshape(-1, 1)
+    own_two = lax.dynamic_slice_in_dim(gain_two, dev * block, block)
+    own_q = lax.dynamic_slice_in_dim(gain_q, dev * upq_rows, upq_rows)
+    own_one, own_two, own_q, two_sum = stage(own_one, own_two, own_q, two_sum)
     *first_got, grad_tokens, result, two_sum, grad_gate_w, grad_up_w, grad_down_w = stage(
         *trade_z(first_slabs), grad_tokens, result, two_sum, grad_gate_w, grad_up_w, grad_down_w
     )
@@ -1055,11 +1061,6 @@
     small = jnp.concatenate([two_sum, q_sum]).reshape(3, -1)
     small = small + send(small, OVER_C) + send(small, OVER_Y) + send(small, OVER_YC)
     small = small.reshape(-1)
-    dev = z * 2 + x
-    block = depth // 8
-    own_one = lax.dynamic_slice_in_dim(gain_one, dev * block, block)
-    own_two = lax.dynamic_slice_in_dim(gain_two, dev * block, block)
-    own_q = lax.dynamic_slice_in_dim(gain_q, dev * upq_rows, upq_rows)
     grad_down_q, grad_key_w, grad_value_w, grad_gain_one = first_finish(
         numbers, quarters, first_w, own_one, latent_width
     )

time: 549 us -> 548 us (level)
    unnamed x160 -> x156, local copies, waits for them, and re-layouts: 19.9 us -> 19.2 us
  transfers between devices with their start and end apart: 89 -> 89, of which waited for: 33 -> 32; matrix products, arithmetic and copies ran while one was open for 11% -> 11% of each run, Pallas kernels for 34% -> 34%
where the time goes in v6:
time: 548 us; the launch traced here: 542 us
  Pallas kernels  185 us (34%)
  waiting for transfers between devices  182 us (33%)
  starting transfers between devices  79.8 us (15%)
  other arithmetic  37.3 us (7%)
  local copies, waits for them, and re-layouts  30 us (5%)
  between operations  15.6 us (3%)
  matrix products  12.6 us (2%)
    ppermute x83, waiting for transfers between devices, send(): return lax.ppermute(array, AXES, pairs)  156 us
    ppermute x83, starting transfers between devices, send(): return lax.ppermute(array, AXES, pairs)  79.3 us
    pallas_call x8, Pallas kernels, place_copies(): pl.pallas_call(body, grid_spec=pltpu.PrefetchScalarGridSpec(num_scalar_pr...  37.8 us
    pallas_call x4, Pallas kernels, weight_grads(): pl.pallas_call(body, grid_spec=pltpu.PrefetchScalarGridSpec(num_scalar_pr...  36.4 us
    all_gather x3, waiting for transfers between devices, gather_z(): return lax.all_gather(array, 'dp', axis=0, tiled=True)  23.6 us
    pallas_call x1, Pallas kernels, ffn_backward(): pl.pallas_call(body, grid_spec=pltpu.PrefetchScalarGridSpec(num_scalar_pr...  20.3 us
    unnamed x156, local copies, waits for them, and re-layouts  19.2 us
    pallas_call x4, Pallas kernels, product_pieces(): pl.pallas_call(body, in_specs=[WHOLE] * len(arrays), out_specs=[WHOLE] *...  18.2 us
  transfers between devices with their start and end apart: 89, of which 32 were waited for; matrix products, arithmetic and copies ran while one was open for 11% of the time, Pallas kernels for 34%

profile of v6, /device:TPU:0, one launch (start us, length us, event | category | flops | bytes accessed | tf_op | source)
XLA Modules:
  0.0 542.1 jit_solution(3945935514592719855)
XLA Ops:
  13.9 5.1 collective-permute-start.2
  23.7 12.5 %collective-permute-done.1 = bf16[256,384]{1,0:T(8,128)(2,1)S(1)} collective-permute-done((bf16[256,384]{1,0:T(8,128)(2,1)S(1)}, bf16[256,384]{1,0:T(8,128)(2,1)S(1)}, u32[]{:S(2)}, u32[]{:S(2)}) %collective-permute-start.1) | collective-permute-done | bytes 196640 | tf_op jit(solution)/shard_map/ppermute | solution.py:83
  42.2 10.9 %collective-permute-done.7.refs_1_ = bf16[128,2048]{1,0:T(8,128)(2,1)} collective-permute-done((bf16[128,2048]{1,0:T(8,128)(2,1)S(1)}, bf16[128,2048]{1,0:T(8,128)(2,1)}, u32[]{:S(2)}, u32[]{:S(2)}) %collective-permute-start.7) | collective-permute-done | bytes 524320 | tf_op jit(solution)/shard_map/ppermute | solution.py:83
  59.5 8.2 %collective-permute-done.9.refs_3_ = bf16[128,2048]{1,0:T(8,128)(2,1)S(1)} collective-permute-done((bf16[128,2048]{1,0:T(8,128)(2,1)}, bf16[128,2048]{1,0:T(8,128)(2,1)S(1)}, u32[]{:S(2)}, u32[]{:S(2)}) %collective-permute-start.9) | collective-permute-done | bytes 524320 | tf_op jit(solution)/shard_map/ppermute | solution.py:83
  72.0 5.2 shard_map.246.tok_ref
  81.6 20.1 %all-gather.4.cloned.1.call-done.refs_0_ = bf16[1536,1024]{1,0:T(8,128)(2,1)} async-done(((bf16[384,1024]{1,0:T(8,128)(2,1)}), bf16[1536,1024]{1,0:T(8,128)(2,1)}) %all-gather.4.cloned.1.call-update) | async-done | bytes 3145744 | tf_op jit(solution)/shard_map/all_gather | solution.py:99
  101.8 5.4 fusion.2.refs_0_
  116.7 6.6 %shard_map.247.first_ref = bf16[2048,1536]{1,0:T(8,128)(2,1)} custom-call(s32[29]{0:T(128)} %concatenate.27.numbers_ref, bf16[1024,384]{1,0:T(8,128)(2,1)} %constant_dynamic-update-slice_fusion.3.refs_0_, bf16[1024,384]{1,0:T(8,128)(2,1)} %collective-permute-done.3.refs_1_, bf16[1024,384]{1,0:T(8,128)(2,1)} %collective-permute-done.4.refs_2_, ...), custom_call_target="tpu_custom_call" | custom-call | bytes 12582912 | tf_op jit(solution)/shard_map/pallas_call | solution.py:145
  123.3 8.8 %fusion.18 = f32[1024,1536]{1,0:T(8,128)S(1)} fusion(bf16[1024,2048]{1,0:T(8,128)(2,1)S(1)} %copy-done, bf16[2048,1536]{1,0:T(8,128)(2,1)} %shard_map.247.first_ref), kind=kOutput, calls=%fused_computation.98 | convolution fusion | flops 6442450944 | bytes 16777216 | tf_op jit(solution)/shard_map/dot_general | solution.py:19
  149.2 8.4 %shard_map.249 = (bf16[1024,512]{1,0:T(8,128)(2,1)}, bf16[1024,512]{1,0:T(8,128)(2,1)}, f32[2,1024,1]{2,1,0:T(8,128)}) custom-call(f32[1024,512]{1,0:T(8,128)} %fusion.19.pre_ref, f32[1024,128]{1,0:T(8,128)} %get-tuple-element.320.cos_ref, f32[1024,128]{1,0:T(8,128)} %get-tuple-element.319.sin_ref, bf16[1024,256]{1,0:T(8,128)(2,1)} %pad_maximum_fusion.1.k_ref, ...), custom_call_target="tpu_custom_call" | custom-call | flops 4294967296 | bytes 3145728 | tf_op jit(solution)/shard_map/pallas_call | solution.py:186
  184.1 5.1 shard_map.253.refs_0_
  195.6 10.3 %collective-permute-done.22 = bf16[128,2048]{1,0:T(8,128)(2,1)S(1)} collective-permute-done((bf16[128,2048]{1,0:T(8,128)(2,1)}, bf16[128,2048]{1,0:T(8,128)(2,1)S(1)}, u32[]{:S(2)}, u32[]{:S(2)}) %collective-permute-start.22) | collective-permute-done | bytes 524320 | tf_op jit(solution)/shard_map/ppermute | solution.py:83
  214.9 12.2 %collective-permute-done.28.refs_3_.refs_11_ = bf16[128,2048]{1,0:T(8,128)(2,1)S(1)} collective-permute-done((bf16[128,2048]{1,0:T(8,128)(2,1)S(1)}, bf16[128,2048]{1,0:T(8,128)(2,1)S(1)}, u32[]{:S(2)}, u32[]{:S(2)}) %collective-permute-start.28) | collective-permute-done | bytes 524320 | tf_op jit(solution)/shard_map/ppermute | solution.py:83
  227.1 10.8 %collective-permute-done.27.refs_2_.refs_10_ = bf16[128,2048]{1,0:T(8,128)(2,1)S(1)} collective-permute-done((bf16[128,2048]{1,0:T(8,128)(2,1)S(1)}, bf16[128,2048]{1,0:T(8,128)(2,1)S(1)}, u32[]{:S(2)}, u32[]{:S(2)}) %collective-permute-start.27) | collective-permute-done | bytes 524320 | tf_op jit(solution)/shard_map/ppermute | solution.py:83
  238.8 17.6 %shard_map.254 = (bf16[512,1408]{1,0:T(8,128)(2,1)}, f32[512,1408]{1,0:T(8,128)}, f32[512,1408]{1,0:T(8,128)}) custom-call(s32[29]{0:T(128)} %concatenate.27.numbers_ref, bf16[128,2048]{1,0:T(8,128)(2,1)} %copy-done.6, bf16[128,2048]{1,0:T(8,128)(2,1)} %copy-done.27, bf16[128,2048]{1,0:T(8,128)(2,1)} %copy-done.26, bf16[128,2048]{1,0:T(8,128)(2,1)} %copy-done.25, ...), custom_call_target="tpu_custom_call" | custom-call | flops 5905580032 | bytes 11534336 | tf_op jit(solution)/shard_map/pallas_call | solution.py:392
  261.1 7.9 %shard_map.255 = bf16[1024,1408]{1,0:T(8,128)(2,1)} custom-call(s32[29]{0:T(128)} %concatenate.27.numbers_ref, bf16[1024,2048]{1,0:T(8,128)(2,1)} %shard_map.253.refs_0_, bf16[512,1408]{1,0:T(8,128)(2,1)} %get-tuple-element.215.refs_1_.hid_ref, bf16[512,1408]{1,0:T(8,128)(2,1)} %copy-done.40), custom_call_target="tpu_custom_call" | custom-call | flops 738197504 | bytes 1441792 | tf_op jit(solution)/shard_map/pallas_call | solution.py:592
  269.4 5.4 collective-permute-done.35.refs_6_.refs_1_
  276.4 20.3 %shard_map.256 = (bf16[512,1408]{1,0:T(8,128)(2,1)}, bf16[512,1408]{1,0:T(8,128)(2,1)}, bf16[128,2048]{1,0:T(8,128)(2,1)}, bf16[128,2048]{1,0:T(8,128)(2,1)}, bf...) custom-call(s32[29]{0:T(128)} %concatenate.27.numbers_ref, bf16[1024,2048]{1,0:T(8,128)(2,1)} %shard_map.253.refs_0_, ...), custom_call_target="tpu_custom_call" | custom-call | flops 8858370048 | bytes 17301504 | tf_op jit(solution)/shard_map/pallas_call | solution.py:470
  303.3 13.2 %shard_map.257 = bf16[2048,1408]{1,0:T(8,128)(2,1)} custom-call(s32[29]{0:T(128)} %concatenate.27.numbers_ref, bf16[128,2048]{1,0:T(8,128)(2,1)} %copy-done.6, bf16[128,2048]{1,0:T(8,128)(2,1)} %copy-done.27, bf16[128,2048]{1,0:T(8,128)(2,1)} %copy-done.26, bf16[128,2048]{1,0:T(8,128)(2,1)} %copy-done.25, bf16[128,2048]{1,0:T(8,128)(2,1)} %copy-done.28, ...), custom_call_target="tpu_custom_call" | custom-call | flops 1476395008 | bytes 2883584 | tf_op jit(solution)/shard_map/pallas_call | solution.py:592
  316.6 7.3 %collective-permute-done.38 = bf16[128,2048]{1,0:T(8,128)(2,1)S(1)} collective-permute-done((bf16[128,2048]{1,0:T(8,128)(2,1)}, bf16[128,2048]{1,0:T(8,128)(2,1)S(1)}, u32[]{:S(2)}, u32[]{:S(2)}) %collective-permute-start.38) | collective-permute-done | bytes 524320 | tf_op jit(solution)/shard_map/ppermute | solution.py:83
  331.7 11.5 %shard_map.258 = (bf16[128,2048]{1,0:T(8,128)(2,1)}, bf16[128,2048]{1,0:T(8,128)(2,1)}, bf16[128,2048]{1,0:T(8,128)(2,1)}, bf16[128,2048]{1,0:T(8,128)(2,1)}) custom-call(s32[29]{0:T(128)} %concatenate.27.numbers_ref, bf16[512,1408]{1,0:T(8,128)(2,1)} %get-tuple-element.215.refs_1_.hid_ref, bf16[1024,1408]{1,0:T(8,128)(2,1)} %all-gather.8.cloned.1.call-done.refs_5_.refs_0_, ...), custom_call_target="tpu_custom_call" | custom-call | flops 738197504 | bytes 1441792 | tf_op jit(solution)/shard_map/pallas_call | solution.py:523
  344.0 9.9 %collective-permute-done.42.refs_2_.refs_3_ = bf16[128,2048]{1,0:T(8,128)(2,1)S(1)} collective-permute-done((bf16[128,2048]{1,0:T(8,128)(2,1)S(1)}, bf16[128,2048]{1,0:T(8,128)(2,1)S(1)}, u32[]{:S(2)}, u32[]{:S(2)}) %collective-permute-start.42) | collective-permute-done | bytes 524320 | tf_op jit(solution)/shard_map/ppermute | solution.py:83
  360.6 5.1 shard_map.261.mid_ref
  365.7 6.2 %shard_map.259.do_ref = bf16[1024,512]{1,0:T(8,128)(2,1)} custom-call(bf16[128,2048]{1,0:T(8,128)(2,1)} %copy-done.5, bf16[128,2048]{1,0:T(8,128)(2,1)} %copy-done.20, bf16[128,2048]{1,0:T(8,128)(2,1)} %copy-done.19, bf16[128,2048]{1,0:T(8,128)(2,1)} %copy-done.18, bf16[128,2048]{1,0:T(8,128)(2,1)} %copy-done.21, bf16[128,2048]{1,0:T(8,128)(2,1)} %copy-done.22, ...), custom_call_target="tpu_custom_call" | custom-call | flops 2147483648 | bytes 2097152 | tf_op jit(solution)/shard_map/pallas_call | solution.py:288
  373.1 13.0 %shard_map.260 = (bf16[1024,512]{1,0:T(8,128)(2,1)}, f32[1024,256]{1,0:T(8,128)}, f32[1024,256]{1,0:T(8,128)}) custom-call(bf16[1024,512]{1,0:T(8,128)(2,1)} %get-tuple-element.224.q_ref, bf16[1024,512]{1,0:T(8,128)(2,1)} %shard_map.259.do_ref, f32[2,1024,1]{2,1,0:T(8,128)} %get-tuple-element.229.lse_ref, f32[1024,128]{1,0:T(8,128)} %get-tuple-element.320.cos_ref, ...), custom_call_target="tpu_custom_call" | custom-call | flops 8589934592 | bytes 3145728 | tf_op jit(solution)/shard_map/pallas_call | solution.py:248
  416.9 9.5 %shard_map.264 = bf16[1536,1024]{1,0:T(8,128)(2,1)} custom-call(s32[29]{0:T(128)} %concatenate.27.numbers_ref, bf16[1024,1024]{1,0:T(8,128)(2,1)} %get-tuple-element.307.refs_0_, bf16[128,2048]{1,0:T(8,128)(2,1)} %copy-done.5, bf16[128,2048]{1,0:T(8,128)(2,1)} %copy-done.20, bf16[128,2048]{1,0:T(8,128)(2,1)} %copy-done.19, bf16[128,2048]{1,0:T(8,128)(2,1)} %copy-done.18, ...), custom_call_target="tpu_custom_call" | custom-call | flops 805306368 | bytes 1572864 | tf_op jit(solution)/shard_map/pallas_call | solution.py:592
  426.4 6.2 %collective-permute-done.60 = bf16[128,1536]{1,0:T(8,128)(2,1)S(1)} collective-permute-done((bf16[128,1536]{1,0:T(8,128)(2,1)}, bf16[128,1536]{1,0:T(8,128)(2,1)S(1)}, u32[]{:S(2)}, u32[]{:S(2)}) %collective-permute-start.60) | collective-permute-done | bytes 393248 | tf_op jit(solution)/shard_map/ppermute | solution.py:83
  439.8 9.5 %collective-permute-done.64.refs_4_.refs_3_ = bf16[128,1536]{1,0:T(8,128)(2,1)S(1)} collective-permute-done((bf16[128,1536]{1,0:T(8,128)(2,1)S(1)}, bf16[128,1536]{1,0:T(8,128)(2,1)S(1)}, u32[]{:S(2)}, u32[]{:S(2)}) %collective-permute-start.64) | collective-permute-done | bytes 393248 | tf_op jit(solution)/shard_map/ppermute | solution.py:83
  449.3 5.3 collective-permute-done.63.refs_3_.refs_2_
  468.6 5.7 %shard_map.265 = bf16[1024,384]{1,0:T(8,128)(2,1)} custom-call(s32[29]{0:T(128)} %concatenate.27.numbers_ref, bf16[1024,2048]{1,0:T(8,128)(2,1)} %fusion.2.refs_0_, bf16[128,1536]{1,0:T(8,128)(2,1)} %copy-done.9, bf16[128,1536]{1,0:T(8,128)(2,1)} %copy-done.36, bf16[128,1536]{1,0:T(8,128)(2,1)} %copy-done.35, bf16[128,1536]{1,0:T(8,128)(2,1)} %copy-done.34, ...), custom_call_target="tpu_custom_call" | custom-call | flops 201326592 | bytes 393216 | tf_op jit(solution)/shard_map/pallas_call | solution.py:592
  487.4 11.9 %shard_map.267 = f32[512,2048]{1,0:T(8,128)} custom-call(s32[29]{0:T(128)} %concatenate.27.numbers_ref, bf16[1024,1536]{1,0:T(8,128)(2,1)} %shard_map.266.lat_ref, bf16[2048,1536]{1,0:T(8,128)(2,1)} %shard_map.247.first_ref, bf16[1024,2048]{1,0:T(8,128)(2,1)} %shard_map.261.mid_ref, bf16[1024,2048]{1,0:T(8,128)(2,1)} %shard_map.246.tok_ref, f32[1,2048]{1,0:T(1,128)} %bitcast.57), custom_call_target="tpu_custom_call" | custom-call | flops 3221225472 | bytes 14680064 | tf_op jit(solution)/shard_map/pallas_call | solution.py:627
  499.3 9.8 %collective-permute-done.71 = bf16[256,384]{1,0:T(8,128)(2,1)S(1)} collective-permute-done((bf16[256,384]{1,0:T(8,128)(2,1)S(1)}, bf16[256,384]{1,0:T(8,128)(2,1)S(1)}, u32[]{:S(2)}, u32[]{:S(2)}) %collective-permute-start.71) | collective-permute-done | bytes 196640 | tf_op jit(solution)/shard_map/ppermute | solution.py:83
  (409 shorter events, 221.6 us)
Async XLA Ops:
  7.2 94.6 %all-gather.4.cloned.1.call-start = ((), (), s32[]{:S(2)}) async-start(), calls=%async_computation.3 | async-start | bytes 3932160 | tf_op jit(solution)/shard_map/all_gather | solution.py:99
  9.3 26.9 %collective-permute-start.6 = (bf16[384,1024]{1,0:T(8,128)(2,1)S(1)}, bf16[384,1024]{1,0:T(8,128)(2,1)}, u32[]{:S(2)}, u32[]{:S(2)}) collective-permute-start(bf16[384,1024]{1,0:T(8,128)(2,1)S(1)} %constant_dynamic-update-slice_fusion.7), channel_id=1, source_target_pairs={{1,4},{3,6},{4,1},{6,3},{9,12},{11,14},{12,9},{14,11},{17,20},{19,... | collective-permute-start | bytes 2359304 | tf_op jit(solution)/shard_map/ppermute | solution.py:83
  37.2 172.0 %all-gather.6.cloned.1.call-start = ((), (), s32[]{:S(2)}) async-start(), calls=%async_computation.4 | async-start | bytes 7208960 | tf_op jit(solution)/shard_map/all_gather | solution.py:99
  56.0 24.3 %collective-permute-start.25 = (bf16[512,1408]{1,0:T(8,128)(2,1)S(1)}, bf16[512,1408]{1,0:T(8,128)(2,1)S(1)}, u32[]{:S(2)}, u32[]{:S(2)}) collective-permute-start(bf16[512,1408]{1,0:T(8,128)(2,1)S(1)} %pad_maximum_fusion), channel_id=1, source_target_pairs={{1,4},{3,6},{4,1},{6,3},{9,12},{11,14},{12,9},{14,11},{17,20},{19,... | collective-permute-start | bytes 4325384 | tf_op jit(solution)/shard_map/ppermute | solution.py:83
  68.5 38.7 %collective-permute-start.5 = (bf16[1024,384]{1,0:T(8,128)(2,1)}, bf16[1024,384]{1,0:T(8,128)(2,1)}, u32[]{:S(2)}, u32[]{:S(2)}) collective-permute-start(bf16[1024,384]{1,0:T(8,128)(2,1)} %constant_dynamic-update-slice_fusion.3.refs_0_), channel_id=1, source_target_pairs={{0,6},{1,7},{2,4},{3,5},{4,2},{5,3},{6,0},{7,1},{8,14},{9,15},{10,... | collective-permute-start | bytes 2359304 | tf_op jit(solution)/shard_map/ppermute | solution.py:83
  69.0 41.7 %collective-permute-start.4 = (bf16[1024,384]{1,0:T(8,128)(2,1)}, bf16[1024,384]{1,0:T(8,128)(2,1)}, u32[]{:S(2)}, u32[]{:S(2)}) collective-permute-start(bf16[1024,384]{1,0:T(8,128)(2,1)} %constant_dynamic-update-slice_fusion.3.refs_0_), channel_id=1, source_target_pairs={{0,4},{1,5},{2,6},{3,7},{4,0},{5,1},{6,2},{7,3},{8,12},{9,13},{10,... | collective-permute-start | bytes 2359304 | tf_op jit(solution)/shard_map/ppermute | solution.py:83
  71.5 39.2 %collective-permute-start.3 = (bf16[1024,384]{1,0:T(8,128)(2,1)}, bf16[1024,384]{1,0:T(8,128)(2,1)}, u32[]{:S(2)}, u32[]{:S(2)}) collective-permute-start(bf16[1024,384]{1,0:T(8,128)(2,1)} %constant_dynamic-update-slice_fusion.3.refs_0_), channel_id=1, source_target_pairs={{0,2},{1,3},{2,0},{3,1},{4,6},{5,7},{6,4},{7,5},{8,10},{9,11},{10,... | collective-permute-start | bytes 2359304 | tf_op jit(solution)/shard_map/ppermute | solution.py:83
  101.8 167.3 %all-gather.8.cloned.1.call-start = ((), (), s32[]{:S(2)}) async-start(), calls=%async_computation.5 | async-start | bytes 3604480 | tf_op jit(solution)/shard_map/all_gather | solution.py:99
  114.1 27.9 %collective-permute-start.18 = (bf16[1536,1024]{1,0:T(8,128)(2,1)S(1)}, bf16[1536,1024]{1,0:T(8,128)(2,1)}, u32[]{:S(2)}, u32[]{:S(2)}) collective-permute-start(bf16[1536,1024]{1,0:T(8,128)(2,1)S(1)} %copy-done.1), channel_id=1, source_target_pairs={{0,1},{1,0},{2,3},{3,2},{4,5},{5,4},{6,7},{7,6},{8,9},{9,8},{10,11... | collective-permute-start | bytes 9437192 | tf_op jit(solution)/shard_map/ppermute | solution.py:83
  114.1 26.3 %collective-permute-start.16 = (bf16[128,2048]{1,0:T(8,128)(2,1)S(1)}, bf16[128,2048]{1,0:T(8,128)(2,1)}, u32[]{:S(2)}, u32[]{:S(2)}) collective-permute-start(bf16[128,2048]{1,0:T(8,128)(2,1)S(1)} %constant_dynamic-slice_fusion.9), channel_id=1, source_target_pairs={{0,4},{1,5},{2,6},{3,7},{4,0},{5,1},{6,2},{7,3},{8,12},{9,13},{10,... | collective-permute-start | bytes 1572872 | tf_op jit(solution)/shard_map/ppermute | solution.py:83
  114.7 26.2 %collective-permute-start.15 = (bf16[256,1408]{1,0:T(8,128)(2,1)}, bf16[256,1408]{1,0:T(8,128)(2,1)}, u32[]{:S(2)}, u32[]{:S(2)}) collective-permute-start(bf16[256,1408]{1,0:T(8,128)(2,1)} %param.29), channel_id=1, source_target_pairs={{1,4},{3,6},{4,1},{6,3},{9,12},{11,14},{12,9},{14,11},{17,20},{19,... | collective-permute-start | bytes 2162696 | tf_op jit(solution)/shard_map/ppermute | solution.py:83
  181.3 24.6 %collective-permute-start.22 = (bf16[128,2048]{1,0:T(8,128)(2,1)}, bf16[128,2048]{1,0:T(8,128)(2,1)S(1)}, u32[]{:S(2)}, u32[]{:S(2)}) collective-permute-start(bf16[128,2048]{1,0:T(8,128)(2,1)} %get-tuple-element.181), channel_id=1, source_target_pairs={{0,6},{1,7},{2,4},{3,5},{4,2},{5,3},{6,0},{7,1},{8,14},{9,15},{10,... | collective-permute-start | bytes 1572872 | tf_op jit(solution)/shard_map/ppermute | solution.py:83
  209.3 28.6 %collective-permute-start.29 = (bf16[2048,1408]{1,0:T(8,128)(2,1)}, bf16[2048,1408]{1,0:T(8,128)(2,1)}, u32[]{:S(2)}, u32[]{:S(2)}) collective-permute-start(bf16[2048,1408]{1,0:T(8,128)(2,1)} %all-gather.6.cloned.1.call-done.refs_4_.refs_3_), channel_id=1, source_target_pairs={{0,1},{1,0},{2,3},{3,2},{4,5},{5,4},{6,7},{7,6},{8,9},{9,8},{10,11... | collective-permute-start | bytes 17301512 | tf_op jit(solution)/shard_map/ppermute | solution.py:83
  209.4 116.6 %reduce-scatter.4.cloned.1.call-start = ((), (), s32[]{:S(2)}) async-start(), calls=%async_computation.6 | async-start | bytes 3604480 | tf_op jit(solution)/shard_map/reduce_scatter | solution.py:103
  213.8 24.1 %collective-permute-start.27 = (bf16[128,2048]{1,0:T(8,128)(2,1)S(1)}, bf16[128,2048]{1,0:T(8,128)(2,1)S(1)}, u32[]{:S(2)}, u32[]{:S(2)}) collective-permute-start(bf16[128,2048]{1,0:T(8,128)(2,1)S(1)} %multiply_convert_fusion.1.refs_0_.refs_8_), channel_id=1, source_target_pairs={{0,4},{1,5},{2,6},{3,7},{4,0},{5,1},{6,2},{7,3},{8,12},{9,13},{10,... | collective-permute-start | bytes 1572872 | tf_op jit(solution)/shard_map/ppermute | solution.py:83
  214.4 23.5 %collective-permute-start.26 = (bf16[128,2048]{1,0:T(8,128)(2,1)S(1)}, bf16[128,2048]{1,0:T(8,128)(2,1)S(1)}, u32[]{:S(2)}, u32[]{:S(2)}) collective-permute-start(bf16[128,2048]{1,0:T(8,128)(2,1)S(1)} %multiply_convert_fusion.1.refs_0_.refs_8_), channel_id=1, source_target_pairs={{0,2},{1,3},{2,0},{3,1},{4,6},{5,7},{6,4},{7,5},{8,10},{9,11},{10,... | collective-permute-start | bytes 1572872 | tf_op jit(solution)/shard_map/ppermute | solution.py:83
  269.1 163.5 %reduce-scatter.6.cloned.1.call-start = ((), (), s32[]{:S(2)}) async-start(), calls=%async_computation.7 | async-start | bytes 7208960 | tf_op jit(solution)/shard_map/reduce_scatter | solution.py:103
  297.3 19.3 %collective-permute-start.36 = (bf16[128,2048]{1,0:T(8,128)(2,1)}, bf16[128,2048]{1,0:T(8,128)(2,1)S(1)}, u32[]{:S(2)}, u32[]{:S(2)}) collective-permute-start(bf16[128,2048]{1,0:T(8,128)(2,1)} %get-tuple-element.201), channel_id=1, source_target_pairs={{0,2},{1,3},{2,0},{3,1},{4,6},{5,7},{6,4},{7,5},{8,10},{9,11},{10,... | collective-permute-start | bytes 1572872 | tf_op jit(solution)/shard_map/ppermute | solution.py:83
  298.6 18.0 %collective-permute-start.37 = (bf16[128,2048]{1,0:T(8,128)(2,1)}, bf16[128,2048]{1,0:T(8,128)(2,1)S(1)}, u32[]{:S(2)}, u32[]{:S(2)}) collective-permute-start(bf16[128,2048]{1,0:T(8,128)(2,1)} %get-tuple-element.202), channel_id=1, source_target_pairs={{0,4},{1,5},{2,6},{3,7},{4,0},{5,1},{6,2},{7,3},{8,12},{9,13},{10,... | collective-permute-start | bytes 1572872 | tf_op jit(solution)/shard_map/ppermute | solution.py:83
  300.1 23.8 %collective-permute-start.38 = (bf16[128,2048]{1,0:T(8,128)(2,1)}, bf16[128,2048]{1,0:T(8,128)(2,1)S(1)}, u32[]{:S(2)}, u32[]{:S(2)}) collective-permute-start(bf16[128,2048]{1,0:T(8,128)(2,1)} %get-tuple-element.203), channel_id=1, source_target_pairs={{0,6},{1,7},{2,4},{3,5},{4,2},{5,3},{6,0},{7,1},{8,14},{9,15},{10,... | collective-permute-start | bytes 1572872 | tf_op jit(solution)/shard_map/ppermute | solution.py:83
  326.0 183.2 %reduce-scatter.8.cloned.1.call-start = ((), (), s32[]{:S(2)}) async-start(), calls=%async_computation.8 | async-start | bytes 3932160 | tf_op jit(solution)/shard_map/reduce_scatter | solution.py:103
  330.6 23.3 %collective-permute-start.42 = (bf16[128,2048]{1,0:T(8,128)(2,1)S(1)}, bf16[128,2048]{1,0:T(8,128)(2,1)S(1)}, u32[]{:S(2)}, u32[]{:S(2)}) collective-permute-start(bf16[128,2048]{1,0:T(8,128)(2,1)S(1)} %add_convert_fusion.1.refs_0_.refs_1_), channel_id=1, source_target_pairs={{0,4},{1,5},{2,6},{3,7},{4,0},{5,1},{6,2},{7,3},{8,12},{9,13},{10,... | collective-permute-start | bytes 1572872 | tf_op jit(solution)/shard_map/ppermute | solution.py:83
  331.2 22.8 %collective-permute-start.41 = (bf16[128,2048]{1,0:T(8,128)(2,1)S(1)}, bf16[128,2048]{1,0:T(8,128)(2,1)S(1)}, u32[]{:S(2)}, u32[]{:S(2)}) collective-permute-start(bf16[128,2048]{1,0:T(8,128)(2,1)S(1)} %add_convert_fusion.1.refs_0_.refs_1_), channel_id=1, source_target_pairs={{0,2},{1,3},{2,0},{3,1},{4,6},{5,7},{6,4},{7,5},{8,10},{9,11},{10,... | collective-permute-start | bytes 1572872 | tf_op jit(solution)/shard_map/ppermute | solution.py:83
  355.1 31.1 %collective-permute-start.44 = (bf16[128,2048]{1,0:T(8,128)(2,1)}, bf16[128,2048]{1,0:T(8,128)(2,1)S(1)}, u32[]{:S(2)}, u32[]{:S(2)}) collective-permute-start(bf16[128,2048]{1,0:T(8,128)(2,1)} %get-tuple-element.221), channel_id=1, source_target_pairs={{0,2},{1,3},{2,0},{3,1},{4,6},{5,7},{6,4},{7,5},{8,10},{9,11},{10,... | collective-permute-start | bytes 1572872 | tf_op jit(solution)/shard_map/ppermute | solution.py:83
  356.4 29.8 %collective-permute-start.45 = (bf16[128,2048]{1,0:T(8,128)(2,1)}, bf16[128,2048]{1,0:T(8,128)(2,1)}, u32[]{:S(2)}, u32[]{:S(2)}) collective-permute-start(bf16[128,2048]{1,0:T(8,128)(2,1)} %get-tuple-element.222), channel_id=1, source_target_pairs={{0,4},{1,5},{2,6},{3,7},{4,0},{5,1},{6,2},{7,3},{8,12},{9,13},{10,... | collective-permute-start | bytes 1572872 | tf_op jit(solution)/shard_map/ppermute | solution.py:83
  357.9 28.3 %collective-permute-start.46 = (bf16[128,2048]{1,0:T(8,128)(2,1)}, bf16[128,2048]{1,0:T(8,128)(2,1)}, u32[]{:S(2)}, u32[]{:S(2)}) collective-permute-start(bf16[128,2048]{1,0:T(8,128)(2,1)} %get-tuple-element.223), channel_id=1, source_target_pairs={{0,6},{1,7},{2,4},{3,5},{4,2},{5,3},{6,0},{7,1},{8,14},{9,15},{10,... | collective-permute-start | bytes 1572872 | tf_op jit(solution)/shard_map/ppermute | solution.py:83
  359.0 27.3 %collective-permute-start.52 = (bf16[1024,512]{1,0:T(8,128)(2,1)S(1)}, bf16[1024,512]{1,0:T(8,128)(2,1)S(1)}, u32[]{:S(2)}, u32[]{:S(2)}) collective-permute-start(bf16[1024,512]{1,0:T(8,128)(2,1)S(1)} %copy-done.2), channel_id=1, source_target_pairs={{0,1},{1,0},{2,3},{3,2},{4,5},{5,4},{6,7},{7,6},{8,9},{9,8},{10,11... | collective-permute-start | bytes 3145736 | tf_op jit(solution)/shard_map/ppermute | solution.py:83
  395.9 20.0 %collective-permute-start.61 = (bf16[1024,512]{1,0:T(8,128)(2,1)S(1)}, bf16[1024,512]{1,0:T(8,128)(2,1)S(1)}, u32[]{:S(2)}, u32[]{:S(2)}) collective-permute-start(bf16[1024,512]{1,0:T(8,128)(2,1)S(1)} %copy-done.3), channel_id=1, source_target_pairs={{0,1},{1,0},{2,3},{3,2},{4,5},{5,4},{6,7},{7,6},{8,9},{9,8},{10,11... | collective-permute-start | bytes 3145736 | tf_op jit(solution)/shard_map/ppermute | solution.py:83
  454.8 19.5 %collective-permute-start.69 = (bf16[512,1408]{1,0:T(8,128)(2,1)}, bf16[512,1408]{1,0:T(8,128)(2,1)}, u32[]{:S(2)}, u32[]{:S(2)}) collective-permute-start(bf16[512,1408]{1,0:T(8,128)(2,1)} %reduce-scatter.6.cloned.1.call-done), channel_id=1, source_target_pairs={{1,4},{3,6},{4,1},{6,3},{9,12},{11,14},{12,9},{14,11},{17,20},{19,... | collective-permute-start | bytes 4325384 | tf_op jit(solution)/shard_map/ppermute | solution.py:83
  476.0 23.3 %collective-permute-start.72 = (bf16[256,384]{1,0:T(8,128)(2,1)S(1)}, bf16[256,384]{1,0:T(8,128)(2,1)S(1)}, u32[]{:S(2)}, u32[]{:S(2)}) collective-permute-start(bf16[256,384]{1,0:T(8,128)(2,1)S(1)} %get-tuple-element.315), channel_id=1, source_target_pairs={{0,24},{1,25},{2,26},{3,27},{4,28},{5,29},{6,30},{7,31},{8,16},{9,... | collective-permute-start | bytes 589832 | tf_op jit(solution)/shard_map/ppermute | solution.py:83
  478.5 30.6 %collective-permute-start.71 = (bf16[256,384]{1,0:T(8,128)(2,1)S(1)}, bf16[256,384]{1,0:T(8,128)(2,1)S(1)}, u32[]{:S(2)}, u32[]{:S(2)}) collective-permute-start(bf16[256,384]{1,0:T(8,128)(2,1)S(1)} %get-tuple-element.316), channel_id=1, source_target_pairs={{0,16},{1,17},{2,18},{3,19},{4,20},{5,21},{6,22},{7,23},{8,24},{9,... | collective-permute-start | bytes 589832 | tf_op jit(solution)/shard_map/ppermute | solution.py:83
  478.5 30.6 %collective-permute-start.70 = (bf16[256,384]{1,0:T(8,128)(2,1)S(1)}, bf16[256,384]{1,0:T(8,128)(2,1)S(1)}, u32[]{:S(2)}, u32[]{:S(2)}) collective-permute-start(bf16[256,384]{1,0:T(8,128)(2,1)S(1)} %get-tuple-element.317), channel_id=1, source_target_pairs={{0,8},{1,9},{2,10},{3,11},{4,12},{5,13},{6,14},{7,15},{8,0},{9,1},... | collective-permute-start | bytes 589832 | tf_op jit(solution)/shard_map/ppermute | solution.py:83
  (133 other events, 1702.3 us)
Sparse Core Ops, SparseCore 0:
  37.3 64.3 all-gather.3
  103.9 105.3 all-gather.5
  211.4 57.4 all-gather.7
  271.1 54.8 reduce-scatter.3
  328.1 102.1 reduce-scatter.5
  432.8 70.4 reduce-scatter.7
